TPU v7x, 256 devices: a whole 4x4x8 slice. The times are simulated.
256 devices in a mesh: layer: 16 (over y, x), tx: 8 (over z), ty: 2 (over core).
Axes of the slice: x: 4, y: 4, z: 8, core: 2. Of those that a mesh axis runs over, the one named last changes fastest.
Arguments:
- krylov_block: float32 [4, 3, 128, 256, 256], P(None, None, 'layer', 'tx', 'ty'), may hold values from -1500 to 1500
- weights: float32 [3, 128, 256, 256], P(None, 'layer', 'tx', 'ty'), may hold values from 0.3 to 1.2
- pivots: float32 [128, 256, 256], P('layer', 'tx', 'ty'), may hold values from 0.015625 to 0.0625
- lower_ratio: float32 [128, 256, 256], P('layer', 'tx', 'ty'), may hold values from 0 to 1
- upper_ratio: float32 [128, 256, 256], P('layer', 'tx', 'ty'), may hold values from 0 to 1
- block_diag: float32 [9, 128, 256, 256], P(None, 'layer', 'tx', 'ty'), may hold values from -4 to 4
- block_inv: float32 [9, 128, 256, 256], P(None, 'layer', 'tx', 'ty'), may hold values from -4 to 4
- face_coef: float32 [6, 128, 256, 256], P(None, 'layer', 'tx', 'ty'), may hold values from 0.1 to 1
- fault_send_rows: int32 [16, 8, 2, 16, 8], P('layer', 'tx', 'ty'), may hold values from 0 to 255
- fault_recv_rows: int32 [16, 8, 2, 16, 8], P('layer', 'tx', 'ty'), may hold values from 0 to 255
- fault_counts: int32 [16, 8, 2, 16], P('layer', 'tx', 'ty'), may hold values from 0 to 8, as said below
- fault_coef: float32 [16, 8, 2, 16, 8, 128], P('layer', 'tx', 'ty'), may hold values from 0.2 to 1
- well_cells: int32 [8, 2, 16], P('tx', 'ty'), may hold values from 0 to 4095
- well_perfs: int32 [8, 2, 16, 8], P('tx', 'ty'), may hold values from 0 to 127
- well_index: float32 [8, 2, 16, 8], P('tx', 'ty'), may hold values from 0.5 to 2
Outputs:
- q_block: float32 [4, 3, 128, 256, 256], P(None, None, 'layer', 'tx', 'ty')
- r_factor: float32 [4, 4], replicated
Inputs may be any that keep to these rules, and one draw needn't show every extreme that they name: `fault_counts`: in every group of tiles at one index of layer, at least one tile receives 8 rows from every source tile.
All inputs are finite; a program needn't handle non-finite values.
Results may differ from a plain program's by a relative error of at most 0.0003.
Values sent between devices are 32-bit elements; how exact they have to be, the bound alone decides.
No kernel may reach another device: no remote copies, remote signals or barrier semaphores. Data moves between devices by JAX's collectives and lax.ppermute only.
A program may use at most 128 MiB of HBM per device.

v0:
```python
import jax
import jax.numpy as jnp
from jax import lax
from jax.sharding import PartitionSpec as P

HIGH = lax.Precision.HIGHEST


def passed_along(array, axis, by):
    size = lax.axis_size(axis)
    pairs = [(i, i + by) for i in range(size) if 0 <= i + by < size]
    return lax.ppermute(array, axis, pairs)


def extended(cells, sides, width):
    for axis, dim in sides:
        count = lax.axis_size(axis)
        ends = count - 1
        head = lax.slice_in_dim(cells, 0, width, axis=dim)
        tail = lax.slice_in_dim(cells, cells.shape[dim] - width, cells.shape[dim], axis=dim)
        cells = jnp.concatenate(
            [
                lax.ppermute(tail, axis, [(i, (i + 1) % count) for i in range(ends)]),
                cells,
                lax.ppermute(head, axis, [((i + 1) % count, i) for i in range(ends)]),
            ],
            axis=dim,
        )
    return cells


def mix(matrix, vectors):
    return (
        matrix[None, :, 0] * vectors[:, 0:1]
        + matrix[None, :, 1] * vectors[:, 1:2]
        + matrix[None, :, 2] * vectors[:, 2:3]
    )


def apply_stencil(values, padded, blocks, faces):
    result = mix(blocks, values)
    beside = [
        padded[:, :, :-2, 1:-1, 1:-1],
        padded[:, :, 2:, 1:-1, 1:-1],
        padded[:, :, 1:-1, :-2, 1:-1],
        padded[:, :, 1:-1, 2:, 1:-1],
        padded[:, :, 1:-1, 1:-1, :-2],
        padded[:, :, 1:-1, 1:-1, 2:],
    ]
    for number in range(6):
        result = result - faces[number][None, None] * beside[number]
    return result


def local_sweep(ratio, source, backward):
    start = (jnp.zeros(source.shape[1:], jnp.float32), jnp.ones((ratio.shape[1],), jnp.float32))

    def advance(carry, inputs):
        level, product = carry
        ratio_row, source_row = inputs
        level = source_row + ratio_row[None] * level
        product = ratio_row * product
        return ((level, product), (level, product))

    _, (levels, products) = lax.scan(advance, start, (ratio, source), reverse=backward)
    return (levels, products)


def incoming_state(factor, offset, backward):
    layers = lax.axis_size("layer")
    empty = jnp.zeros_like(offset)
    if backward:

        def relay_down(count, state):
            return passed_along(offset + factor[None] * state, "layer", -1)

        return lax.fori_loop(0, layers - 1, relay_down, empty)

    def relay_up(count, state):
        return passed_along(offset + factor[None] * state, "layer", 1)

    return lax.fori_loop(0, layers - 1, relay_up, empty)


def on_device(
    krylov_block,
    weights,
    pivots,
    lower_ratio,
    upper_ratio,
    block_diag,
    block_inv,
    face_coef,
    fault_send_rows,
    fault_recv_rows,
    fault_counts,
    fault_coef,
    well_cells,
    well_perfs,
    well_index,
):
    krylov_cols, _, depth_dev, tile_xdim, tile_ydim = krylov_block.shape
    cell_count = tile_xdim * tile_ydim
    sources = jnp.sum(weights[None] * krylov_block, axis=1)
    source_rows = jnp.moveaxis(sources.reshape(krylov_cols, depth_dev, cell_count), 1, 0)
    forward_term = pivots.reshape(depth_dev, 1, cell_count) * source_rows
    levels, products = local_sweep(lower_ratio.reshape(depth_dev, cell_count), forward_term, False)
    entering = incoming_state(products[-1], levels[-1], False)
    upward = levels + products[:, None] * entering[None]
    levels_down, products_down = local_sweep(
        upper_ratio.reshape(depth_dev, cell_count), upward, True
    )
    entering_down = incoming_state(products_down[0], levels_down[0], True)
    pressure = levels_down + products_down[:, None] * entering_down[None]
    pressure = jnp.moveaxis(pressure, 0, 1).reshape(krylov_cols, depth_dev, tile_xdim, tile_ydim)
    blocks = block_diag.reshape(3, 3, depth_dev, tile_xdim, tile_ydim)
    inverse = block_inv.reshape(3, 3, depth_dev, tile_xdim, tile_ydim)
    residue = krylov_block - blocks[None, :, 0] * pressure[:, None]
    precond = mix(inverse, residue)
    precond = precond.at[:, 0].add(pressure)
    padded = extended(precond, (("layer", 2), ("tx", 3), ("ty", 4)), 1)
    image = apply_stencil(precond, padded, blocks, face_coef)
    slots = fault_send_rows.shape[-1]
    row_count = depth_dev * tile_xdim
    outgoing = jnp.take(
        precond.reshape(krylov_cols, 3, row_count, tile_ydim), fault_send_rows.reshape(-1), axis=2
    )
    live = (jnp.arange(slots, dtype=jnp.int32)[None, :] < fault_counts.reshape(-1)[:, None]).astype(
        jnp.float32
    )
    weight_rows = fault_coef.reshape(-1, tile_ydim) * live.reshape(-1, 1)
    arrived = (
        lax.all_to_all(outgoing, ("tx", "ty"), split_axis=2, concat_axis=2, tiled=True)
        * weight_rows[None, None]
    )
    image_rows = image.reshape(krylov_cols, 3, row_count, tile_ydim)
    image_rows = image_rows.at[:, :, fault_recv_rows.reshape(-1)].add(-arrived)
    image = image_rows.reshape(krylov_cols, 3, depth_dev, tile_xdim, tile_ydim)
    layer_start = lax.axis_index("layer") * depth_dev
    cells_flat = well_cells.reshape(-1)
    perf_layers = well_perfs.reshape(cells_flat.shape[0], -1)
    strengths = well_index.reshape(perf_layers.shape)
    local_layer = perf_layers - layer_start
    inside = (local_layer >= 0) & (local_layer < depth_dev)
    spots = (jnp.clip(local_layer, 0, depth_dev - 1) * cell_count + cells_flat[:, None]).reshape(-1)
    base_pressure = precond[:, 0].reshape(krylov_cols, -1)
    drawn = jnp.take(base_pressure, spots, axis=1).reshape(
        krylov_cols, perf_layers.shape[0], perf_layers.shape[1]
    )
    active = jnp.where(inside, strengths, 0.0)
    partial_rates = jnp.sum(active[None] * drawn, axis=2)
    rates = lax.psum(partial_rates, "layer")
    added = active[None] * rates[:, :, None] / perf_layers.shape[1]
    image_zero = (
        image[:, 0].reshape(krylov_cols, -1).at[:, spots].add(added.reshape(krylov_cols, -1))
    )
    image = image.at[:, 0].set(image_zero.reshape(krylov_cols, depth_dev, tile_xdim, tile_ydim))
    flat = image.reshape(krylov_cols, -1)
    entries = (
        3.0
        * depth_dev
        * cell_count
        * lax.axis_size("layer")
        * lax.axis_size("tx")
        * lax.axis_size("ty")
    )
    local_gram = jnp.dot(flat, flat.T, precision=HIGH) / entries
    gram = lax.psum(local_gram, ("layer", "tx", "ty"))
    lower = jnp.linalg.cholesky(gram)
    q_flat = lax.linalg.triangular_solve(lower, flat, left_side=True, lower=True)
    return (q_flat.reshape(image.shape), lower.T)


def solution(mesh):
    placed = (
        P(None, None, "layer", "tx", "ty"),
        P(None, "layer", "tx", "ty"),
        P("layer", "tx", "ty"),
        P("layer", "tx", "ty"),
        P("layer", "tx", "ty"),
        P(None, "layer", "tx", "ty"),
        P(None, "layer", "tx", "ty"),
        P(None, "layer", "tx", "ty"),
        P("layer", "tx", "ty", None, None),
        P("layer", "tx", "ty", None, None),
        P("layer", "tx", "ty", None),
        P("layer", "tx", "ty", None, None, None),
        P("tx", "ty", None),
        P("tx", "ty", None, None),
        P("tx", "ty", None, None),
    )
    return jax.shard_map(
        on_device,
        mesh=mesh,
        in_specs=placed,
        out_specs=(P(None, None, "layer", "tx", "ty"), P()),
        check_vma=False,
    )
```

profile of v0, /device:TPU:1, one launch (start us, length us, event | category | flops | bytes accessed | tf_op | source)
XLA Modules:
  0.0 516.9 jit_solution(8015730407921296582)
XLA Ops:
  3.3 4.3 while.62
  7.7 97.8 %while.60 = (s32[]{:T(128)}, f32[4,4096]{1,0:T(4,128)S(1)}, f32[1,4096]{1,0:T(1,128)S(1)}, f32[4,4096]{1,0:T(4,128)S(1)}, s32[]{:T(128)}) while((s32[]{:T(128)}, f32[4,4096]{1,0:T(4,128)S(1)}, f32[1,4096]{1,0:T(1,128)S(1)}, f32[4,4096]{1,0:T(4,128)S(1)}, s32[]{:T(128)}) %tuple.125), condition=%wide.region_4.5_spmd, body=%wide.region_3.4_spmd.sunk | while | flops 32770 | bytes 475237 | solution.py:82
  7.8 3.9 collective-permute-start
  13.0 3.7 collective-permute-start
  18.1 3.7 collective-permute-start
  28.2 3.8 collective-permute-start
  33.3 5.8 %collective-permute-start = (f32[4,4096]{1,0:T(4,128)S(1)}, f32[4,4096]{1,0:T(4,128)S(1)}, u32[]{:S(2)}, u32[]{:S(2)}) collective-permute-start(f32[4,4096]{1,0:T(4,128)S(1)} %multiply_add_fusion.6), channel_id=1, source_target_pairs={{0,16},{16,32},{32,48},{48,64},{64,80},{80,96},{96,112},{112,128},... | collective-permute-start | bytes 196616 | tf_op jit(solution)/shard_map/while/body/eval_jaxpr/ppermute | solution.py:12
  40.4 5.8 %collective-permute-start = (f32[4,4096]{1,0:T(4,128)S(1)}, f32[4,4096]{1,0:T(4,128)S(1)}, u32[]{:S(2)}, u32[]{:S(2)}) collective-permute-start(f32[4,4096]{1,0:T(4,128)S(1)} %multiply_add_fusion.6), channel_id=1, source_target_pairs={{0,16},{16,32},{32,48},{48,64},{64,80},{80,96},{96,112},{112,128},... | collective-permute-start | bytes 196616 | tf_op jit(solution)/shard_map/while/body/eval_jaxpr/ppermute | solution.py:12
  47.6 5.8 %collective-permute-start = (f32[4,4096]{1,0:T(4,128)S(1)}, f32[4,4096]{1,0:T(4,128)S(1)}, u32[]{:S(2)}, u32[]{:S(2)}) collective-permute-start(f32[4,4096]{1,0:T(4,128)S(1)} %multiply_add_fusion.6), channel_id=1, source_target_pairs={{0,16},{16,32},{32,48},{48,64},{64,80},{80,96},{96,112},{112,128},... | collective-permute-start | bytes 196616 | tf_op jit(solution)/shard_map/while/body/eval_jaxpr/ppermute | solution.py:12
  55.3 5.6 %collective-permute-start = (f32[4,4096]{1,0:T(4,128)S(1)}, f32[4,4096]{1,0:T(4,128)S(1)}, u32[]{:S(2)}, u32[]{:S(2)}) collective-permute-start(f32[4,4096]{1,0:T(4,128)S(1)} %multiply_add_fusion.6), channel_id=1, source_target_pairs={{0,16},{16,32},{32,48},{48,64},{64,80},{80,96},{96,112},{112,128},... | collective-permute-start | bytes 196616 | tf_op jit(solution)/shard_map/while/body/eval_jaxpr/ppermute | solution.py:12
  62.2 5.8 %collective-permute-start = (f32[4,4096]{1,0:T(4,128)S(1)}, f32[4,4096]{1,0:T(4,128)S(1)}, u32[]{:S(2)}, u32[]{:S(2)}) collective-permute-start(f32[4,4096]{1,0:T(4,128)S(1)} %multiply_add_fusion.6), channel_id=1, source_target_pairs={{0,16},{16,32},{32,48},{48,64},{64,80},{80,96},{96,112},{112,128},... | collective-permute-start | bytes 196616 | tf_op jit(solution)/shard_map/while/body/eval_jaxpr/ppermute | solution.py:12
  69.4 5.9 %collective-permute-start = (f32[4,4096]{1,0:T(4,128)S(1)}, f32[4,4096]{1,0:T(4,128)S(1)}, u32[]{:S(2)}, u32[]{:S(2)}) collective-permute-start(f32[4,4096]{1,0:T(4,128)S(1)} %multiply_add_fusion.6), channel_id=1, source_target_pairs={{0,16},{16,32},{32,48},{48,64},{64,80},{80,96},{96,112},{112,128},... | collective-permute-start | bytes 196616 | tf_op jit(solution)/shard_map/while/body/eval_jaxpr/ppermute | solution.py:12
  76.7 5.8 %collective-permute-start = (f32[4,4096]{1,0:T(4,128)S(1)}, f32[4,4096]{1,0:T(4,128)S(1)}, u32[]{:S(2)}, u32[]{:S(2)}) collective-permute-start(f32[4,4096]{1,0:T(4,128)S(1)} %multiply_add_fusion.6), channel_id=1, source_target_pairs={{0,16},{16,32},{32,48},{48,64},{64,80},{80,96},{96,112},{112,128},... | collective-permute-start | bytes 196616 | tf_op jit(solution)/shard_map/while/body/eval_jaxpr/ppermute | solution.py:12
  83.8 5.8 %collective-permute-start = (f32[4,4096]{1,0:T(4,128)S(1)}, f32[4,4096]{1,0:T(4,128)S(1)}, u32[]{:S(2)}, u32[]{:S(2)}) collective-permute-start(f32[4,4096]{1,0:T(4,128)S(1)} %multiply_add_fusion.6), channel_id=1, source_target_pairs={{0,16},{16,32},{32,48},{48,64},{64,80},{80,96},{96,112},{112,128},... | collective-permute-start | bytes 196616 | tf_op jit(solution)/shard_map/while/body/eval_jaxpr/ppermute | solution.py:12
  91.0 5.8 %collective-permute-start = (f32[4,4096]{1,0:T(4,128)S(1)}, f32[4,4096]{1,0:T(4,128)S(1)}, u32[]{:S(2)}, u32[]{:S(2)}) collective-permute-start(f32[4,4096]{1,0:T(4,128)S(1)} %multiply_add_fusion.6), channel_id=1, source_target_pairs={{0,16},{16,32},{32,48},{48,64},{64,80},{80,96},{96,112},{112,128},... | collective-permute-start | bytes 196616 | tf_op jit(solution)/shard_map/while/body/eval_jaxpr/ppermute | solution.py:12
  98.1 5.8 %collective-permute-start = (f32[4,4096]{1,0:T(4,128)S(1)}, f32[4,4096]{1,0:T(4,128)S(1)}, u32[]{:S(2)}, u32[]{:S(2)}) collective-permute-start(f32[4,4096]{1,0:T(4,128)S(1)} %multiply_add_fusion.6), channel_id=1, source_target_pairs={{0,16},{16,32},{32,48},{48,64},{64,80},{80,96},{96,112},{112,128},... | collective-permute-start | bytes 196616 | tf_op jit(solution)/shard_map/while/body/eval_jaxpr/ppermute | solution.py:12
  105.9 4.3 while.63
  110.2 109.9 %while.61 = (s32[]{:T(128)}, f32[4,4096]{1,0:T(4,128)S(1)}, f32[1,4096]{1,0:T(1,128)S(1)}, f32[4,4096]{1,0:T(4,128)S(1)}, s32[]{:T(128)}) while((s32[]{:T(128)}, f32[4,4096]{1,0:T(4,128)S(1)}, f32[1,4096]{1,0:T(1,128)S(1)}, f32[4,4096]{1,0:T(4,128)S(1)}, s32[]{:T(128)}) %tuple.131), condition=%wide.region_8.9_spmd, body=%wide.region_7.8_spmd.sunk | while | flops 32770 | bytes 475237 | solution.py:77
  111.6 6.4 %collective-permute-done.1 = f32[4,4096]{1,0:T(4,128)S(1)} collective-permute-done((f32[4,4096]{1,0:T(4,128)S(1)}, f32[4,4096]{1,0:T(4,128)S(1)}, u32[]{:S(2)}, u32[]{:S(2)}) %collective-permute-start.1) | collective-permute-done | bytes 65568 | tf_op jit(solution)/shard_map/while/body/eval_jaxpr/ppermute | solution.py:12
  119.3 5.9 %collective-permute-done.1 = f32[4,4096]{1,0:T(4,128)S(1)} collective-permute-done((f32[4,4096]{1,0:T(4,128)S(1)}, f32[4,4096]{1,0:T(4,128)S(1)}, u32[]{:S(2)}, u32[]{:S(2)}) %collective-permute-start.1) | collective-permute-done | bytes 65568 | tf_op jit(solution)/shard_map/while/body/eval_jaxpr/ppermute | solution.py:12
  126.6 6.0 %collective-permute-done.1 = f32[4,4096]{1,0:T(4,128)S(1)} collective-permute-done((f32[4,4096]{1,0:T(4,128)S(1)}, f32[4,4096]{1,0:T(4,128)S(1)}, u32[]{:S(2)}, u32[]{:S(2)}) %collective-permute-start.1) | collective-permute-done | bytes 65568 | tf_op jit(solution)/shard_map/while/body/eval_jaxpr/ppermute | solution.py:12
  133.9 6.5 %collective-permute-done.1 = f32[4,4096]{1,0:T(4,128)S(1)} collective-permute-done((f32[4,4096]{1,0:T(4,128)S(1)}, f32[4,4096]{1,0:T(4,128)S(1)}, u32[]{:S(2)}, u32[]{:S(2)}) %collective-permute-start.1) | collective-permute-done | bytes 65568 | tf_op jit(solution)/shard_map/while/body/eval_jaxpr/ppermute | solution.py:12
  141.7 5.8 %collective-permute-done.1 = f32[4,4096]{1,0:T(4,128)S(1)} collective-permute-done((f32[4,4096]{1,0:T(4,128)S(1)}, f32[4,4096]{1,0:T(4,128)S(1)}, u32[]{:S(2)}, u32[]{:S(2)}) %collective-permute-start.1) | collective-permute-done | bytes 65568 | tf_op jit(solution)/shard_map/while/body/eval_jaxpr/ppermute | solution.py:12
  148.9 5.8 %collective-permute-done.1 = f32[4,4096]{1,0:T(4,128)S(1)} collective-permute-done((f32[4,4096]{1,0:T(4,128)S(1)}, f32[4,4096]{1,0:T(4,128)S(1)}, u32[]{:S(2)}, u32[]{:S(2)}) %collective-permute-start.1) | collective-permute-done | bytes 65568 | tf_op jit(solution)/shard_map/while/body/eval_jaxpr/ppermute | solution.py:12
  156.0 5.8 %collective-permute-done.1 = f32[4,4096]{1,0:T(4,128)S(1)} collective-permute-done((f32[4,4096]{1,0:T(4,128)S(1)}, f32[4,4096]{1,0:T(4,128)S(1)}, u32[]{:S(2)}, u32[]{:S(2)}) %collective-permute-start.1) | collective-permute-done | bytes 65568 | tf_op jit(solution)/shard_map/while/body/eval_jaxpr/ppermute | solution.py:12
  163.2 6.7 %collective-permute-done.1 = f32[4,4096]{1,0:T(4,128)S(1)} collective-permute-done((f32[4,4096]{1,0:T(4,128)S(1)}, f32[4,4096]{1,0:T(4,128)S(1)}, u32[]{:S(2)}, u32[]{:S(2)}) %collective-permute-start.1) | collective-permute-done | bytes 65568 | tf_op jit(solution)/shard_map/while/body/eval_jaxpr/ppermute | solution.py:12
  171.2 5.8 %collective-permute-done.1 = f32[4,4096]{1,0:T(4,128)S(1)} collective-permute-done((f32[4,4096]{1,0:T(4,128)S(1)}, f32[4,4096]{1,0:T(4,128)S(1)}, u32[]{:S(2)}, u32[]{:S(2)}) %collective-permute-start.1) | collective-permute-done | bytes 65568 | tf_op jit(solution)/shard_map/while/body/eval_jaxpr/ppermute | solution.py:12
  178.3 6.1 %collective-permute-done.1 = f32[4,4096]{1,0:T(4,128)S(1)} collective-permute-done((f32[4,4096]{1,0:T(4,128)S(1)}, f32[4,4096]{1,0:T(4,128)S(1)}, u32[]{:S(2)}, u32[]{:S(2)}) %collective-permute-start.1) | collective-permute-done | bytes 65568 | tf_op jit(solution)/shard_map/while/body/eval_jaxpr/ppermute | solution.py:12
  185.7 5.3 %collective-permute-done.1 = f32[4,4096]{1,0:T(4,128)S(1)} collective-permute-done((f32[4,4096]{1,0:T(4,128)S(1)}, f32[4,4096]{1,0:T(4,128)S(1)}, u32[]{:S(2)}, u32[]{:S(2)}) %collective-permute-start.1) | collective-permute-done | bytes 65568 | tf_op jit(solution)/shard_map/while/body/eval_jaxpr/ppermute | solution.py:12
  192.3 5.8 %collective-permute-done.1 = f32[4,4096]{1,0:T(4,128)S(1)} collective-permute-done((f32[4,4096]{1,0:T(4,128)S(1)}, f32[4,4096]{1,0:T(4,128)S(1)}, u32[]{:S(2)}, u32[]{:S(2)}) %collective-permute-start.1) | collective-permute-done | bytes 65568 | tf_op jit(solution)/shard_map/while/body/eval_jaxpr/ppermute | solution.py:12
  199.5 5.8 %collective-permute-done.1 = f32[4,4096]{1,0:T(4,128)S(1)} collective-permute-done((f32[4,4096]{1,0:T(4,128)S(1)}, f32[4,4096]{1,0:T(4,128)S(1)}, u32[]{:S(2)}, u32[]{:S(2)}) %collective-permute-start.1) | collective-permute-done | bytes 65568 | tf_op jit(solution)/shard_map/while/body/eval_jaxpr/ppermute | solution.py:12
  206.6 5.8 %collective-permute-done.1 = f32[4,4096]{1,0:T(4,128)S(1)} collective-permute-done((f32[4,4096]{1,0:T(4,128)S(1)}, f32[4,4096]{1,0:T(4,128)S(1)}, u32[]{:S(2)}, u32[]{:S(2)}) %collective-permute-start.1) | collective-permute-done | bytes 65568 | tf_op jit(solution)/shard_map/while/body/eval_jaxpr/ppermute | solution.py:12
  213.8 6.3 %collective-permute-done.1 = f32[4,4096]{1,0:T(4,128)S(1)} collective-permute-done((f32[4,4096]{1,0:T(4,128)S(1)}, f32[4,4096]{1,0:T(4,128)S(1)}, u32[]{:S(2)}, u32[]{:S(2)}) %collective-permute-start.1) | collective-permute-done | bytes 65568 | tf_op jit(solution)/shard_map/while/body/eval_jaxpr/ppermute | solution.py:12
  227.7 7.4 %collective-permute-start.2 = (f32[4,3,1,32,128]{4,3,2,0,1:T(8,128)}, f32[4,3,1,32,128]{4,3,2,0,1:T(8,128)}, u32[]{:S(2)}, u32[]{:S(2)}) collective-permute-start(f32[4,3,1,32,128]{4,3,2,0,1:T(8,128)} %get-tuple-element.370), channel_id=1, source_target_pairs={{0,16},{16,32},{32,48},{48,64},{64,80},{80,96},{96,112},{112,128},... | collective-permute-start | bytes 589832 | tf_op jit(solution)/shard_map/ppermute | solution.py:23
  242.4 42.0 %all-to-all-start = ((f32[4,3,128,128]{3,0,1,2:T(4,128)}), f32[4,3,128,128]{3,0,1,2:T(4,128)S(1)}, u32[]{:S(2)}, u32[]{:S(2)}) async-start(f32[4,3,128,128]{3,0,1,2:T(4,128)} %select_bitcast_fusion), calls=%async_computation | async-start | bytes 1572864 | tf_op jit(solution)/shard_map/all_to_all | solution.py:133
  291.3 4.6 collective-permute-start.4
  296.6 8.6 %copy.114 = f32[4,1,8,32,128]{0,4,3,2,1:T(8,128)} copy(f32[4,1,8,32,128]{4,3,2,0,1:T(8,128)S(1)} %get-tuple-element.363) | data formatting | bytes 1048576 | tf_op jit(solution)/shard_map/add | solution.py:120
  306.0 7.1 %gather_fusion.1 = f32[128,4]{1,0:T(8,128)} fusion(f32[4,32768]{0,1:T(8,128)} %bitcast.196, s32[1024]{0:T(1024)} %pad_clamp_fusion), kind=kCustom, calls=%fused_computation.1 | custom fusion | bytes 4608 | tf_op jit(solution)/shard_map/jit(_take)/gather | solution.py:147
  317.5 3.8 copy.101
  324.5 3.8 copy.99
  331.3 35.8 %psum.14 = f32[4,16]{0,1:T(8,128)S(1)} all-reduce(f32[4,16]{0,1:T(8,128)} %fusion.17), channel_id=1, replica_groups=mesh['layer'=16,'tx'=8,'ty'=2] {'layer'}, use_global_device_ids=true, to_apply=%region_11.12 | all-reduce | flops 64 | bytes 512 | tf_op jit(solution)/shard_map/psum | solution.py:152
  373.8 5.2 %fusion.1 = f32[4,3,8,32,128]{4,3,2,0,1:T(8,128)S(1)} fusion(f32[4,3,10,34,1]{4,3,2,0,1:T(8,128)} %copy.102, f32[4,3,10,1,128]{4,3,2,0,1:T(1,128)} %collective-permute-done.5, f32[4,3,10,1,128]{4,3,2,0,1:T(1,128)} %collective-permute-done.4, f32[4,3,1,32,128]{4,3,2,0,1:T(8,128)S(1)} %collective-permute-done.3, ...), kind=kLoop, calls=%fused_computation.19 | loop fusion | flops 13762560 | bytes 7233408 | tf_op jit(solution)/shard_map/sub | solution.py:51
  380.9 7.9 %scatter_fusion = f32[4,3,256,128]{3,0,2,1:T(4,128)S(1)} fusion(f32[4,3,256,128]{3,0,2,1:T(4,128)S(1)} %bitcast.193, s32[128]{0:T(128)S(1)} %copy-done.12, f32[128,4,3,128]{3,1,2,0:T(4,128)S(1)} %negate_bitcast_fusion), kind=kCustom, calls=%fused_computation.2 | custom fusion | flops 196608 | bytes 2359808 | tf_op jit(solution)/shard_map/scatter-add | solution.py:137
  388.8 8.2 %copy.108 = f32[4,1,8,32,128]{0,4,3,2,1:T(8,128)} copy(f32[4,1,8,32,128]{4,0,3,2,1:T(4,128)S(1)} %slice.238) | data formatting | bytes 1048576 | tf_op jit(solution)/shard_map/slice | solution.py:155
  397.0 13.0 %scatter_custom_fusion.1 = f32[4,32768]{0,1:T(8,128)} fusion(f32[4,32768]{0,1:T(8,128)} %bitcast.191, s32[128]{0:T(128)} %copy-done.11, f32[]{:T(128)} %constant.199.clone.1, f32[4,16]{0,1:T(8,128)S(1)} %psum.14, f32[128]{0:T(128)S(1)} %select_n.77), kind=kCustom, calls=%fused_computation.84 | custom fusion | flops 1536 | bytes 525568 | tf_op jit(solution)/shard_map/scatter-add | solution.py:155
  410.1 9.3 %copy.115 = f32[4,1,8,32,128]{4,0,3,2,1:T(4,128)S(1)} copy(f32[4,1,8,32,128]{0,4,3,2,1:T(8,128)} %bitcast.192) | data formatting | bytes 1048576 | tf_op jit(solution)/shard_map/reshape.91
  419.5 6.8 %fusion.14 = f32[4,4]{0,1:T(4,128)S(1)} fusion(f32[4,3,8,32,128]{4,0,3,2,1:T(4,128)S(1)} %constant_dynamic-update-slice_fusion), kind=kOutput, calls=%fused_computation.53 | convolution fusion | flops 18874384 | bytes 1572928 | tf_op jit(solution)/shard_map/dot_general | solution.py:167
  426.3 83.1 %psum.15 = f32[4,4]{0,1:T(4,128)S(1)} all-reduce(f32[4,4]{0,1:T(4,128)S(1)} %fusion.14), channel_id=1, replica_groups=mesh['layer'=16,'tx'=8,'ty'=2] {'layer','tx','ty'}, use_global_device_ids=true, to_apply=%region_13.14 | all-reduce | flops 16 | bytes 128 | tf_op jit(solution)/shard_map/psum | solution.py:168
  (243 shorter events, 104.9 us)
Async XLA Ops:
  0.7 2.0 copy-start.3
  0.7 2.0 copy-start.4
  7.6 98.0 %copy-start.5 = (f32[8,32,128]{2,1,0:T(8,128)S(1)}, f32[8,32,128]{2,1,0:T(8,128)}, u32[]{:S(2)}) copy-start(f32[8,32,128]{2,1,0:T(8,128)} %param.31) | copy-start | bytes 393220
  7.8 5.3 %collective-permute-start = (f32[4,4096]{1,0:T(4,128)S(1)}, f32[4,4096]{1,0:T(4,128)S(1)}, u32[]{:S(2)}, u32[]{:S(2)}) collective-permute-start(f32[4,4096]{1,0:T(4,128)S(1)} %multiply_add_fusion.6), channel_id=1, source_target_pairs={{0,16},{16,32},{32,48},{48,64},{64,80},{80,96},{96,112},{112,128},... | collective-permute-start | bytes 196616 | tf_op jit(solution)/shard_map/while/body/eval_jaxpr/ppermute | solution.py:12
  13.0 5.0 collective-permute-start
  18.1 5.0 collective-permute-start
  23.1 5.0 collective-permute-start
  28.2 5.1 collective-permute-start
  33.3 7.1 %collective-permute-start = (f32[4,4096]{1,0:T(4,128)S(1)}, f32[4,4096]{1,0:T(4,128)S(1)}, u32[]{:S(2)}, u32[]{:S(2)}) collective-permute-start(f32[4,4096]{1,0:T(4,128)S(1)} %multiply_add_fusion.6), channel_id=1, source_target_pairs={{0,16},{16,32},{32,48},{48,64},{64,80},{80,96},{96,112},{112,128},... | collective-permute-start | bytes 196616 | tf_op jit(solution)/shard_map/while/body/eval_jaxpr/ppermute | solution.py:12
  40.4 7.1 %collective-permute-start = (f32[4,4096]{1,0:T(4,128)S(1)}, f32[4,4096]{1,0:T(4,128)S(1)}, u32[]{:S(2)}, u32[]{:S(2)}) collective-permute-start(f32[4,4096]{1,0:T(4,128)S(1)} %multiply_add_fusion.6), channel_id=1, source_target_pairs={{0,16},{16,32},{32,48},{48,64},{64,80},{80,96},{96,112},{112,128},... | collective-permute-start | bytes 196616 | tf_op jit(solution)/shard_map/while/body/eval_jaxpr/ppermute | solution.py:12
  47.6 7.7 %collective-permute-start = (f32[4,4096]{1,0:T(4,128)S(1)}, f32[4,4096]{1,0:T(4,128)S(1)}, u32[]{:S(2)}, u32[]{:S(2)}) collective-permute-start(f32[4,4096]{1,0:T(4,128)S(1)} %multiply_add_fusion.6), channel_id=1, source_target_pairs={{0,16},{16,32},{32,48},{48,64},{64,80},{80,96},{96,112},{112,128},... | collective-permute-start | bytes 196616 | tf_op jit(solution)/shard_map/while/body/eval_jaxpr/ppermute | solution.py:12
  55.3 6.9 %collective-permute-start = (f32[4,4096]{1,0:T(4,128)S(1)}, f32[4,4096]{1,0:T(4,128)S(1)}, u32[]{:S(2)}, u32[]{:S(2)}) collective-permute-start(f32[4,4096]{1,0:T(4,128)S(1)} %multiply_add_fusion.6), channel_id=1, source_target_pairs={{0,16},{16,32},{32,48},{48,64},{64,80},{80,96},{96,112},{112,128},... | collective-permute-start | bytes 196616 | tf_op jit(solution)/shard_map/while/body/eval_jaxpr/ppermute | solution.py:12
  62.2 7.1 %collective-permute-start = (f32[4,4096]{1,0:T(4,128)S(1)}, f32[4,4096]{1,0:T(4,128)S(1)}, u32[]{:S(2)}, u32[]{:S(2)}) collective-permute-start(f32[4,4096]{1,0:T(4,128)S(1)} %multiply_add_fusion.6), channel_id=1, source_target_pairs={{0,16},{16,32},{32,48},{48,64},{64,80},{80,96},{96,112},{112,128},... | collective-permute-start | bytes 196616 | tf_op jit(solution)/shard_map/while/body/eval_jaxpr/ppermute | solution.py:12
  69.4 7.3 %collective-permute-start = (f32[4,4096]{1,0:T(4,128)S(1)}, f32[4,4096]{1,0:T(4,128)S(1)}, u32[]{:S(2)}, u32[]{:S(2)}) collective-permute-start(f32[4,4096]{1,0:T(4,128)S(1)} %multiply_add_fusion.6), channel_id=1, source_target_pairs={{0,16},{16,32},{32,48},{48,64},{64,80},{80,96},{96,112},{112,128},... | collective-permute-start | bytes 196616 | tf_op jit(solution)/shard_map/while/body/eval_jaxpr/ppermute | solution.py:12
  76.7 7.1 %collective-permute-start = (f32[4,4096]{1,0:T(4,128)S(1)}, f32[4,4096]{1,0:T(4,128)S(1)}, u32[]{:S(2)}, u32[]{:S(2)}) collective-permute-start(f32[4,4096]{1,0:T(4,128)S(1)} %multiply_add_fusion.6), channel_id=1, source_target_pairs={{0,16},{16,32},{32,48},{48,64},{64,80},{80,96},{96,112},{112,128},... | collective-permute-start | bytes 196616 | tf_op jit(solution)/shard_map/while/body/eval_jaxpr/ppermute | solution.py:12
  83.8 7.1 %collective-permute-start = (f32[4,4096]{1,0:T(4,128)S(1)}, f32[4,4096]{1,0:T(4,128)S(1)}, u32[]{:S(2)}, u32[]{:S(2)}) collective-permute-start(f32[4,4096]{1,0:T(4,128)S(1)} %multiply_add_fusion.6), channel_id=1, source_target_pairs={{0,16},{16,32},{32,48},{48,64},{64,80},{80,96},{96,112},{112,128},... | collective-permute-start | bytes 196616 | tf_op jit(solution)/shard_map/while/body/eval_jaxpr/ppermute | solution.py:12
  91.0 7.1 %collective-permute-start = (f32[4,4096]{1,0:T(4,128)S(1)}, f32[4,4096]{1,0:T(4,128)S(1)}, u32[]{:S(2)}, u32[]{:S(2)}) collective-permute-start(f32[4,4096]{1,0:T(4,128)S(1)} %multiply_add_fusion.6), channel_id=1, source_target_pairs={{0,16},{16,32},{32,48},{48,64},{64,80},{80,96},{96,112},{112,128},... | collective-permute-start | bytes 196616 | tf_op jit(solution)/shard_map/while/body/eval_jaxpr/ppermute | solution.py:12
  98.1 7.4 %collective-permute-start = (f32[4,4096]{1,0:T(4,128)S(1)}, f32[4,4096]{1,0:T(4,128)S(1)}, u32[]{:S(2)}, u32[]{:S(2)}) collective-permute-start(f32[4,4096]{1,0:T(4,128)S(1)} %multiply_add_fusion.6), channel_id=1, source_target_pairs={{0,16},{16,32},{32,48},{48,64},{64,80},{80,96},{96,112},{112,128},... | collective-permute-start | bytes 196616 | tf_op jit(solution)/shard_map/while/body/eval_jaxpr/ppermute | solution.py:12
  110.3 7.7 %collective-permute-start.1 = (f32[4,4096]{1,0:T(4,128)S(1)}, f32[4,4096]{1,0:T(4,128)S(1)}, u32[]{:S(2)}, u32[]{:S(2)}) collective-permute-start(f32[4,4096]{1,0:T(4,128)S(1)} %multiply_add_fusion.7), channel_id=1, source_target_pairs={{16,0},{32,16},{48,32},{64,48},{80,64},{96,80},{112,96},{128,112},... | collective-permute-start | bytes 196616 | tf_op jit(solution)/shard_map/while/body/eval_jaxpr/ppermute | solution.py:12
  118.0 7.2 %collective-permute-start.1 = (f32[4,4096]{1,0:T(4,128)S(1)}, f32[4,4096]{1,0:T(4,128)S(1)}, u32[]{:S(2)}, u32[]{:S(2)}) collective-permute-start(f32[4,4096]{1,0:T(4,128)S(1)} %multiply_add_fusion.7), channel_id=1, source_target_pairs={{16,0},{32,16},{48,32},{64,48},{80,64},{96,80},{112,96},{128,112},... | collective-permute-start | bytes 196616 | tf_op jit(solution)/shard_map/while/body/eval_jaxpr/ppermute | solution.py:12
  125.3 7.3 %collective-permute-start.1 = (f32[4,4096]{1,0:T(4,128)S(1)}, f32[4,4096]{1,0:T(4,128)S(1)}, u32[]{:S(2)}, u32[]{:S(2)}) collective-permute-start(f32[4,4096]{1,0:T(4,128)S(1)} %multiply_add_fusion.7), channel_id=1, source_target_pairs={{16,0},{32,16},{48,32},{64,48},{80,64},{96,80},{112,96},{128,112},... | collective-permute-start | bytes 196616 | tf_op jit(solution)/shard_map/while/body/eval_jaxpr/ppermute | solution.py:12
  132.6 7.8 %collective-permute-start.1 = (f32[4,4096]{1,0:T(4,128)S(1)}, f32[4,4096]{1,0:T(4,128)S(1)}, u32[]{:S(2)}, u32[]{:S(2)}) collective-permute-start(f32[4,4096]{1,0:T(4,128)S(1)} %multiply_add_fusion.7), channel_id=1, source_target_pairs={{16,0},{32,16},{48,32},{64,48},{80,64},{96,80},{112,96},{128,112},... | collective-permute-start | bytes 196616 | tf_op jit(solution)/shard_map/while/body/eval_jaxpr/ppermute | solution.py:12
  140.4 7.1 %collective-permute-start.1 = (f32[4,4096]{1,0:T(4,128)S(1)}, f32[4,4096]{1,0:T(4,128)S(1)}, u32[]{:S(2)}, u32[]{:S(2)}) collective-permute-start(f32[4,4096]{1,0:T(4,128)S(1)} %multiply_add_fusion.7), channel_id=1, source_target_pairs={{16,0},{32,16},{48,32},{64,48},{80,64},{96,80},{112,96},{128,112},... | collective-permute-start | bytes 196616 | tf_op jit(solution)/shard_map/while/body/eval_jaxpr/ppermute | solution.py:12
  147.6 7.1 %collective-permute-start.1 = (f32[4,4096]{1,0:T(4,128)S(1)}, f32[4,4096]{1,0:T(4,128)S(1)}, u32[]{:S(2)}, u32[]{:S(2)}) collective-permute-start(f32[4,4096]{1,0:T(4,128)S(1)} %multiply_add_fusion.7), channel_id=1, source_target_pairs={{16,0},{32,16},{48,32},{64,48},{80,64},{96,80},{112,96},{128,112},... | collective-permute-start | bytes 196616 | tf_op jit(solution)/shard_map/while/body/eval_jaxpr/ppermute | solution.py:12
  154.7 7.1 %collective-permute-start.1 = (f32[4,4096]{1,0:T(4,128)S(1)}, f32[4,4096]{1,0:T(4,128)S(1)}, u32[]{:S(2)}, u32[]{:S(2)}) collective-permute-start(f32[4,4096]{1,0:T(4,128)S(1)} %multiply_add_fusion.7), channel_id=1, source_target_pairs={{16,0},{32,16},{48,32},{64,48},{80,64},{96,80},{112,96},{128,112},... | collective-permute-start | bytes 196616 | tf_op jit(solution)/shard_map/while/body/eval_jaxpr/ppermute | solution.py:12
  161.9 8.0 %collective-permute-start.1 = (f32[4,4096]{1,0:T(4,128)S(1)}, f32[4,4096]{1,0:T(4,128)S(1)}, u32[]{:S(2)}, u32[]{:S(2)}) collective-permute-start(f32[4,4096]{1,0:T(4,128)S(1)} %multiply_add_fusion.7), channel_id=1, source_target_pairs={{16,0},{32,16},{48,32},{64,48},{80,64},{96,80},{112,96},{128,112},... | collective-permute-start | bytes 196616 | tf_op jit(solution)/shard_map/while/body/eval_jaxpr/ppermute | solution.py:12
  169.9 7.1 %collective-permute-start.1 = (f32[4,4096]{1,0:T(4,128)S(1)}, f32[4,4096]{1,0:T(4,128)S(1)}, u32[]{:S(2)}, u32[]{:S(2)}) collective-permute-start(f32[4,4096]{1,0:T(4,128)S(1)} %multiply_add_fusion.7), channel_id=1, source_target_pairs={{16,0},{32,16},{48,32},{64,48},{80,64},{96,80},{112,96},{128,112},... | collective-permute-start | bytes 196616 | tf_op jit(solution)/shard_map/while/body/eval_jaxpr/ppermute | solution.py:12
  177.0 7.4 %collective-permute-start.1 = (f32[4,4096]{1,0:T(4,128)S(1)}, f32[4,4096]{1,0:T(4,128)S(1)}, u32[]{:S(2)}, u32[]{:S(2)}) collective-permute-start(f32[4,4096]{1,0:T(4,128)S(1)} %multiply_add_fusion.7), channel_id=1, source_target_pairs={{16,0},{32,16},{48,32},{64,48},{80,64},{96,80},{112,96},{128,112},... | collective-permute-start | bytes 196616 | tf_op jit(solution)/shard_map/while/body/eval_jaxpr/ppermute | solution.py:12
  184.4 6.6 %collective-permute-start.1 = (f32[4,4096]{1,0:T(4,128)S(1)}, f32[4,4096]{1,0:T(4,128)S(1)}, u32[]{:S(2)}, u32[]{:S(2)}) collective-permute-start(f32[4,4096]{1,0:T(4,128)S(1)} %multiply_add_fusion.7), channel_id=1, source_target_pairs={{16,0},{32,16},{48,32},{64,48},{80,64},{96,80},{112,96},{128,112},... | collective-permute-start | bytes 196616 | tf_op jit(solution)/shard_map/while/body/eval_jaxpr/ppermute | solution.py:12
  191.0 7.1 %collective-permute-start.1 = (f32[4,4096]{1,0:T(4,128)S(1)}, f32[4,4096]{1,0:T(4,128)S(1)}, u32[]{:S(2)}, u32[]{:S(2)}) collective-permute-start(f32[4,4096]{1,0:T(4,128)S(1)} %multiply_add_fusion.7), channel_id=1, source_target_pairs={{16,0},{32,16},{48,32},{64,48},{80,64},{96,80},{112,96},{128,112},... | collective-permute-start | bytes 196616 | tf_op jit(solution)/shard_map/while/body/eval_jaxpr/ppermute | solution.py:12
  198.2 7.1 %collective-permute-start.1 = (f32[4,4096]{1,0:T(4,128)S(1)}, f32[4,4096]{1,0:T(4,128)S(1)}, u32[]{:S(2)}, u32[]{:S(2)}) collective-permute-start(f32[4,4096]{1,0:T(4,128)S(1)} %multiply_add_fusion.7), channel_id=1, source_target_pairs={{16,0},{32,16},{48,32},{64,48},{80,64},{96,80},{112,96},{128,112},... | collective-permute-start | bytes 196616 | tf_op jit(solution)/shard_map/while/body/eval_jaxpr/ppermute | solution.py:12
  205.3 7.1 %collective-permute-start.1 = (f32[4,4096]{1,0:T(4,128)S(1)}, f32[4,4096]{1,0:T(4,128)S(1)}, u32[]{:S(2)}, u32[]{:S(2)}) collective-permute-start(f32[4,4096]{1,0:T(4,128)S(1)} %multiply_add_fusion.7), channel_id=1, source_target_pairs={{16,0},{32,16},{48,32},{64,48},{80,64},{96,80},{112,96},{128,112},... | collective-permute-start | bytes 196616 | tf_op jit(solution)/shard_map/while/body/eval_jaxpr/ppermute | solution.py:12
  212.5 7.6 %collective-permute-start.1 = (f32[4,4096]{1,0:T(4,128)S(1)}, f32[4,4096]{1,0:T(4,128)S(1)}, u32[]{:S(2)}, u32[]{:S(2)}) collective-permute-start(f32[4,4096]{1,0:T(4,128)S(1)} %multiply_add_fusion.7), channel_id=1, source_target_pairs={{16,0},{32,16},{48,32},{64,48},{80,64},{96,80},{112,96},{128,112},... | collective-permute-start | bytes 196616 | tf_op jit(solution)/shard_map/while/body/eval_jaxpr/ppermute | solution.py:12
  220.6 2.8 copy-start
  226.4 62.1 %collective-permute-start.3 = (f32[4,3,1,32,128]{4,3,2,0,1:T(8,128)}, f32[4,3,1,32,128]{4,3,2,0,1:T(8,128)S(1)}, u32[]{:S(2)}, u32[]{:S(2)}) collective-permute-start(f32[4,3,1,32,128]{4,3,2,0,1:T(8,128)} %get-tuple-element.371), channel_id=1, source_target_pairs={{16,0},{32,16},{48,32},{64,48},{80,64},{96,80},{112,96},{128,112},... | collective-permute-start | bytes 589832 | tf_op jit(solution)/shard_map/ppermute | solution.py:25
  227.7 9.8 %copy-start.7 = (s32[1,1,1,16,8]{3,4,2,1,0:T(8,128)S(1)}, s32[1,1,1,16,8]{3,4,2,1,0:T(8,128)}, u32[]{:S(2)}) copy-start(s32[1,1,1,16,8]{3,4,2,1,0:T(8,128)} %param.35) | copy-start | bytes 1540
  227.7 10.0 %copy-start.6 = (s32[1,1,16,8]{2,3,1,0:T(8,128)S(1)}, s32[1,1,16,8]{2,3,1,0:T(8,128)}, u32[]{:S(2)}) copy-start(s32[1,1,16,8]{2,3,1,0:T(8,128)} %param.40) | copy-start | bytes 1540
  227.7 10.0 %copy-start.10 = (s32[1,1,16]{2,1,0:T(1,128)S(1)}, s32[1,1,16]{2,1,0:T(1,128)}, u32[]{:S(2)}) copy-start(s32[1,1,16]{2,1,0:T(1,128)} %param.39) | copy-start | bytes 196
  227.7 60.8 %collective-permute-start.2 = (f32[4,3,1,32,128]{4,3,2,0,1:T(8,128)}, f32[4,3,1,32,128]{4,3,2,0,1:T(8,128)}, u32[]{:S(2)}, u32[]{:S(2)}) collective-permute-start(f32[4,3,1,32,128]{4,3,2,0,1:T(8,128)} %get-tuple-element.370), channel_id=1, source_target_pairs={{0,16},{16,32},{32,48},{48,64},{64,80},{80,96},{96,112},{112,128},... | collective-permute-start | bytes 589832 | tf_op jit(solution)/shard_map/ppermute | solution.py:23
  238.7 57.3 %copy-start.11 = (s32[128]{0:T(128)}, s32[128]{0:T(128)S(1)}, u32[]{:S(2)}) copy-start(s32[128]{0:T(128)S(1)} %get-tuple-element.390) | copy-start | bytes 1540
  242.4 137.9 %all-to-all-start = ((f32[4,3,128,128]{3,0,1,2:T(4,128)}), f32[4,3,128,128]{3,0,1,2:T(4,128)S(1)}, u32[]{:S(2)}, u32[]{:S(2)}) async-start(f32[4,3,128,128]{3,0,1,2:T(4,128)} %select_bitcast_fusion), calls=%async_computation | async-start | bytes 1572864 | tf_op jit(solution)/shard_map/all_to_all | solution.py:133
  284.4 2.3 copy-start.8
  284.4 2.4 copy-start.13
  284.4 2.6 copy-start.9
  290.1 23.1 %collective-permute-start.5 = (f32[4,3,10,1,128]{4,3,2,0,1:T(1,128)}, f32[4,3,10,1,128]{4,3,2,0,1:T(1,128)}, u32[]{:S(2)}, u32[]{:S(2)}) collective-permute-start(f32[4,3,10,1,128]{4,3,2,0,1:T(1,128)} %get-tuple-element.367), channel_id=1, source_target_pairs={{2,0},{4,2},{6,4},{8,6},{10,8},{12,10},{14,12},{3,1},{5,3},{7,5},{... | collective-permute-start | bytes 184328 | tf_op jit(solution)/shard_map/ppermute | solution.py:25
  291.3 21.8 %collective-permute-start.4 = (f32[4,3,10,1,128]{4,3,2,0,1:T(1,128)}, f32[4,3,10,1,128]{4,3,2,0,1:T(1,128)}, u32[]{:S(2)}, u32[]{:S(2)}) collective-permute-start(f32[4,3,10,1,128]{4,3,2,0,1:T(1,128)} %get-tuple-element.366), channel_id=1, source_target_pairs={{0,2},{2,4},{4,6},{6,8},{8,10},{10,12},{12,14},{1,3},{3,5},{5,7},{... | collective-permute-start | bytes 184328 | tf_op jit(solution)/shard_map/ppermute | solution.py:23
  321.3 45.8 %collective-permute-start.7 = (f32[4,3,10,34,1]{3,2,4,1,0:T(8,128)}, f32[4,3,10,34,1]{3,2,4,1,0:T(8,128)}, u32[]{:S(2)}, u32[]{:S(2)}) collective-permute-start(f32[4,3,10,34,1]{3,2,4,1,0:T(8,128)} %copy.101), channel_id=1, source_target_pairs={{1,0},{3,2},{5,4},{7,6},{9,8},{11,10},{13,12},{15,14},{17,16},{19,... | collective-permute-start | bytes 48968 | tf_op jit(solution)/shard_map/ppermute | solution.py:25
  328.3 42.2 %collective-permute-start.6 = (f32[4,3,10,34,1]{3,2,4,1,0:T(8,128)}, f32[4,3,10,34,1]{3,2,4,1,0:T(8,128)}, u32[]{:S(2)}, u32[]{:S(2)}) collective-permute-start(f32[4,3,10,34,1]{3,2,4,1,0:T(8,128)} %copy.99), channel_id=1, source_target_pairs={{0,1},{2,3},{4,5},{6,7},{8,9},{10,11},{12,13},{14,15},{16,17},{18,... | collective-permute-start | bytes 48968 | tf_op jit(solution)/shard_map/ppermute | solution.py:23
  (3 other events, 3.3 us)
where the time goes:
time: 519 us; the launch traced here: 517 us
  starting transfers between devices  157 us (30%)
  blocking collectives  119 us (23%)
  waiting for transfers between devices  110 us (21%)
  local copies, waits for them, and re-layouts  75.7 us (15%)
  other arithmetic  42.3 us (8%)
  matrix products  10.1 us (2%)
    ppermute x30, waiting for transfers between devices, passed_along(): return lax.ppermute(array, axis, pairs)  110 us
    ppermute x30, starting transfers between devices, passed_along(): return lax.ppermute(array, axis, pairs)  96.1 us
    psum x1, blocking collectives, on_device(): gram = lax.psum(local_gram, ('layer', 'tx', 'ty'))  83.1 us
    all_to_all x1, starting transfers between devices, on_device(): lax.all_to_all(outgoing, ('tx', 'ty'), split_axis=2, concat_axis=2, tiled...  42 us
    psum x1, blocking collectives, on_device(): rates = lax.psum(partial_rates, 'layer')  35.8 us
    ppermute x3, starting transfers between devices, extended(): lax.ppermute(tail, axis, [(i, (i + 1) % count) for i in range(ends)])  13.3 us
    scatter-add x1, other arithmetic, on_device(): image[:, 0].reshape(krylov_cols, -1).at[:, spots]  13 us
  transfers between devices with their start and end apart: 37, of which 30 were waited for; matrix products, arithmetic and copies ran while one was open for 11% of the time, Pallas kernels for 0%

commit v1 on v0

v1 whole, which is shorter than its diff:
```python
import jax
import jax.numpy as jnp
from jax import lax
from jax.experimental import pallas as pl
from jax.experimental.pallas import tpu as pltpu
from jax.sharding import PartitionSpec as P

F32 = jnp.float32
COLS, COMPS, LAYERS, XS, LANES = 4, 3, 8, 32, 128
BLOCKS = XS // 8
PLANE = LAYERS * XS
TILES, SLOTS = 16, 8
CHUNKS = 16
MSG = 24
WELLS, PERFS = 16, 8
ALL = ("layer", "tx", "ty")


def iota(shape, dim):
    return lax.broadcasted_iota(jnp.int32, shape, dim)


def rows_at(plane, layer, block):
    return pl.ds(plane * PLANE + layer * XS + block * 8, 8)


def chunk_rows(row, block):
    return pl.ds(MSG * 8 * (block % 2) + row + block // 2, 8, stride=MSG)


def sweep_kernel(
    ids, cells, perfs, index, krylov, weights, pivots, lower, upper, diag0, diag3, diag6, inv,
    message, base, from_below, from_above, well_weights, drawn,
):
    for block in range(BLOCKS):
        levels = [[] for _ in range(COLS)]
        products = []
        for k in range(LAYERS):
            at = rows_at(0, k, block)
            restrict = [weights[rows_at(c, k, block), :] for c in range(COMPS)]
            pivot = pivots[at, :]
            ratio = lower[at, :]
            products.append(ratio if k == 0 else ratio * products[-1])
            for s in range(COLS):
                source = restrict[0] * krylov[rows_at(s * 3, k, block), :]
                source += restrict[1] * krylov[rows_at(s * 3 + 1, k, block), :]
                source += restrict[2] * krylov[rows_at(s * 3 + 2, k, block), :]
                level = pivot * source
                levels[s].append(level if k == 0 else level + ratio * levels[s][-1])
        for s in range(COLS):
            message[chunk_rows(2 * s, block), :] = levels[s][-1]
        message[chunk_rows(16, block), :] = products[-1]
        down = [None] * COLS
        low = high = None
        for k in reversed(range(LAYERS)):
            at = rows_at(0, k, block)
            ratio = upper[at, :]
            first = k == LAYERS - 1
            low = products[k] if first else products[k] + ratio * low
            high = ratio if first else ratio * high
            from_below[at, :] = low
            from_above[at, :] = high
            inverse = [inv[rows_at(c, k, block), :] for c in range(COMPS)]
            share = 1.0 - (
                inverse[0] * diag0[at, :] + inverse[1] * diag3[at, :] + inverse[2] * diag6[at, :]
            )
            drawn[rows_at(4, k, block), :] = share * low
            drawn[rows_at(5, k, block), :] = share * high
            for s in range(COLS):
                down[s] = levels[s][k] if first else levels[s][k] + ratio * down[s]
                base[rows_at(s, k, block), :] = down[s]
                value = inverse[0] * krylov[rows_at(s * 3, k, block), :]
                value += inverse[1] * krylov[rows_at(s * 3 + 1, k, block), :]
                value += inverse[2] * krylov[rows_at(s * 3 + 2, k, block), :]
                drawn[rows_at(s, k, block), :] = value + share * down[s]
        for s in range(COLS):
            message[chunk_rows(8 + 2 * s, block), :] = down[s]
        message[chunk_rows(18, block), :] = high
        message[chunk_rows(20, block), :] = low
    sub, lane = iota((8, LANES), 0), iota((8, LANES), 1)
    first_layer = ids[0, 0] * LAYERS
    total = jnp.zeros((8, LANES), F32)
    for w in range(WELLS):
        cell = cells[0, w]
        x, y = lax.shift_right_logical(cell, 7), cell & 127
        strength = jnp.zeros((8, LANES), F32)
        for p in range(PERFS):
            strength += jnp.where(sub == perfs[w, p] - first_layer, index[w, p], 0.0)
        well_weights[pl.ds(w * 8, 8), :] = strength
        picked = jnp.where(lane == y, strength, 0.0)
        for q in range(6):
            value = drawn[pl.ds(q * PLANE + x, 8, stride=XS), :] * picked
            total += pltpu.roll(value, (q * WELLS + w + LANES - y) & 127, 1)
    row = jnp.sum(total, axis=0, keepdims=True)
    message[pl.ds(22, CHUNKS, stride=MSG), :] = jnp.broadcast_to(row, (CHUNKS, LANES))
    message[pl.ds(23, CHUNKS, stride=MSG), :] = jnp.zeros((CHUNKS, LANES), F32)


def pick(matrix, chosen):
    high = matrix.astype(jnp.bfloat16)
    rest = matrix - high.astype(F32)
    middle = rest.astype(jnp.bfloat16)
    low = (rest - middle.astype(F32)).astype(jnp.bfloat16)
    chosen = chosen.astype(jnp.bfloat16)
    return (
        jnp.dot(high, chosen, preferred_element_type=F32)
        + jnp.dot(middle, chosen, preferred_element_type=F32)
        + jnp.dot(low, chosen, preferred_element_type=F32)
    )


def chain_kernel(ids, cells, message, reply, states):
    sub, lane = iota((8, LANES), 0), iota((8, LANES), 1)

    def spread(rows, first):
        pair = pltpu.roll(rows, (8 - first) % 8, 0) if first else rows
        pair = jnp.where(sub < 2, pair, 0.0)
        pair += pltpu.roll(pair, 2, 0)
        return pair + pltpu.roll(pair, 4, 0)

    tails = [message[pl.ds(l * MSG + 16, 8), :] for l in range(CHUNKS)]
    state = jnp.zeros((8, LANES), F32)
    entering = []
    for l in range(CHUNKS):
        entering.append(state)
        reply[pl.ds(l * MSG, 8), :] = state
        states[pl.ds(l * 8, 8), pl.ds(0, LANES)] = state
        if l < CHUNKS - 1:
            state = message[pl.ds(l * MSG, 8), :] + spread(tails[l], 0) * state
    state = jnp.zeros((8, LANES), F32)
    for l in reversed(range(CHUNKS)):
        reply[pl.ds(l * MSG + 8, 8), :] = state
        states[pl.ds(l * 8, 8), pl.ds(LANES, LANES)] = state
        if l > 0:
            state = (
                message[pl.ds(l * MSG + 8, 8), :]
                + spread(tails[l], 4) * entering[l]
                + spread(tails[l], 2) * state
            )
    me = ids[0, 0]
    wide = (2 * LANES, 2 * LANES)
    col = iota((1, 2 * LANES), 1)
    owner = jnp.zeros((1, 2 * LANES), jnp.int32)
    for w in range(WELLS):
        owner = jnp.where((col & 15) == w, cells[0, w], owner)
    line, column = iota(wide, 0), iota(wide, 1)
    place = (lax.shift_right_logical(column, 7) * 16 + me) * LANES + (line & 127)
    group = lax.shift_right_logical(column & 127, 4) - 4
    chosen = jnp.where(
        (jnp.broadcast_to(owner, wide) == place) & (group == lax.shift_right_logical(line, 7)),
        1.0,
        0.0,
    )
    found = pick(states[...], chosen)
    odd = (sub & 1) == 1
    total = jnp.zeros((8, LANES), F32)
    fixed = jnp.zeros((1, LANES), F32)
    for l in range(CHUNKS):
        row = tails[l][6:7, :]
        fixed += row
        here = found[l * 8 : l * 8 + 8, :]
        total += row * jnp.where(odd, here[:, LANES:], here[:, :LANES])
    rates = pltpu.roll(total, 64, 1) + pltpu.roll(total, 48, 1)
    fixed = jnp.broadcast_to(jnp.where(me == 0, fixed, 0.0), (8, LANES))
    for s in range(COLS):
        mine = fixed if s == 0 else pltpu.roll(fixed, LANES - 16 * s, 1)
        rates += jnp.where(sub == 2 * s, mine, 0.0)
    rates = jnp.where(lane < WELLS, rates, 0.0)
    for l in range(CHUNKS):
        reply[pl.ds(l * MSG + 16, 8), :] = rates


def precond_kernel(
    ids, send_rows, reply, base, from_below, from_above, krylov, diag0, diag3, diag6, inv,
    precond, x_a, x_b, layer_a, layer_b, outgoing, rates,
):
    for block in range(BLOCKS):
        below = [reply[chunk_rows(2 * s, block), :] for s in range(COLS)]
        above = [reply[chunk_rows(8 + 2 * s, block), :] for s in range(COLS)]
        for k in range(LAYERS):
            at = rows_at(0, k, block)
            low, high = from_below[at, :], from_above[at, :]
            diag = [diag0[at, :], diag3[at, :], diag6[at, :]]
            inverse = [inv[rows_at(e, k, block), :] for e in range(9)]
            for s in range(COLS):
                pressure = base[rows_at(s, k, block), :] + low * below[s] + high * above[s]
                residue = [
                    krylov[rows_at(s * 3 + c, k, block), :] - diag[c] * pressure
                    for c in range(COMPS)
                ]
                for c in range(COMPS):
                    value = (
                        inverse[3 * c] * residue[0]
                        + inverse[3 * c + 1] * residue[1]
                        + inverse[3 * c + 2] * residue[2]
                    )
                    precond[rows_at(s * 3 + c, k, block), :] = value + pressure if c == 0 else value
    layer_even = (ids[0, 0] & 1) == 0
    x_even = (ids[0, 1] & 1) == 0
    x_a[...] = precond[pl.ds(jnp.where(x_even, XS - 1, 0), 96, stride=XS), :]
    x_b[...] = precond[pl.ds(jnp.where(x_even, 0, XS - 1), 96, stride=XS), :]
    layer_first = pl.multiple_of(jnp.where(layer_even, (LAYERS - 1) * XS, 0), XS)
    layer_second = pl.multiple_of(jnp.where(layer_even, 0, (LAYERS - 1) * XS), XS)
    for plane in range(12):
        layer_a[pl.ds(plane * XS, XS), :] = precond[pl.ds(plane * PLANE + layer_first, XS), :]
        layer_b[pl.ds(plane * XS, XS), :] = precond[pl.ds(plane * PLANE + layer_second, XS), :]
    for u in range(TILES):
        for j in range(SLOTS):
            row = send_rows[u, j]
            outgoing[pl.ds(u * 96 + j * 8, 8), :] = precond[pl.ds(row, 8, stride=PLANE), :]
            outgoing[pl.ds(u * 96 + 64 + j * 4, 4), :] = precond[
                pl.ds(row + 8 * PLANE, 4, stride=PLANE), :
            ]
    total = reply[pl.ds(16, 8), :]
    for j in range(1, CHUNKS):
        total += reply[pl.ds(j * MSG + 16, 8), :]
    rates[...] = total


def image_kernel(
    ids, cells, recv_rows, counts, precond, across, x_a, x_b, layer_a, layer_b, arrived, coef,
    diag, faces, rates, well_weights, image, gram,
):
    sub, lane = iota((8, LANES), 0), iota((8, LANES), 1)
    layer_even = (ids[0, 0] & 1) == 0
    x_even = (ids[0, 1] & 1) == 0
    y_first = ids[0, 2] == 0
    image[...] = jnp.zeros(image.shape, F32)
    for u in range(TILES):
        for j in range(SLOTS):
            row = recv_rows[u, j]
            slot = u * SLOTS + j
            weight = jnp.where(j < counts[0, u], coef[pl.ds(slot, 1), :], 0.0)
            image[pl.ds(row, 8, stride=PLANE), :] -= weight * arrived[pl.ds(u * 96 + j * 8, 8), :]
            image[pl.ds(row + 8 * PLANE, 4, stride=PLANE), :] -= (
                weight * arrived[pl.ds(u * 96 + 64 + j * 4, 4), :]
            )
    rate = rates[...]
    rate = (rate + pltpu.roll(rate, 7, 0)) * (1.0 / PERFS)
    for w in range(WELLS):
        cell = cells[0, w]
        x, y = lax.shift_right_logical(cell, 7), cell & 127
        strength = well_weights[pl.ds(w * 8, 8), :]
        placed = pltpu.roll(jnp.where(lane == w, rate, 0.0), (y + LANES - w) & 127, 1)
        for s in range(COLS):
            image[pl.ds(s * 3 * PLANE + x, 8, stride=XS), :] += strength * placed[2 * s : 2 * s + 1, :]
    sums = {}
    row_x = iota((XS, LANES), 0)
    lane_y = iota((XS, LANES), 1)

    def column(k, _):
        def at(plane, size=XS, layer=None):
            layer = k if layer is None else layer
            return pl.ds(pl.multiple_of(plane * PLANE + layer * XS, XS), size)

        totals = list(_)
        blocks = [diag[at(e), :] for e in range(9)]
        face = [faces[at(f), :] for f in range(6)]
        images = []
        for s in range(COLS):
            value = [precond[at(s * 3 + c), :] for c in range(COMPS)]
            for c in range(COMPS):
                plane = s * 3 + c
                here = value[c]
                out = image[at(plane), :]
                out += blocks[3 * c] * value[0]
                out += blocks[3 * c + 1] * value[1]
                out += blocks[3 * c + 2] * value[2]
                edge = pl.ds(plane * XS, XS)
                inner = precond[at(plane, layer=jnp.maximum(k - 1, 0)), :]
                outer = jnp.where(layer_even, layer_b[edge, :], layer_a[edge, :])
                out -= face[0] * jnp.where(k == 0, outer, inner)
                inner = precond[at(plane, layer=jnp.minimum(k + 1, LAYERS - 1)), :]
                outer = jnp.where(layer_even, layer_a[edge, :], layer_b[edge, :])
                out -= face[1] * jnp.where(k == LAYERS - 1, outer, inner)
                side = pl.ds(plane * LAYERS + k, 1)
                first, second = x_a[side, :], x_b[side, :]
                outer = jnp.where(x_even, second, first)
                out -= face[2] * jnp.where(row_x == 0, outer, pltpu.roll(here, 1, 0))
                outer = jnp.where(x_even, first, second)
                out -= face[3] * jnp.where(row_x == XS - 1, outer, pltpu.roll(here, XS - 1, 0))
                other = across[at(plane), :]
                edge_low = jnp.where(y_first, 0.0, other)
                edge_high = jnp.where(y_first, other, 0.0)
                out -= face[4] * pltpu.roll(jnp.where(lane_y == LANES - 1, edge_low, here), 1, 1)
                out -= face[5] * pltpu.roll(jnp.where(lane_y == 0, edge_high, here), LANES - 1, 1)
                image[at(plane), :] = out
                images.append(out)
        n = 0
        for s in range(COLS):
            for t in range(s + 1):
                value = images[s * 3] * images[t * 3]
                value += images[s * 3 + 1] * images[t * 3 + 1]
                value += images[s * 3 + 2] * images[t * 3 + 2]
                totals[n] += jnp.sum(value.reshape(BLOCKS, 8, LANES), axis=0)
                n += 1
        return tuple(totals)

    sums = lax.fori_loop(
        0, LAYERS, column, tuple(jnp.zeros((8, LANES), F32) for _ in range(10))
    )
    packed = jnp.zeros((1, LANES), F32)
    lanes = iota((1, LANES), 1)
    for n in range(10):
        value = jnp.sum(jnp.sum(sums[n], axis=0, keepdims=True), axis=1, keepdims=True)
        packed = jnp.where(lanes == n, value, packed)
    gram[...] = jnp.broadcast_to(packed, gram.shape)


def factor_kernel(scale, gathered, image, q, factor):
    total = jnp.sum(gathered[...].reshape(-1, 8, LANES), axis=0)
    total = jnp.sum(total, axis=0, keepdims=True) * scale
    lanes = iota((1, LANES), 1)
    entry, n = {}, 0
    for s in range(COLS):
        for t in range(s + 1):
            entry[s, t] = jnp.sum(jnp.where(lanes == n, total, 0.0), axis=1, keepdims=True)
            n += 1
    lower = {}
    for t in range(COLS):
        value = entry[t, t]
        for i in range(t):
            value -= lower[t, i] * lower[t, i]
        lower[t, t] = jnp.sqrt(value)
        for s in range(t + 1, COLS):
            value = entry[s, t]
            for i in range(t):
                value -= lower[s, i] * lower[t, i]
            lower[s, t] = value / lower[t, t]
    line, col = iota((COLS, COLS), 0), iota((COLS, COLS), 1)
    result = jnp.zeros((COLS, COLS), F32)
    for (s, t), value in lower.items():
        result = jnp.where((line == t) & (col == s), value, result)
    factor[...] = result
    wide = {key: jnp.broadcast_to(value, (8, LANES)) for key, value in lower.items()}
    inverse = {t: 1.0 / wide[t, t] for t in range(COLS)}

    def step(i, _):
        at = pl.multiple_of(i * 8, 8)
        done = []
        for s in range(COLS):
            for_s = []
            for c in range(COMPS):
                value = image[pl.ds((s * 3 + c) * PLANE + at, 8), :]
                for t in range(s):
                    value -= wide[s, t] * done[t][c]
                value *= inverse[s]
                q[pl.ds((s * 3 + c) * PLANE + at, 8), :] = value
                for_s.append(value)
            done.append(for_s)
        return _

    lax.fori_loop(0, PLANE // 8, step, 0, unroll=4)


SMEM = pl.BlockSpec(memory_space=pltpu.SMEM)
VMEM = pl.BlockSpec(memory_space=pltpu.VMEM)


def part(plane, planes=1):
    return pl.BlockSpec((planes * PLANE, LANES), lambda i: (plane, 0))


def whole(rows):
    return pl.BlockSpec((rows, LANES), lambda i: (0, 0))


def shape(*rows):
    return tuple(jax.ShapeDtypeStruct((r, LANES), F32) for r in rows)


def call(kernel, name, outs, ins, smems=1, scratch=(), flops=1_000_000):
    def run(*args):
        specs = [SMEM] * smems
        for arg, spec in zip(args[smems:], ins, strict=True):
            specs.append(whole(arg.shape[0]) if spec is None else spec)
        size = sum(a.size * 4 for a in args)
        return pl.pallas_call(
            kernel,
            name=name,
            grid=(1,),
            out_shape=outs,
            in_specs=specs,
            out_specs=tuple(
                pl.BlockSpec(o.shape, lambda i: (0,) * len(o.shape)) for o in outs
            ),
            scratch_shapes=list(scratch),
            compiler_params=pltpu.CompilerParams(vmem_limit_bytes=28 << 20),
            cost_estimate=pl.CostEstimate(flops=flops, bytes_accessed=size, transcendentals=0),
        )(*args)

    return run


def pairs(size, odd):
    found = []
    for i in range(1 if odd else 0, size - 1, 2):
        found += [(i, i + 1), (i + 1, i)]
    return found


def on_device(
    krylov_block,
    weights,
    pivots,
    lower_ratio,
    upper_ratio,
    block_diag,
    block_inv,
    face_coef,
    fault_send_rows,
    fault_recv_rows,
    fault_counts,
    fault_coef,
    well_cells,
    well_perfs,
    well_index,
):
    n_layer, n_tx, n_ty = (lax.axis_size(a) for a in ALL)

    def flat(array):
        return array.reshape(-1, LANES)

    krylov, diag, inv, faces = (
        flat(a) for a in (krylov_block, block_diag, block_inv, face_coef)
    )
    ids = jnp.stack([lax.axis_index(a) for a in ALL]).astype(jnp.int32).reshape(1, 3)
    cells = well_cells.reshape(1, WELLS)
    perfs = well_perfs.reshape(WELLS, PERFS)
    index = well_index.reshape(WELLS, PERFS)
    send_rows = fault_send_rows.reshape(TILES, SLOTS)
    recv_rows = fault_recv_rows.reshape(TILES, SLOTS)
    counts = fault_counts.reshape(1, TILES)
    columns = (part(0), part(3), part(6))
    message, base, from_below, from_above, well_weights = call(
        sweep_kernel,
        "sweep",
        shape(CHUNKS * MSG, COLS * PLANE, PLANE, PLANE, WELLS * 8),
        (None,) * 5 + columns + (part(0, 3),),
        smems=4,
        scratch=(pltpu.VMEM((6 * PLANE, LANES), F32),),
    )(
        ids, cells, perfs, index, krylov, flat(weights), flat(pivots), flat(lower_ratio),
        flat(upper_ratio), diag, diag, diag, inv,
    )
    message = lax.all_to_all(
        message.reshape(CHUNKS, MSG, LANES), "layer", split_axis=0, concat_axis=0, tiled=True
    )
    (reply,) = call(
        chain_kernel,
        "chain",
        shape(CHUNKS * MSG),
        (None,),
        smems=2,
        scratch=(pltpu.VMEM((LANES, 2 * LANES), F32),),
    )(ids, cells, flat(message))
    reply = lax.all_to_all(
        reply.reshape(CHUNKS, MSG, LANES), "layer", split_axis=0, concat_axis=0, tiled=True
    )
    precond, x_a, x_b, layer_a, layer_b, outgoing, rates = call(
        precond_kernel,
        "precond",
        shape(12 * PLANE, 96, 96, 12 * XS, 12 * XS, TILES * 96, 8),
        (None,) * 5 + columns + (None,),
        smems=2,
    )(
        ids, send_rows, flat(reply), base, from_below, from_above, krylov, diag, diag, diag, inv
    )
    across = lax.ppermute(precond, "ty", pairs(n_ty, False))
    x_a = lax.ppermute(x_a, "tx", pairs(n_tx, False))
    x_b = lax.ppermute(x_b, "tx", pairs(n_tx, True))
    layer_a = lax.ppermute(layer_a, "layer", pairs(n_layer, False))
    layer_b = lax.ppermute(layer_b, "layer", pairs(n_layer, True))
    arrived = lax.all_to_all(
        outgoing.reshape(TILES, 96, LANES), ("tx", "ty"), split_axis=0, concat_axis=0, tiled=True
    )
    devices = n_layer * n_tx * n_ty
    image, gram = call(
        image_kernel,
        "image",
        shape(12 * PLANE, devices),
        (None,) * 12,
        smems=4,
    )(
        ids, cells, recv_rows, counts, precond, across, x_a, x_b, layer_a, layer_b, flat(arrived),
        flat(fault_coef), diag, faces, rates, well_weights,
    )
    gathered = lax.all_to_all(gram, ALL, split_axis=0, concat_axis=0, tiled=True)
    entries = float(12 * PLANE * LANES // COLS * devices)

    def factor(*refs):
        factor_kernel(1.0 / entries, *refs)

    q, r_factor = call(
        factor,
        "factor",
        shape(12 * PLANE) + (jax.ShapeDtypeStruct((COLS, COLS), F32),),
        (None, None),
        smems=0,
    )(gathered, image)
    return (q.reshape(krylov_block.shape), r_factor)


def solution(mesh):
    placed = (
        P(None, None, "layer", "tx", "ty"),
        P(None, "layer", "tx", "ty"),
        P("layer", "tx", "ty"),
        P("layer", "tx", "ty"),
        P("layer", "tx", "ty"),
        P(None, "layer", "tx", "ty"),
        P(None, "layer", "tx", "ty"),
        P(None, "layer", "tx", "ty"),
        P("layer", "tx", "ty", None, None),
        P("layer", "tx", "ty", None, None),
        P("layer", "tx", "ty", None),
        P("layer", "tx", "ty", None, None, None),
        P("tx", "ty", None),
        P("tx", "ty", None, None),
        P("tx", "ty", None, None),
    )
    return jax.shard_map(
        on_device,
        mesh=mesh,
        in_specs=placed,
        out_specs=(P(None, None, "layer", "tx", "ty"), P()),
        check_vma=False,
    )
```

time: 519 us -> 116 us (0.22)
  starting transfers between devices: 157 us -> 20.1 us
  blocking collectives: 119 us -> 33.6 us
  waiting for transfers between devices: 110 us -> 24.7 us
  local copies, waits for them, and re-layouts: 75.7 us -> 21.4 us
  other arithmetic: 42.3 us -> 0.08 us
  Pallas kernels: 0 us -> 14.8 us
  matrix products: 10.1 us -> 0 us
    psum x2 -> x0, blocking collectives: 119 us -> none  [the longest x1 83.1 us: on_device(): gram = lax.psum(local_gram, ('layer', 'tx', 'ty'))]
    ppermute x36 -> x5, starting transfers between devices: 115 us -> 7.53 us  [the longest x1 3.25 us: on_device(): across = lax.ppermute(precond, 'ty', pairs(n_ty, False))]
    ppermute x36 -> x5, waiting for transfers between devices: 110 us -> 15.4 us  [the longest x1 15.4 us: on_device(): x_a = lax.ppermute(x_a, 'tx', pairs(n_tx, False))]
    all_to_all x0 -> x2, blocking collectives: none -> 33.6 us  [the longest x1 18.9 us: on_device(): lax.all_to_all(gram, ALL, split_axis=0, concat_axis=0, tiled=True)]
    all_to_all x1 -> x2, starting transfers between devices: 42 us -> 12.6 us  [the longest x1 9.05 us: on_device(): lax.all_to_all(outgoing.reshape(TILES, 96, LANES), ('tx', 'ty'), split_ax...]
    scatter-add x3 -> x0, other arithmetic: 21.1 us -> none  [the longest x1 13 us: on_device(): image[:, 0].reshape(krylov_cols, -1).at[:, spots]]
    slice x8 -> x0, local copies, waits for them, and re-layouts: 19.6 us -> none  [the longest x2 8.28 us: on_device(): image[:, 0].reshape(krylov_cols, -1).at[:, spots]]
    pallas_call x0 -> x5, Pallas kernels: none -> 14.8 us  [run(): pl.pallas_call(kernel, name=name, grid=(1,), out_shape=outs, in_specs=spe...]
  transfers between devices with their start and end apart: 37 -> 7, of which waited for: 30 -> 3; matrix products, arithmetic and copies ran while one was open for 11% -> 1% of each run, Pallas kernels for 0% -> 0%
where the time goes in v1:
time: 116 us; the launch traced here: 115 us
  blocking collectives  33.6 us (29%)
  waiting for transfers between devices  24.7 us (21%)
  local copies, waits for them, and re-layouts  21.4 us (18%)
  starting transfers between devices  20.1 us (17%)
  Pallas kernels  14.8 us (13%)
    unnamed x58, local copies, waits for them, and re-layouts  19 us
    all_to_all x1, blocking collectives, on_device(): lax.all_to_all(gram, ALL, split_axis=0, concat_axis=0, tiled=True)  18.9 us
    ppermute x1, waiting for transfers between devices, on_device(): x_a = lax.ppermute(x_a, 'tx', pairs(n_tx, False))  15.4 us
    pallas_call x5, Pallas kernels, run(): pl.pallas_call(kernel, name=name, grid=(1,), out_shape=outs, in_specs=spe...  14.8 us
    all_to_all x1, blocking collectives, on_device(): lax.all_to_all(message.reshape(CHUNKS, MSG, LANES), 'layer', split_axis=0...  14.7 us
    all_to_all x1, starting transfers between devices, on_device(): lax.all_to_all(outgoing.reshape(TILES, 96, LANES), ('tx', 'ty'), split_ax...  9.05 us
    all_to_all x1, waiting for transfers between devices, on_device(): lax.all_to_all(reply.reshape(CHUNKS, MSG, LANES), 'layer', split_axis=0,...  7.07 us
    all_to_all x1, starting transfers between devices, on_device(): lax.all_to_all(reply.reshape(CHUNKS, MSG, LANES), 'layer', split_axis=0,...  3.53 us
  transfers between devices with their start and end apart: 7, of which 3 were waited for; matrix products, arithmetic and copies ran while one was open for 1% of the time, Pallas kernels for 0%

profile of v1, /device:TPU:1, one launch (start us, length us, event | category | flops | bytes accessed | tf_op | source)
XLA Modules:
  0.0 115.4 jit_solution(10617758338832418623)
XLA Ops:
  0.6 0.8 copy.21.perfs
  1.4 0.8 copy.22.index
  2.2 0.1 add_bitcast_fusion.ids
  2.2 1.3 %copy-done = f32[9,8,32,128]{3,2,1,0:T(8,128)S(1)} copy-done((f32[9,8,32,128]{3,2,1,0:T(8,128)S(1)}, f32[9,8,32,128]{3,2,1,0:T(8,128)}, u32[]{:S(2)}) %copy-start) | copy-done | bytes 1179672
  3.5 1.4 %copy-done.2 = f32[4,3,8,32,128]{4,3,2,1,0:T(8,128)S(1)} copy-done((f32[4,3,8,32,128]{4,3,2,1,0:T(8,128)S(1)}, f32[4,3,8,32,128]{4,3,2,1,0:T(8,128)}, u32[]{:S(2)}) %copy-start.2) | copy-done | bytes 1572888
  4.9 1.3 %copy-done.4 = f32[9,8,32,128]{3,2,1,0:T(8,128)S(1)} copy-done((f32[9,8,32,128]{3,2,1,0:T(8,128)S(1)}, f32[9,8,32,128]{3,2,1,0:T(8,128)}, u32[]{:S(2)}) %copy-start.4) | copy-done | bytes 1179672
  6.2 1.0 copy-done.8
  7.2 0.9 copy-done.13
  8.1 0.9 copy-done.14
  9.0 0.9 copy-done.15
  9.9 0.7 copy-done.19
  10.6 1.9 %sweep.1 = (f32[384,128]{1,0:T(8,128)S(1)}, f32[1024,128]{1,0:T(8,128)S(1)}, f32[256,128]{1,0:T(8,128)S(1)}, f32[256,128]{1,0:T(8,128)S(1)}, f32[128,128]{1,0:T(8,128)S(1)}) custom-call(s32[1,3]{1,0:T(1,128)S(1)} %add_bitcast_fusion.ids, s32[1,16]{1,0:T(1,128)S(1)} %bitcast.55, s32[16,8]{1,0:T(8,128)S(1)} %copy.21.perfs, f32[16,8]{1,0:T(8,128)S(1)} %copy.22.index, ...), custom_call_target="tpu_custom_call" | custom-call | flops 1000000 | bytes 7078988 | tf_op jit(solution)/shard_map/sweep/pallas_call | solution.py:378
  12.4 0.0 copy-start.1
  12.5 14.7 %all_to_all.26 = f32[16,24,128]{2,1,0:T(8,128)S(1)} all-to-all(f32[16,24,128]{2,1,0:T(8,128)S(1)} %bitcast.49), channel_id=1, replica_groups=mesh['layer'=16,'tx'=8,'ty'=2] {'layer'}, dimensions={0} | all-to-all | bytes 393216 | tf_op jit(solution)/shard_map/all_to_all | solution.py:446
  27.2 1.6 %chain.1 = f32[384,128]{1,0:T(8,128)} custom-call(s32[1,3]{1,0:T(1,128)S(1)} %add_bitcast_fusion.ids, s32[1,16]{1,0:T(1,128)S(1)} %bitcast.56, f32[384,128]{1,0:T(8,128)S(1)} %bitcast.45), custom_call_target="tpu_custom_call" | custom-call | flops 1000000 | bytes 196684 | tf_op jit(solution)/shard_map/chain/pallas_call | solution.py:378
  28.8 3.5 %all-to-all-start.1 = ((f32[16,24,128]{2,1,0:T(8,128)}), f32[16,24,128]{2,1,0:T(8,128)S(1)}, u32[]{:S(2)}, u32[]{:S(2)}) async-start(f32[16,24,128]{2,1,0:T(8,128)} %bitcast.19), calls=%async_computation.1 | async-start | bytes 393216 | tf_op jit(solution)/shard_map/all_to_all | solution.py:457
  32.4 0.1 copy.23.send_rows
  32.4 7.1 %all-to-all-done.1 = f32[16,24,128]{2,1,0:T(8,128)S(1)} async-done(((f32[16,24,128]{2,1,0:T(8,128)}), f32[16,24,128]{2,1,0:T(8,128)S(1)}, u32[]{:S(2)}, u32[]{:S(2)}) %all-to-all-start.1) | async-done | bytes 196640 | tf_op jit(solution)/shard_map/all_to_all | solution.py:457
  39.5 1.3 %copy-done.5 = f32[9,8,32,128]{3,2,1,0:T(8,128)S(1)} copy-done((f32[9,8,32,128]{3,2,1,0:T(8,128)S(1)}, f32[9,8,32,128]{3,2,1,0:T(8,128)}, u32[]{:S(2)}) %copy-start.5) | copy-done | bytes 1179672
  40.8 0.9 copy-done.10
  41.7 0.9 copy-done.12
  42.6 3.3 %precond.1 = (f32[3072,128]{1,0:T(8,128)}, f32[96,128]{1,0:T(8,128)S(1)}, f32[96,128]{1,0:T(8,128)S(1)}, f32[384,128]{1,0:T(8,128)S(1)}, f32[384,128]{1,0:T(8,12...) custom-call(s32[1,3]{1,0:T(1,128)S(1)} %add_bitcast_fusion.ids, s32[16,8]{1,0:T(8,128)S(1)} %copy.23.send_rows, ...), custom_call_target="tpu_custom_call" | custom-call | flops 1000000 | bytes 7275020 | tf_op jit(solution)/shard_map/precond/pallas_call | solution.py:378
  45.9 0.9 copy-done.7
  46.8 0.7 copy-done.24
  47.5 0.7 copy-done.25
  48.1 0.6 copy-done.26
  48.8 0.6 copy-done.27
  49.4 3.3 %collective-permute-start = (f32[3072,128]{1,0:T(8,128)}, f32[3072,128]{1,0:T(8,128)S(1)}, u32[]{:S(2)}, u32[]{:S(2)}) collective-permute-start(f32[3072,128]{1,0:T(8,128)} %get-tuple-element.22.precond), channel_id=1, source_target_pairs={{0,1},{1,0},{2,3},{3,2},{4,5},{5,4},{6,7},{7,6},{8,9},{9,8},{10,11... | collective-permute-start | bytes 4718600 | tf_op jit(solution)/shard_map/ppermute | solution.py:469
  52.6 9.0 %all-to-all-start.2 = ((f32[16,96,128]{2,1,0:T(8,128)}), f32[16,96,128]{2,1,0:T(8,128)S(1)}, u32[]{:S(2)}, u32[]{:S(2)}) async-start(f32[16,96,128]{2,1,0:T(8,128)} %bitcast.44), calls=%async_computation.2 | async-start | bytes 1572864 | tf_op jit(solution)/shard_map/all_to_all | solution.py:474
  61.7 0.3 collective-permute-start.3
  62.0 1.3 %collective-permute-start.4 = (f32[384,128]{1,0:T(8,128)}, f32[384,128]{1,0:T(8,128)}, u32[]{:S(2)}, u32[]{:S(2)}) collective-permute-start(f32[384,128]{1,0:T(8,128)} %copy-done.24), channel_id=1, source_target_pairs={{16,32},{32,16},{48,64},{64,48},{80,96},{96,80},{112,128},{128,112... | collective-permute-start | bytes 589832 | tf_op jit(solution)/shard_map/ppermute | solution.py:473
  63.3 1.4 %collective-permute-start.1 = (f32[96,128]{1,0:T(8,128)}, f32[96,128]{1,0:T(8,128)}, u32[]{:S(2)}, u32[]{:S(2)}) collective-permute-start(f32[96,128]{1,0:T(8,128)} %copy-done.27), channel_id=1, source_target_pairs={{0,2},{2,0},{4,6},{6,4},{8,10},{10,8},{12,14},{14,12},{1,3},{3,1},... | collective-permute-start | bytes 147464 | tf_op jit(solution)/shard_map/ppermute | solution.py:470
  64.7 1.3 %collective-permute-start.2 = (f32[96,128]{1,0:T(8,128)}, f32[96,128]{1,0:T(8,128)}, u32[]{:S(2)}, u32[]{:S(2)}) collective-permute-start(f32[96,128]{1,0:T(8,128)} %copy-done.26), channel_id=1, source_target_pairs={{2,4},{4,2},{6,8},{8,6},{10,12},{12,10},{3,5},{5,3},{7,9},{9,7},{1... | collective-permute-start | bytes 147464 | tf_op jit(solution)/shard_map/ppermute | solution.py:471
  66.0 0.8 copy.24.recv_rows
  66.7 15.4 %collective-permute-done.1.x_a = f32[96,128]{1,0:T(8,128)} collective-permute-done((f32[96,128]{1,0:T(8,128)}, f32[96,128]{1,0:T(8,128)}, u32[]{:S(2)}, u32[]{:S(2)}) %collective-permute-start.1) | collective-permute-done | bytes 49184 | tf_op jit(solution)/shard_map/ppermute | solution.py:470
  82.1 0.0 collective-permute-done.2.x_b
  82.1 0.0 collective-permute-done.3.layer_a
  82.1 0.0 collective-permute-done.4.layer_b
  82.1 2.2 %all-to-all-done.2 = f32[16,96,128]{2,1,0:T(8,128)S(1)} async-done(((f32[16,96,128]{2,1,0:T(8,128)}), f32[16,96,128]{2,1,0:T(8,128)S(1)}, u32[]{:S(2)}, u32[]{:S(2)}) %all-to-all-start.2) | async-done | bytes 786464 | tf_op jit(solution)/shard_map/all_to_all | solution.py:474
  84.3 0.0 collective-permute-done.across
  84.4 1.1 copy-done.6
  85.5 0.8 copy-done.16
  86.3 0.8 copy-done.18
  87.2 0.7 copy-done.22
  87.8 0.7 copy-done.23
  88.5 6.5 %image.1 = (f32[3072,128]{1,0:T(8,128)S(1)}, f32[256,128]{1,0:T(8,128)S(1)}) custom-call(s32[1,3]{1,0:T(1,128)S(1)} %add_bitcast_fusion.ids, s32[1,16]{1,0:T(1,128)S(1)} %bitcast.57, s32[16,8]{1,0:T(8,128)S(1)} %copy.24.recv_rows, s32[1,16]{1,0:T(1,128)S(1)} %bitcast.58, f32[3072,128]{1,0:T(8,128)} %get-tuple-element.22.precond, ...), custom_call_target="tpu_custom_call" | custom-call | flops 1000000 | bytes 6525580 | tf_op jit(solution)/shard_map/image/pallas_call | solution.py:378
  95.0 18.9 %all_to_all.27 = f32[256,1,128]{2,1,0:T(1,128)S(1)} all-to-all(f32[256,1,128]{2,1,0:T(1,128)S(1)} %bitcast.50), channel_id=1, replica_groups=mesh['layer'=16,'tx'=8,'ty'=2] {'layer','tx','ty'}, dimensions={0} | all-to-all | bytes 262144 | tf_op jit(solution)/shard_map/all_to_all | solution.py:488
  113.9 1.6 %factor.1 = (f32[3072,128]{1,0:T(8,128)}, f32[4,4]{1,0:T(4,128)}) custom-call(f32[256,128]{1,0:T(8,128)S(1)} %bitcast.47, f32[3072,128]{1,0:T(8,128)S(1)} %get-tuple-element.31.refs_1_), custom_call_target="tpu_custom_call" | custom-call | flops 1000000 | bytes 1703936 | tf_op jit(solution)/shard_map/factor/pallas_call | solution.py:378
  (36 shorter events, 0.1 us)
Async XLA Ops:
  2.2 1.3 %copy-start = (f32[9,8,32,128]{3,2,1,0:T(8,128)S(1)}, f32[9,8,32,128]{3,2,1,0:T(8,128)}, u32[]{:S(2)}) copy-start(f32[9,8,32,128]{3,2,1,0:T(8,128)} %param.20) | copy-start | bytes 3538948
  3.5 1.4 %copy-start.2 = (f32[4,3,8,32,128]{4,3,2,1,0:T(8,128)S(1)}, f32[4,3,8,32,128]{4,3,2,1,0:T(8,128)}, u32[]{:S(2)}) copy-start(f32[4,3,8,32,128]{4,3,2,1,0:T(8,128)} %param.15) | copy-start | bytes 4718596
  4.9 1.3 %copy-start.4 = (f32[9,8,32,128]{3,2,1,0:T(8,128)S(1)}, f32[9,8,32,128]{3,2,1,0:T(8,128)}, u32[]{:S(2)}) copy-start(f32[9,8,32,128]{3,2,1,0:T(8,128)} %param.21) | copy-start | bytes 3538948
  6.2 1.0 copy-start.8
  7.2 0.9 copy-start.13
  8.1 0.9 copy-start.14
  9.0 0.9 copy-start.15
  9.9 0.7 copy-start.19
  10.5 21.8 %copy-start.28 = (s32[1,1,1,16,8]{3,4,2,1,0:T(8,128)S(1)}, s32[1,1,1,16,8]{3,4,2,1,0:T(8,128)}, u32[]{:S(2)}) copy-start(s32[1,1,1,16,8]{3,4,2,1,0:T(8,128)} %param.23) | copy-start | bytes 1540
  10.5 29.0 %copy-start.3 = (f32[4,3,8,32,128]{4,3,2,1,0:T(8,128)S(1)}, f32[4,3,8,32,128]{4,3,2,1,0:T(8,128)}, u32[]{:S(2)}) copy-start(f32[4,3,8,32,128]{4,3,2,1,0:T(8,128)} %param.15) | copy-start | bytes 4718596
  12.4 16.4 %copy-start.9 = (f32[256,128]{1,0:T(8,128)}, f32[256,128]{1,0:T(8,128)S(1)}, u32[]{:S(2)}) copy-start(f32[256,128]{1,0:T(8,128)S(1)} %get-tuple-element.20.from_below) | copy-start | bytes 393220
  12.4 16.4 %copy-start.11 = (f32[256,128]{1,0:T(8,128)}, f32[256,128]{1,0:T(8,128)S(1)}, u32[]{:S(2)}) copy-start(f32[256,128]{1,0:T(8,128)S(1)} %get-tuple-element.21.from_above) | copy-start | bytes 393220
  12.4 16.4 %copy-start.17 = (f32[128,128]{1,0:T(8,128)}, f32[128,128]{1,0:T(8,128)S(1)}, u32[]{:S(2)}) copy-start(f32[128,128]{1,0:T(8,128)S(1)} %get-tuple-element.29.well_weights) | copy-start | bytes 196612
  12.4 27.1 %copy-start.1 = (f32[9,8,32,128]{3,2,1,0:T(8,128)S(1)}, f32[9,8,32,128]{3,2,1,0:T(8,128)}, u32[]{:S(2)}) copy-start(f32[9,8,32,128]{3,2,1,0:T(8,128)} %param.20) | copy-start | bytes 3538948
  28.8 10.7 %all-to-all-start.1 = ((f32[16,24,128]{2,1,0:T(8,128)}), f32[16,24,128]{2,1,0:T(8,128)S(1)}, u32[]{:S(2)}, u32[]{:S(2)}) async-start(f32[16,24,128]{2,1,0:T(8,128)} %bitcast.19), calls=%async_computation.1 | async-start | bytes 393216 | tf_op jit(solution)/shard_map/all_to_all | solution.py:457
  39.5 1.3 %copy-start.5 = (f32[9,8,32,128]{3,2,1,0:T(8,128)S(1)}, f32[9,8,32,128]{3,2,1,0:T(8,128)}, u32[]{:S(2)}) copy-start(f32[9,8,32,128]{3,2,1,0:T(8,128)} %param.21) | copy-start | bytes 3538948
  40.8 0.9 copy-start.10
  41.7 0.9 copy-start.12
  45.9 0.9 copy-start.7
  46.8 0.7 copy-start.24
  47.4 0.7 copy-start.25
  48.1 0.6 copy-start.26
  48.8 0.6 copy-start.27
  49.4 3.3 %copy-start.21 = (f32[8,128]{1,0:T(8,128)}, f32[8,128]{1,0:T(8,128)S(1)}, u32[]{:S(2)}) copy-start(f32[8,128]{1,0:T(8,128)S(1)} %get-tuple-element.28.rates) | copy-start | bytes 12292
  49.4 35.0 %copy-start.20 = (s32[1,1,16]{2,1,0:T(1,128)S(1)}, s32[1,1,16]{2,1,0:T(1,128)}, u32[]{:S(2)}) copy-start(s32[1,1,16]{2,1,0:T(1,128)} %param.27) | copy-start | bytes 196
  49.4 35.0 %collective-permute-start = (f32[3072,128]{1,0:T(8,128)}, f32[3072,128]{1,0:T(8,128)S(1)}, u32[]{:S(2)}, u32[]{:S(2)}) collective-permute-start(f32[3072,128]{1,0:T(8,128)} %get-tuple-element.22.precond), channel_id=1, source_target_pairs={{0,1},{1,0},{2,3},{3,2},{4,5},{5,4},{6,7},{7,6},{8,9},{9,8},{10,11... | collective-permute-start | bytes 4718600 | tf_op jit(solution)/shard_map/ppermute | solution.py:469
  52.6 31.7 %all-to-all-start.2 = ((f32[16,96,128]{2,1,0:T(8,128)}), f32[16,96,128]{2,1,0:T(8,128)S(1)}, u32[]{:S(2)}, u32[]{:S(2)}) async-start(f32[16,96,128]{2,1,0:T(8,128)} %bitcast.44), calls=%async_computation.2 | async-start | bytes 1572864 | tf_op jit(solution)/shard_map/all_to_all | solution.py:474
  61.7 20.4 %collective-permute-start.3 = (f32[384,128]{1,0:T(8,128)}, f32[384,128]{1,0:T(8,128)}, u32[]{:S(2)}, u32[]{:S(2)}) collective-permute-start(f32[384,128]{1,0:T(8,128)} %copy-done.25), channel_id=1, source_target_pairs={{0,16},{16,0},{32,48},{48,32},{64,80},{80,64},{96,112},{112,96},{1... | collective-permute-start | bytes 589832 | tf_op jit(solution)/shard_map/ppermute | solution.py:472
  62.0 20.1 %collective-permute-start.4 = (f32[384,128]{1,0:T(8,128)}, f32[384,128]{1,0:T(8,128)}, u32[]{:S(2)}, u32[]{:S(2)}) collective-permute-start(f32[384,128]{1,0:T(8,128)} %copy-done.24), channel_id=1, source_target_pairs={{16,32},{32,16},{48,64},{64,48},{80,96},{96,80},{112,128},{128,112... | collective-permute-start | bytes 589832 | tf_op jit(solution)/shard_map/ppermute | solution.py:473
  63.3 18.8 %collective-permute-start.1 = (f32[96,128]{1,0:T(8,128)}, f32[96,128]{1,0:T(8,128)}, u32[]{:S(2)}, u32[]{:S(2)}) collective-permute-start(f32[96,128]{1,0:T(8,128)} %copy-done.27), channel_id=1, source_target_pairs={{0,2},{2,0},{4,6},{6,4},{8,10},{10,8},{12,14},{14,12},{1,3},{3,1},... | collective-permute-start | bytes 147464 | tf_op jit(solution)/shard_map/ppermute | solution.py:470
  64.7 17.4 %collective-permute-start.2 = (f32[96,128]{1,0:T(8,128)}, f32[96,128]{1,0:T(8,128)}, u32[]{:S(2)}, u32[]{:S(2)}) collective-permute-start(f32[96,128]{1,0:T(8,128)} %copy-done.26), channel_id=1, source_target_pairs={{2,4},{4,2},{6,8},{8,6},{10,12},{12,10},{3,5},{5,3},{7,9},{9,7},{1... | collective-permute-start | bytes 147464 | tf_op jit(solution)/shard_map/ppermute | solution.py:471
  84.4 1.1 copy-start.6
  85.5 0.8 copy-start.16
  86.3 0.8 copy-start.18
  87.2 0.7 copy-start.22
  87.8 0.7 copy-start.23

commit v2 on v1

--- a/solution.py
+++ b/solution.py
@@ -85,7 +85,7 @@
         x, y = lax.shift_right_logical(cell, 7), cell & 127
         strength = jnp.zeros((8, LANES), F32)
         for p in range(PERFS):
-            strength += jnp.where(sub == perfs[w, p] - first_layer, index[w, p], 0.0)
+            strength += jnp.where(sub == perfs[p, w] - first_layer, index[p, w], 0.0)
         well_weights[pl.ds(w * 8, 8), :] = strength
         picked = jnp.where(lane == y, strength, 0.0)
         for q in range(6):
@@ -206,7 +206,7 @@
         layer_b[pl.ds(plane * XS, XS), :] = precond[pl.ds(plane * PLANE + layer_second, XS), :]
     for u in range(TILES):
         for j in range(SLOTS):
-            row = send_rows[u, j]
+            row = send_rows[j, u]
             outgoing[pl.ds(u * 96 + j * 8, 8), :] = precond[pl.ds(row, 8, stride=PLANE), :]
             outgoing[pl.ds(u * 96 + 64 + j * 4, 4), :] = precond[
                 pl.ds(row + 8 * PLANE, 4, stride=PLANE), :
@@ -228,7 +228,7 @@
     image[...] = jnp.zeros(image.shape, F32)
     for u in range(TILES):
         for j in range(SLOTS):
-            row = recv_rows[u, j]
+            row = recv_rows[j, u]
             slot = u * SLOTS + j
             weight = jnp.where(j < counts[0, u], coef[pl.ds(slot, 1), :], 0.0)
             image[pl.ds(row, 8, stride=PLANE), :] -= weight * arrived[pl.ds(u * 96 + j * 8, 8), :]
@@ -385,7 +385,7 @@
                 pl.BlockSpec(o.shape, lambda i: (0,) * len(o.shape)) for o in outs
             ),
             scratch_shapes=list(scratch),
-            compiler_params=pltpu.CompilerParams(vmem_limit_bytes=28 << 20),
+            compiler_params=pltpu.CompilerParams(vmem_limit_bytes=60 << 20),
             cost_estimate=pl.CostEstimate(flops=flops, bytes_accessed=size, transcendentals=0),
         )(*args)
 
@@ -426,10 +426,10 @@
     )
     ids = jnp.stack([lax.axis_index(a) for a in ALL]).astype(jnp.int32).reshape(1, 3)
     cells = well_cells.reshape(1, WELLS)
-    perfs = well_perfs.reshape(WELLS, PERFS)
-    index = well_index.reshape(WELLS, PERFS)
-    send_rows = fault_send_rows.reshape(TILES, SLOTS)
-    recv_rows = fault_recv_rows.reshape(TILES, SLOTS)
+    perfs = well_perfs.reshape(WELLS, PERFS).T
+    index = well_index.reshape(WELLS, PERFS).T
+    send_rows = fault_send_rows.reshape(TILES, SLOTS).T
+    recv_rows = fault_recv_rows.reshape(TILES, SLOTS).T
     counts = fault_counts.reshape(1, TILES)
     columns = (part(0), part(3), part(6))
     message, base, from_below, from_above, well_weights = call(

time: 116 us -> 106 us (0.914)
  local copies, waits for them, and re-layouts: 21.4 us -> 1.4 us
  blocking collectives: 33.6 us -> 46 us
  Pallas kernels: 14.8 us -> 22.5 us
  waiting for transfers between devices: 24.7 us -> 19.4 us
  starting transfers between devices: 20.1 us -> 15.1 us
    unnamed x58 -> x20, local copies, waits for them, and re-layouts: 19 us -> 1.4 us
    all_to_all x0 -> x1, blocking collectives: none -> 11.4 us  [on_device(): lax.all_to_all(reply.reshape(CHUNKS, MSG, LANES), 'layer', split_axis=0,...]
    pallas_call x5, Pallas kernels: 14.8 us -> 22.5 us  [run(): pl.pallas_call(kernel, name=name, grid=(1,), out_shape=outs, in_specs=spe...]
    all_to_all x1 -> x0, waiting for transfers between devices: 7.07 us -> none  [on_device(): lax.all_to_all(reply.reshape(CHUNKS, MSG, LANES), 'layer', split_axis=0,...]
    all_to_all x1 -> x0, starting transfers between devices: 3.53 us -> none  [on_device(): lax.all_to_all(reply.reshape(CHUNKS, MSG, LANES), 'layer', split_axis=0,...]
    reshape x4 -> x0, local copies, waits for them, and re-layouts: 2.34 us -> none  [the longest x1 0.76 us: on_device(): perfs = well_perfs.reshape(WELLS, PERFS)]
    ppermute x1, waiting for transfers between devices: 15.4 us -> 17.1 us  [on_device(): x_a = lax.ppermute(x_a, 'tx', pairs(n_tx, False))]
  transfers between devices with their start and end apart: 7 -> 6, of which waited for: 3 -> 2; matrix products, arithmetic and copies ran while one was open for 1% -> 0% of each run, Pallas kernels for 0% -> 0%
where the time goes in v2:
time: 106 us
  blocking collectives  46 us (43%)
  Pallas kernels  22.5 us (21%)
  waiting for transfers between devices  19.4 us (18%)
  starting transfers between devices  15.1 us (14%)
  local copies, waits for them, and re-layouts  1.4 us (1%)
    pallas_call x5, Pallas kernels, run(): pl.pallas_call(kernel, name=name, grid=(1,), out_shape=outs, in_specs=spe...  22.5 us
    all_to_all x1, blocking collectives, on_device(): lax.all_to_all(gram, ALL, split_axis=0, concat_axis=0, tiled=True)  19.8 us
    ppermute x1, waiting for transfers between devices, on_device(): x_a = lax.ppermute(x_a, 'tx', pairs(n_tx, False))  17.1 us
    all_to_all x1, blocking collectives, on_device(): lax.all_to_all(message.reshape(CHUNKS, MSG, LANES), 'layer', split_axis=0...  14.9 us
    all_to_all x1, blocking collectives, on_device(): lax.all_to_all(reply.reshape(CHUNKS, MSG, LANES), 'layer', split_axis=0,...  11.4 us
    all_to_all x1, starting transfers between devices, on_device(): lax.all_to_all(outgoing.reshape(TILES, 96, LANES), ('tx', 'ty'), split_ax...  8.63 us
    ppermute x1, starting transfers between devices, on_device(): across = lax.ppermute(precond, 'ty', pairs(n_ty, False))  3.34 us
    all_to_all x1, waiting for transfers between devices, on_device(): lax.all_to_all(outgoing.reshape(TILES, 96, LANES), ('tx', 'ty'), split_ax...  2.31 us
  transfers between devices with their start and end apart: 6, of which 2 were waited for; matrix products, arithmetic and copies ran while one was open for 0% of the time, Pallas kernels for 0%

profile of v2, /device:TPU:1, one launch (start us, length us, event | category | flops | bytes accessed | tf_op | source)
XLA Modules:
  0.0 105.9 jit_solution(12966205386157069043)
XLA Ops:
  0.6 0.6 add_bitcast_fusion.ids
  1.2 3.8 %sweep.1 = (f32[384,128]{1,0:T(8,128)}, f32[1024,128]{1,0:T(8,128)}, f32[256,128]{1,0:T(8,128)}, f32[256,128]{1,0:T(8,128)}, f32[128,128]{1,0:T(8,128)}) custom-call(s32[1,3]{1,0:T(1,128)} %add_bitcast_fusion.ids, s32[1,16]{1,0:T(1,128)} %bitcast.64, s32[8,16]{1,0:T(8,128)} %bitcast.67, f32[8,16]{1,0:T(8,128)} %bitcast.68, f32[3072,128]{1,0:T(8,128)} %bitcast.46, ...), custom_call_target="tpu_custom_call" | custom-call | flops 1000000 | bytes 7078988 | tf_op jit(solution)/shard_map/sweep/pallas_call | solution.py:378
  5.1 14.9 %all_to_all.26 = f32[16,24,128]{2,1,0:T(8,128)} all-to-all(f32[16,24,128]{2,1,0:T(8,128)} %bitcast.58), channel_id=1, replica_groups=mesh['layer'=16,'tx'=8,'ty'=2] {'layer'}, dimensions={0} | all-to-all | bytes 393216 | tf_op jit(solution)/shard_map/all_to_all | solution.py:446
  19.9 2.0 %chain.1 = f32[384,128]{1,0:T(8,128)} custom-call(s32[1,3]{1,0:T(1,128)} %add_bitcast_fusion.ids, s32[1,16]{1,0:T(1,128)} %bitcast.65, f32[384,128]{1,0:T(8,128)} %bitcast.52), custom_call_target="tpu_custom_call" | custom-call | flops 1000000 | bytes 196684 | tf_op jit(solution)/shard_map/chain/pallas_call | solution.py:378
  22.0 11.4 %all_to_all.27 = f32[16,24,128]{2,1,0:T(8,128)} all-to-all(f32[16,24,128]{2,1,0:T(8,128)} %bitcast.53), channel_id=1, replica_groups=mesh['layer'=16,'tx'=8,'ty'=2] {'layer'}, dimensions={0} | all-to-all | bytes 393216 | tf_op jit(solution)/shard_map/all_to_all | solution.py:457
  33.3 5.1 %precond.1 = (f32[3072,128]{1,0:T(8,128)}, f32[96,128]{1,0:T(8,128)}, f32[96,128]{1,0:T(8,128)}, f32[384,128]{1,0:T(8,128)}, f32[384,128]{1,0:T(8,128)}, /*index=5*/f32[1536,128]{1,0:T(8,128)}, f32[8,128]{1,0:T(8,128)}) custom-call(s32[1,3]{1,0:T(1,128)} %add_bitcast_fusion.ids, s32[8,16]{1,0:T(8,128)} %bitcast.69, f32[384,128]{1,0:T(8,128)} %bitcast.55, ...), custom_call_target="tpu_custom_call" | custom-call | flops 1000000 | bytes 7275020 | tf_op jit(solution)/shard_map/precond/pallas_call | solution.py:378
  38.4 0.0 copy-start.7
  38.4 0.0 copy-start.6
  38.4 0.0 copy-start.9
  38.4 0.0 copy-start.8
  38.5 3.3 %collective-permute-start = (f32[3072,128]{1,0:T(8,128)}, f32[3072,128]{1,0:T(8,128)S(1)}, u32[]{:S(2)}, u32[]{:S(2)}) collective-permute-start(f32[3072,128]{1,0:T(8,128)} %get-tuple-element.22.precond), channel_id=1, source_target_pairs={{0,1},{1,0},{2,3},{3,2},{4,5},{5,4},{6,7},{7,6},{8,9},{9,8},{10,11... | collective-permute-start | bytes 4718600 | tf_op jit(solution)/shard_map/ppermute | solution.py:469
  41.8 8.6 %all-to-all-start.2 = ((f32[16,96,128]{2,1,0:T(8,128)}), f32[16,96,128]{2,1,0:T(8,128)S(1)}, u32[]{:S(2)}, u32[]{:S(2)}) async-start(f32[16,96,128]{2,1,0:T(8,128)} %bitcast.51), calls=%async_computation.2 | async-start | bytes 1572864 | tf_op jit(solution)/shard_map/all_to_all | solution.py:474
  50.4 0.0 copy-done.7
  50.4 0.4 collective-permute-start.3
  50.8 0.0 copy-done.6
  50.8 0.7 collective-permute-start.4
  51.5 0.0 copy-done.9
  51.5 1.4 %collective-permute-start.1 = (f32[96,128]{1,0:T(8,128)S(1)}, f32[96,128]{1,0:T(8,128)S(1)}, u32[]{:S(2)}, u32[]{:S(2)}) collective-permute-start(f32[96,128]{1,0:T(8,128)S(1)} %copy-done.9), channel_id=1, source_target_pairs={{0,2},{2,0},{4,6},{6,4},{8,10},{10,8},{12,14},{14,12},{1,3},{3,1},... | collective-permute-start | bytes 147464 | tf_op jit(solution)/shard_map/ppermute | solution.py:470
  53.0 0.0 copy-done.8
  53.0 0.7 collective-permute-start.2
  53.6 17.1 %collective-permute-done.1.x_a = f32[96,128]{1,0:T(8,128)S(1)} collective-permute-done((f32[96,128]{1,0:T(8,128)S(1)}, f32[96,128]{1,0:T(8,128)S(1)}, u32[]{:S(2)}, u32[]{:S(2)}) %collective-permute-start.1) | collective-permute-done | bytes 49184 | tf_op jit(solution)/shard_map/ppermute | solution.py:470
  70.7 0.0 copy-start.4
  70.7 0.0 collective-permute-done.2.x_b
  70.7 0.0 copy-start.5
  70.7 0.0 collective-permute-done.3.layer_a
  70.8 0.0 copy-start.2
  70.8 0.0 collective-permute-done.4.layer_b
  70.8 0.0 copy-start.3
  70.8 2.3 %all-to-all-done.2 = f32[16,96,128]{2,1,0:T(8,128)S(1)} async-done(((f32[16,96,128]{2,1,0:T(8,128)}), f32[16,96,128]{2,1,0:T(8,128)S(1)}, u32[]{:S(2)}, u32[]{:S(2)}) %all-to-all-start.2) | async-done | bytes 786464 | tf_op jit(solution)/shard_map/all_to_all | solution.py:474
  73.1 0.0 copy-start
  73.1 0.0 collective-permute-done.across
  73.1 0.0 copy-start.1
  73.1 0.0 copy-done.4
  73.1 0.0 copy-done.5
  73.1 0.0 copy-done.2
  73.1 0.0 copy-done.3
  73.1 0.9 copy-done
  74.0 0.5 copy-done.1
  74.5 8.5 %image.1 = (f32[3072,128]{1,0:T(8,128)}, f32[256,128]{1,0:T(8,128)}) custom-call(s32[1,3]{1,0:T(1,128)} %add_bitcast_fusion.ids, s32[1,16]{1,0:T(1,128)} %bitcast.66, s32[8,16]{1,0:T(8,128)} %bitcast.70, s32[1,16]{1,0:T(1,128)} %bitcast.71, f32[3072,128]{1,0:T(8,128)} %get-tuple-element.22.precond, f32[3072,128]{1,0:T(8,128)} %copy-done.1, ...), custom_call_target="tpu_custom_call" | custom-call | flops 1000000 | bytes 6525580 | tf_op jit(solution)/shard_map/image/pallas_call | solution.py:378
  83.0 19.8 %all_to_all.28 = f32[256,1,128]{2,1,0:T(1,128)} all-to-all(f32[256,1,128]{2,1,0:T(1,128)} %bitcast.62), channel_id=1, replica_groups=mesh['layer'=16,'tx'=8,'ty'=2] {'layer','tx','ty'}, dimensions={0} | all-to-all | bytes 262144 | tf_op jit(solution)/shard_map/all_to_all | solution.py:488
  102.8 3.1 %factor.1 = (f32[3072,128]{1,0:T(8,128)}, f32[4,4]{1,0:T(4,128)}) custom-call(f32[256,128]{1,0:T(8,128)} %bitcast.56, f32[3072,128]{1,0:T(8,128)} %get-tuple-element.31.refs_1_), custom_call_target="tpu_custom_call" | custom-call | flops 1000000 | bytes 1703936 | tf_op jit(solution)/shard_map/factor/pallas_call | solution.py:378
Async XLA Ops:
  38.4 12.0 %copy-start.7 = (f32[384,128]{1,0:T(8,128)S(1)}, f32[384,128]{1,0:T(8,128)}, u32[]{:S(2)}) copy-start(f32[384,128]{1,0:T(8,128)} %get-tuple-element.25) | copy-start | bytes 589828
  38.4 12.4 %copy-start.6 = (f32[384,128]{1,0:T(8,128)S(1)}, f32[384,128]{1,0:T(8,128)}, u32[]{:S(2)}) copy-start(f32[384,128]{1,0:T(8,128)} %get-tuple-element.26) | copy-start | bytes 589828
  38.4 13.1 %copy-start.9 = (f32[96,128]{1,0:T(8,128)S(1)}, f32[96,128]{1,0:T(8,128)}, u32[]{:S(2)}) copy-start(f32[96,128]{1,0:T(8,128)} %get-tuple-element.23) | copy-start | bytes 147460
  38.4 14.5 %copy-start.8 = (f32[96,128]{1,0:T(8,128)S(1)}, f32[96,128]{1,0:T(8,128)}, u32[]{:S(2)}) copy-start(f32[96,128]{1,0:T(8,128)} %get-tuple-element.24) | copy-start | bytes 147460
  38.5 34.6 %collective-permute-start = (f32[3072,128]{1,0:T(8,128)}, f32[3072,128]{1,0:T(8,128)S(1)}, u32[]{:S(2)}, u32[]{:S(2)}) collective-permute-start(f32[3072,128]{1,0:T(8,128)} %get-tuple-element.22.precond), channel_id=1, source_target_pairs={{0,1},{1,0},{2,3},{3,2},{4,5},{5,4},{6,7},{7,6},{8,9},{9,8},{10,11... | collective-permute-start | bytes 4718600 | tf_op jit(solution)/shard_map/ppermute | solution.py:469
  41.8 31.3 %all-to-all-start.2 = ((f32[16,96,128]{2,1,0:T(8,128)}), f32[16,96,128]{2,1,0:T(8,128)S(1)}, u32[]{:S(2)}, u32[]{:S(2)}) async-start(f32[16,96,128]{2,1,0:T(8,128)} %bitcast.51), calls=%async_computation.2 | async-start | bytes 1572864 | tf_op jit(solution)/shard_map/all_to_all | solution.py:474
  50.4 20.3 %collective-permute-start.3 = (f32[384,128]{1,0:T(8,128)S(1)}, f32[384,128]{1,0:T(8,128)S(1)}, u32[]{:S(2)}, u32[]{:S(2)}) collective-permute-start(f32[384,128]{1,0:T(8,128)S(1)} %copy-done.7), channel_id=1, source_target_pairs={{0,16},{16,0},{32,48},{48,32},{64,80},{80,64},{96,112},{112,96},{1... | collective-permute-start | bytes 589832 | tf_op jit(solution)/shard_map/ppermute | solution.py:472
  50.8 19.9 %collective-permute-start.4 = (f32[384,128]{1,0:T(8,128)S(1)}, f32[384,128]{1,0:T(8,128)S(1)}, u32[]{:S(2)}, u32[]{:S(2)}) collective-permute-start(f32[384,128]{1,0:T(8,128)S(1)} %copy-done.6), channel_id=1, source_target_pairs={{16,32},{32,16},{48,64},{64,48},{80,96},{96,80},{112,128},{128,112... | collective-permute-start | bytes 589832 | tf_op jit(solution)/shard_map/ppermute | solution.py:473
  51.5 19.2 %collective-permute-start.1 = (f32[96,128]{1,0:T(8,128)S(1)}, f32[96,128]{1,0:T(8,128)S(1)}, u32[]{:S(2)}, u32[]{:S(2)}) collective-permute-start(f32[96,128]{1,0:T(8,128)S(1)} %copy-done.9), channel_id=1, source_target_pairs={{0,2},{2,0},{4,6},{6,4},{8,10},{10,8},{12,14},{14,12},{1,3},{3,1},... | collective-permute-start | bytes 147464 | tf_op jit(solution)/shard_map/ppermute | solution.py:470
  53.0 17.8 %collective-permute-start.2 = (f32[96,128]{1,0:T(8,128)S(1)}, f32[96,128]{1,0:T(8,128)S(1)}, u32[]{:S(2)}, u32[]{:S(2)}) collective-permute-start(f32[96,128]{1,0:T(8,128)S(1)} %copy-done.8), channel_id=1, source_target_pairs={{2,4},{4,2},{6,8},{8,6},{10,12},{12,10},{3,5},{5,3},{7,9},{9,7},{1... | collective-permute-start | bytes 147464 | tf_op jit(solution)/shard_map/ppermute | solution.py:471
  70.7 2.4 %copy-start.4 = (f32[96,128]{1,0:T(8,128)}, f32[96,128]{1,0:T(8,128)S(1)}, u32[]{:S(2)}) copy-start(f32[96,128]{1,0:T(8,128)S(1)} %collective-permute-done.1.x_a) | copy-start | bytes 147460
  70.7 2.4 %copy-start.5 = (f32[96,128]{1,0:T(8,128)}, f32[96,128]{1,0:T(8,128)S(1)}, u32[]{:S(2)}) copy-start(f32[96,128]{1,0:T(8,128)S(1)} %collective-permute-done.2.x_b) | copy-start | bytes 147460
  70.8 2.4 %copy-start.2 = (f32[384,128]{1,0:T(8,128)}, f32[384,128]{1,0:T(8,128)S(1)}, u32[]{:S(2)}) copy-start(f32[384,128]{1,0:T(8,128)S(1)} %collective-permute-done.3.layer_a) | copy-start | bytes 589828
  70.8 2.4 %copy-start.3 = (f32[384,128]{1,0:T(8,128)}, f32[384,128]{1,0:T(8,128)S(1)}, u32[]{:S(2)}) copy-start(f32[384,128]{1,0:T(8,128)S(1)} %collective-permute-done.4.layer_b) | copy-start | bytes 589828
  73.1 0.9 copy-start
  73.1 1.4 %copy-start.1 = (f32[3072,128]{1,0:T(8,128)}, f32[3072,128]{1,0:T(8,128)S(1)}, u32[]{:S(2)}) copy-start(f32[3072,128]{1,0:T(8,128)S(1)} %collective-permute-done.across) | copy-start | bytes 4718596

commit v3 on v2

v3 whole, which is shorter than its diff:
```python
import jax
import jax.numpy as jnp
from jax import lax
from jax.experimental import pallas as pl
from jax.experimental.pallas import tpu as pltpu
from jax.sharding import PartitionSpec as P

F32 = jnp.float32
COLS, COMPS, LAYERS, XS, LANES = 4, 3, 8, 32, 128
BLOCKS = XS // 8
PLANE = LAYERS * XS
TILES, SLOTS = 16, 8
CHUNKS = 16
MSG = 24
WELLS, PERFS = 16, 8
ALL = ("layer", "tx", "ty")


def iota(shape, dim):
    return lax.broadcasted_iota(jnp.int32, shape, dim)


def rows_at(plane, layer, block):
    return pl.ds(plane * PLANE + layer * XS + block * 8, 8)


def chunk_rows(row, block):
    return pl.ds(MSG * 8 * (block % 2) + row + block // 2, 8, stride=MSG)


def fetch(copies, sems):
    handles = [
        pltpu.make_async_copy(a, b, sems.at[i]) for i, (a, b) in enumerate(copies)
    ]
    for handle in handles:
        handle.start()
    waited = []

    def ready(count=None):
        count = len(handles) if count is None else count
        while len(waited) < count:
            handles[len(waited)].wait()
            waited.append(None)

    return ready


def halves(pieces):
    return [
        (a.at[:, pl.ds(i * 16, 16)], b.at[:, pl.ds(i * 16, 16)]) for i in range(2) for a, b in pieces
    ]


def sweep_kernel(
    ids, cells_h, perfs_h, index_h, krylov_h, weights_h, pivots_h, lower_h, upper_h, diag_h, inv_h,
    message, base, from_below, from_above, well_weights,
    krylov, weights, pivots, lower, upper, diag, inv, cells, perfs, index, sems,
):
    pieces = [(krylov_h, krylov), (weights_h, weights), (pivots_h, pivots), (lower_h, lower)]
    pieces += [(upper_h, upper)]
    late = [(inv_h.at[pl.ds(0, 24)], inv)]
    late += [(diag_h.at[pl.ds(24 * c, 8)], diag.at[pl.ds(8 * c, 8)]) for c in range(3)]
    late += [(cells_h, cells), (perfs_h, perfs), (index_h, index)]
    ready = fetch(halves(pieces) + late, sems)
    for block in range(BLOCKS):
        half = block // 2 * len(pieces)
        xs = pl.ds(block * 8, 8)
        ready(half + 4)
        levels = [[] for _ in range(COLS)]
        products = []
        for k in range(LAYERS):
            restrict = [weights[c * 8 + k, xs, :] for c in range(COMPS)]
            pivot = pivots[k, xs, :]
            ratio = lower[k, xs, :]
            products.append(ratio if k == 0 else ratio * products[-1])
            for s in range(COLS):
                source = restrict[0] * krylov[s * 24 + k, xs, :]
                source += restrict[1] * krylov[s * 24 + 8 + k, xs, :]
                source += restrict[2] * krylov[s * 24 + 16 + k, xs, :]
                level = pivot * source
                levels[s].append(level if k == 0 else level + ratio * levels[s][-1])
        for s in range(COLS):
            message[chunk_rows(2 * s, block), :] = levels[s][-1]
        message[chunk_rows(16, block), :] = products[-1]
        ready(half + len(pieces))
        down = [None] * COLS
        low = high = None
        for k in reversed(range(LAYERS)):
            at = rows_at(0, k, block)
            ratio = upper[k, xs, :]
            first = k == LAYERS - 1
            low = products[k] if first else products[k] + ratio * low
            high = ratio if first else ratio * high
            from_below[at, :] = low
            from_above[at, :] = high
            for s in range(COLS):
                down[s] = levels[s][k] if first else levels[s][k] + ratio * down[s]
                base[rows_at(s, k, block), :] = down[s]
        for s in range(COLS):
            message[chunk_rows(8 + 2 * s, block), :] = down[s]
        message[chunk_rows(18, block), :] = high
        message[chunk_rows(20, block), :] = low
    ready()

    def near(ref, plane, x):
        return ref.reshape(-1, LANES)[pl.ds(plane * PLANE + x, 8, stride=XS), :]

    sub, lane = iota((8, LANES), 0), iota((8, LANES), 1)
    first_layer = ids[0, 0] * LAYERS
    total = jnp.zeros((8, LANES), F32)
    for w in range(WELLS):
        cell = cells[0, w]
        x, y = lax.shift_right_logical(cell, 7), cell & 127
        strength = jnp.zeros((8, LANES), F32)
        for p in range(PERFS):
            strength += jnp.where(sub == perfs[p, w] - first_layer, index[p, w], 0.0)
        well_weights[pl.ds(w * 8, 8), :] = strength
        picked = jnp.where(lane == y, strength, 0.0)
        column = [near(inv, c, x) for c in range(COMPS)]
        part = column[0] * near(diag, 0, x) + column[1] * near(diag, 1, x)
        part = picked * (1.0 - (part + column[2] * near(diag, 2, x)))
        values = []
        for s in range(COLS):
            value = column[0] * near(krylov, s * 3, x) + column[1] * near(krylov, s * 3 + 1, x)
            value += column[2] * near(krylov, s * 3 + 2, x)
            values.append(picked * value + part * base[pl.ds(s * PLANE + x, 8, stride=XS), :])
        values.append(part * from_below[pl.ds(x, 8, stride=XS), :])
        values.append(part * from_above[pl.ds(x, 8, stride=XS), :])
        for q in range(6):
            total += pltpu.roll(values[q], (q * WELLS + w + LANES - y) & 127, 1)
    row = jnp.sum(total, axis=0, keepdims=True)
    message[pl.ds(22, CHUNKS, stride=MSG), :] = jnp.broadcast_to(row, (CHUNKS, LANES))
    message[pl.ds(23, CHUNKS, stride=MSG), :] = jnp.zeros((CHUNKS, LANES), F32)


def split(matrix):
    high = matrix.astype(jnp.bfloat16)
    return high, (matrix - high.astype(F32)).astype(jnp.bfloat16)


def chain_kernel(ids, cells_h, message, reply, states, cells, sems):
    ready = fetch([(cells_h, cells)], sems)
    sub, lane = iota((8, LANES), 0), iota((8, LANES), 1)

    def spread(rows, first):
        pair = pltpu.roll(rows, (8 - first) % 8, 0) if first else rows
        pair = jnp.where(sub < 2, pair, 0.0)
        pair += pltpu.roll(pair, 2, 0)
        return pair + pltpu.roll(pair, 4, 0)

    tails = [message[pl.ds(l * MSG + 16, 8), :] for l in range(CHUNKS)]
    state = jnp.zeros((8, LANES), F32)
    entering = []
    for l in range(CHUNKS):
        entering.append(state)
        reply[pl.ds(l * MSG, 8), :] = state
        states[pl.ds(l * 8, 8), pl.ds(0, LANES)] = state
        if l < CHUNKS - 1:
            state = message[pl.ds(l * MSG, 8), :] + spread(tails[l], 0) * state
    state = jnp.zeros((8, LANES), F32)
    for l in reversed(range(CHUNKS)):
        reply[pl.ds(l * MSG + 8, 8), :] = state
        states[pl.ds(l * 8, 8), pl.ds(LANES, LANES)] = state
        if l > 0:
            state = (
                message[pl.ds(l * MSG + 8, 8), :]
                + spread(tails[l], 4) * entering[l]
                + spread(tails[l], 2) * state
            )
    ready()
    me = ids[0, 0]
    wide = (2 * LANES, 2 * LANES)
    col = iota((1, 2 * LANES), 1)
    owner = jnp.zeros((1, 2 * LANES), jnp.int32)
    for w in range(WELLS):
        owner = jnp.where((col & 15) == w, cells[0, w], owner)
    line, column = iota(wide, 0), iota(wide, 1)
    place = (lax.shift_right_logical(column, 7) * 16 + me) * LANES + (line & 127)
    group = lax.shift_right_logical(column & 127, 4) - 4
    chosen = jnp.where(
        (jnp.broadcast_to(owner, wide) == place) & (group == lax.shift_right_logical(line, 7)),
        1.0,
        0.0,
    )
    chosen = chosen.astype(jnp.bfloat16)
    found = sum(jnp.dot(p, chosen, preferred_element_type=F32) for p in split(states[...]))
    odd = (sub & 1) == 1
    total = jnp.zeros((8, LANES), F32)
    fixed = jnp.zeros((1, LANES), F32)
    for l in range(CHUNKS):
        row = tails[l][6:7, :]
        fixed += row
        here = found[l * 8 : l * 8 + 8, :]
        total += row * jnp.where(odd, here[:, LANES:], here[:, :LANES])
    rates = pltpu.roll(total, 64, 1) + pltpu.roll(total, 48, 1)
    fixed = jnp.broadcast_to(jnp.where(me == 0, fixed, 0.0), (8, LANES))
    for s in range(COLS):
        mine = fixed if s == 0 else pltpu.roll(fixed, LANES - 16 * s, 1)
        rates += jnp.where(sub == 2 * s, mine, 0.0)
    rates = jnp.where(lane < WELLS, rates, 0.0)
    for l in range(CHUNKS):
        reply[pl.ds(l * MSG + 16, 8), :] = rates


def ahead_kernel(
    krylov_h, diag_h, inv_h, base, from_below, from_above,
    fixed, by_below, by_above, krylov, diag, inv, sems,
):
    pieces = [(krylov_h, krylov), (inv_h, inv)]
    pieces += [(diag_h.at[pl.ds(24 * c, 8)], diag.at[pl.ds(8 * c, 8)]) for c in range(3)]
    ready = fetch(halves(pieces), sems)
    for block in range(BLOCKS):
        ready((block // 2 + 1) * len(pieces))
        xs = pl.ds(block * 8, 8)
        for k in range(LAYERS):
            at = rows_at(0, k, block)
            column = [diag[c * 8 + k, xs, :] for c in range(COMPS)]
            inverse = [inv[e * 8 + k, xs, :] for e in range(9)]
            low, high = from_below[at, :], from_above[at, :]
            share = []
            for c in range(COMPS):
                row = inverse[3 * c : 3 * c + 3]
                value = row[0] * column[0] + row[1] * column[1] + row[2] * column[2]
                share.append(1.0 - value if c == 0 else -value)
                by_below[rows_at(c, k, block), :] = share[c] * low
                by_above[rows_at(c, k, block), :] = share[c] * high
            for s in range(COLS):
                value = [krylov[(s * 3 + c) * 8 + k, xs, :] for c in range(COMPS)]
                pressure = base[rows_at(s, k, block), :]
                for c in range(COMPS):
                    row = inverse[3 * c : 3 * c + 3]
                    fixed[rows_at(s * 3 + c, k, block), :] = (
                        row[0] * value[0] + row[1] * value[1] + row[2] * value[2]
                    ) + share[c] * pressure


def precond_kernel(
    ids, send_rows_h, reply, fixed, by_below, by_above,
    precond, precond_h, x_a_h, x_b_h, layer_a_h, layer_b_h, outgoing_h, rates,
    x_a, x_b, outgoing, send_rows, sems,
):
    listed = fetch([(send_rows_h, send_rows)], sems.at[pl.ds(6, 1)])
    for block in range(BLOCKS):
        below = [reply[chunk_rows(2 * s, block), :] for s in range(COLS)]
        above = [reply[chunk_rows(8 + 2 * s, block), :] for s in range(COLS)]
        for k in range(LAYERS):
            for c in range(COMPS):
                at = rows_at(c, k, block)
                low, high = by_below[at, :], by_above[at, :]
                for s in range(COLS):
                    at = rows_at(s * 3 + c, k, block)
                    precond[at, :] = fixed[at, :] + low * below[s] + high * above[s]
    layer_even = (ids[0, 0] & 1) == 0
    x_even = (ids[0, 1] & 1) == 0
    layer_first = pl.multiple_of(jnp.where(layer_even, (LAYERS - 1) * XS, 0), XS)
    layer_second = pl.multiple_of(jnp.where(layer_even, 0, (LAYERS - 1) * XS), XS)
    planes = precond.reshape(12, PLANE, LANES)
    ready = fetch(
        [
            (precond, precond_h),
            (planes.at[:, pl.ds(layer_first, XS)], layer_a_h),
            (planes.at[:, pl.ds(layer_second, XS)], layer_b_h),
        ],
        sems,
    )
    x_a[...] = precond[pl.ds(jnp.where(x_even, XS - 1, 0), 96, stride=XS), :]
    x_b[...] = precond[pl.ds(jnp.where(x_even, 0, XS - 1), 96, stride=XS), :]
    listed()
    for u in range(TILES):
        for j in range(SLOTS):
            row = send_rows[j, u]
            outgoing[pl.ds(u * 96 + j, 8, stride=8), :] = precond[pl.ds(row, 8, stride=PLANE), :]
            outgoing[pl.ds(u * 96 + 64 + j, 4, stride=8), :] = precond[
                pl.ds(row + 8 * PLANE, 4, stride=PLANE), :
            ]
    sent = fetch(
        [(outgoing, outgoing_h), (x_a, x_a_h), (x_b, x_b_h)], sems.at[pl.ds(3, 3)]
    )
    total = reply[pl.ds(16, 8), :]
    for j in range(1, CHUNKS):
        total += reply[pl.ds(j * MSG + 16, 8), :]
    rates[...] = total
    ready()
    sent()


def stencil_kernel(
    ids, cells_h, recv_rows_h, counts_h, precond, across_h, layer_a_h, layer_b_h, diag_h, faces_h,
    rates, well_weights, image, edges, targets,
    across, layer_a, layer_b, diag, faces, cells, recv_rows, counts, sems,
):
    ready = fetch(
        [
            (cells_h, cells), (recv_rows_h, recv_rows), (counts_h, counts), (across_h, across),
            (layer_a_h, layer_a), (layer_b_h, layer_b), (diag_h, diag), (faces_h, faces),
        ],
        sems,
    )
    sub, lane = iota((8, LANES), 0), iota((8, LANES), 1)
    layer_even = (ids[0, 0] & 1) == 0
    y_first = ids[0, 2] == 0
    row_x = iota((XS, LANES), 0)
    lane_y = iota((XS, LANES), 1)
    ready()

    def column(k, _):
        def at(plane, layer=None):
            layer = k if layer is None else layer
            return pl.ds(pl.multiple_of(plane * PLANE + layer * XS, XS), XS)

        blocks = [diag[at(e), :] for e in range(9)]
        face = [faces[at(f), :] for f in range(6)]
        for s in range(COLS):
            value = [precond[at(s * 3 + c), :] for c in range(COMPS)]
            for c in range(COMPS):
                plane = s * 3 + c
                here = value[c]
                out = blocks[3 * c] * value[0]
                out += blocks[3 * c + 1] * value[1]
                out += blocks[3 * c + 2] * value[2]
                edge = pl.ds(plane * XS, XS)
                inner = precond[at(plane, jnp.maximum(k - 1, 0)), :]
                outer = jnp.where(layer_even, layer_b[edge, :], layer_a[edge, :])
                out -= face[0] * jnp.where(k == 0, outer, inner)
                inner = precond[at(plane, jnp.minimum(k + 1, LAYERS - 1)), :]
                outer = jnp.where(layer_even, layer_a[edge, :], layer_b[edge, :])
                out -= face[1] * jnp.where(k == LAYERS - 1, outer, inner)
                out -= face[2] * jnp.where(row_x == 0, 0.0, pltpu.roll(here, 1, 0))
                out -= face[3] * jnp.where(row_x == XS - 1, 0.0, pltpu.roll(here, XS - 1, 0))
                other = across[at(plane), :]
                edge_low = jnp.where(y_first, 0.0, other)
                edge_high = jnp.where(y_first, other, 0.0)
                out -= face[4] * pltpu.roll(jnp.where(lane_y == LANES - 1, edge_low, here), 1, 1)
                out -= face[5] * pltpu.roll(jnp.where(lane_y == 0, edge_high, here), LANES - 1, 1)
                image[at(plane), :] = out
        return _

    lax.fori_loop(0, LAYERS, column, 0)
    slot = iota((1, LANES), 1)
    target = jnp.full((1, LANES), -1, jnp.int32)
    for u in range(TILES):
        for j in range(SLOTS):
            row = jnp.where(j < counts[0, u], recv_rows[j, u], -1)
            target = jnp.where(slot == u * SLOTS + j, row, target)
    targets[...] = jnp.where(iota((PLANE, LANES), 0) == target, 1.0, 0.0)
    edges[pl.ds(0, 8), :] = faces[pl.ds(2 * PLANE, 8, stride=XS), :]
    edges[pl.ds(8, 8), :] = faces[pl.ds(3 * PLANE + XS - 1, 8, stride=XS), :]
    rate = rates[...]
    rate = (rate + pltpu.roll(rate, 7, 0)) * (1.0 / PERFS)
    for w in range(WELLS):
        cell = cells[0, w]
        x, y = lax.shift_right_logical(cell, 7), cell & 127
        strength = well_weights[pl.ds(w * 8, 8), :]
        placed = pltpu.roll(jnp.where(lane == w, rate, 0.0), (y + LANES - w) & 127, 1)
        for s in range(COLS):
            image[pl.ds(s * 3 * PLANE + x, 8, stride=XS), :] += strength * placed[2 * s : 2 * s + 1, :]


def finish_kernel(ids, _, x_a, x_b, arrived, coef_h, edges, targets, image, gram, coef, sems):
    ready = fetch([(coef_h, coef)], sems)
    x_even = (ids[0, 1] & 1) == 0
    for plane in range(12):
        side = pl.ds(plane * LAYERS, LAYERS)
        first, second = x_a[side, :], x_b[side, :]
        at = pl.ds(plane * PLANE, 8, stride=XS)
        image[at, :] -= edges[pl.ds(0, 8), :] * jnp.where(x_even, second, first)
        at = pl.ds(plane * PLANE + XS - 1, 8, stride=XS)
        image[at, :] -= edges[pl.ds(8, 8), :] * jnp.where(x_even, first, second)
    ready()
    chosen = targets[...].astype(jnp.bfloat16)
    chosen = jnp.concatenate([chosen, chosen], axis=1)
    weight = coef[...]
    for pair in range(6):
        parts = []
        for plane in (2 * pair, 2 * pair + 1):
            came = arrived[:, pl.ds(plane * 8, 8), :].reshape(TILES * SLOTS, LANES)
            parts.append(jnp.concatenate(split(came * weight), axis=0))
        added = jnp.dot(
            chosen, jnp.concatenate(parts, axis=1), preferred_element_type=F32
        )
        for i in range(2):
            at = pl.ds((2 * pair + i) * PLANE, PLANE)
            image[at, :] -= added[:, i * LANES : (i + 1) * LANES]

    def add(i, totals):
        at = pl.multiple_of(i * 8, 8)
        totals = list(totals)
        images = []
        for plane in range(12):
            value = image[pl.ds(plane * PLANE + at, 8), :]
            images.append(value)
        n = 0
        for s in range(COLS):
            for t in range(s + 1):
                value = images[s * 3] * images[t * 3]
                value += images[s * 3 + 1] * images[t * 3 + 1]
                value += images[s * 3 + 2] * images[t * 3 + 2]
                totals[n] += value
                n += 1
        return tuple(totals)

    sums = lax.fori_loop(
        0, PLANE // 8, add, tuple(jnp.zeros((8, LANES), F32) for _ in range(10)), unroll=4
    )
    packed = jnp.zeros((1, LANES), F32)
    lanes = iota((1, LANES), 1)
    for n in range(10):
        value = jnp.sum(jnp.sum(sums[n], axis=0, keepdims=True), axis=1, keepdims=True)
        packed = jnp.where(lanes == n, value, packed)
    gram[...] = jnp.broadcast_to(packed, gram.shape)


def factor_kernel(scale, gathered, image, q_h, factor_h, q, factor, sems):
    total = jnp.sum(gathered[...].reshape(-1, 8, LANES), axis=0)
    total = jnp.sum(total, axis=0, keepdims=True) * scale
    lanes = iota((1, LANES), 1)
    entry, n = {}, 0
    for s in range(COLS):
        for t in range(s + 1):
            entry[s, t] = jnp.sum(jnp.where(lanes == n, total, 0.0), axis=1, keepdims=True)
            n += 1
    lower = {}
    for t in range(COLS):
        value = entry[t, t]
        for i in range(t):
            value -= lower[t, i] * lower[t, i]
        lower[t, t] = jnp.sqrt(value)
        for s in range(t + 1, COLS):
            value = entry[s, t]
            for i in range(t):
                value -= lower[s, i] * lower[t, i]
            lower[s, t] = value / lower[t, t]
    line, col = iota((COLS, COLS), 0), iota((COLS, COLS), 1)
    result = jnp.zeros((COLS, COLS), F32)
    for (s, t), value in lower.items():
        result = jnp.where((line == t) & (col == s), value, result)
    factor[...] = result
    sent = [fetch([(factor, factor_h)], sems)]
    wide = {key: jnp.broadcast_to(value, (8, LANES)) for key, value in lower.items()}
    inverse = {t: 1.0 / wide[t, t] for t in range(COLS)}

    for half in range(4):

        def step(i, _, half=half):
            at = pl.multiple_of(half * 64 + i * 8, 8)
            done = []
            for s in range(COLS):
                for_s = []
                for c in range(COMPS):
                    value = image[pl.ds((s * 3 + c) * PLANE + at, 8), :]
                    for t in range(s):
                        value -= wide[s, t] * done[t][c]
                    value *= inverse[s]
                    q[s * 3 + c, pl.ds(at, 8), :] = value
                    for_s.append(value)
                done.append(for_s)
            return _

        lax.fori_loop(0, 8, step, 0, unroll=4)
        rows = pl.ds(half * 64, 64)
        sent.append(
            fetch([(q.at[:, rows], q_h.at[:, rows])], sems.at[pl.ds(1 + half, 1)])
        )
    for wait in sent:
        wait()


LIMIT = 24 << 20
SPACES = {"smem": pltpu.SMEM, "vmem": pltpu.VMEM, "hbm": pltpu.HBM}


def call(kernel, name, ins, outs, scratch=(), sems=1, flops=1_000_000, alias=None):
    args = [
        a if where == "smem" else pltpu.with_memory_space_constraint(a, SPACES[where])
        for a, where in ins
    ]
    size = sum(a.size * 4 for a in args)
    return pl.pallas_call(
        kernel,
        name=name,
        out_shape=tuple(SPACES[where](dims, F32) for dims, where in outs),
        in_specs=[pl.BlockSpec(memory_space=SPACES[where]) for _, where in ins],
        out_specs=tuple(pl.BlockSpec(memory_space=SPACES[where]) for _, where in outs),
        scratch_shapes=[pltpu.VMEM(d, F32) if isinstance(d, tuple) else d for d in scratch]
        + ([pltpu.SemaphoreType.DMA((sems,))] if sems else []),
        input_output_aliases=alias or {},
        compiler_params=pltpu.CompilerParams(vmem_limit_bytes=LIMIT),
        cost_estimate=pl.CostEstimate(flops=flops, bytes_accessed=size, transcendentals=0),
    )(*args)


def pairs(size, odd):
    found = []
    for i in range(1 if odd else 0, size - 1, 2):
        found += [(i, i + 1), (i + 1, i)]
    return found


def on_device(
    krylov_block,
    weights,
    pivots,
    lower_ratio,
    upper_ratio,
    block_diag,
    block_inv,
    face_coef,
    fault_send_rows,
    fault_recv_rows,
    fault_counts,
    fault_coef,
    well_cells,
    well_perfs,
    well_index,
):
    n_layer, n_tx, n_ty = (lax.axis_size(a) for a in ALL)

    def rows(array):
        return array.reshape(-1, LANES)

    def planes(array):
        return (array.reshape(-1, XS, LANES), "hbm")

    ids = jnp.stack([lax.axis_index(a) for a in ALL]).astype(jnp.int32).reshape(1, 3)
    ids = (ids, "smem")
    cells = (well_cells.reshape(1, WELLS), "hbm")
    perfs = (well_perfs.reshape(WELLS, PERFS).T, "hbm")
    index = (well_index.reshape(WELLS, PERFS).T, "hbm")
    send_rows = (fault_send_rows.reshape(TILES, SLOTS).T, "hbm")
    recv_rows = (fault_recv_rows.reshape(TILES, SLOTS).T, "hbm")
    counts = (fault_counts.reshape(1, TILES), "hbm")
    krylov, diag, inv = planes(krylov_block), planes(block_diag), planes(block_inv)
    fields = [planes(a) for a in (weights, pivots, lower_ratio, upper_ratio)]

    def line(count):
        return (count, LANES)

    message, base, from_below, from_above, well_weights = call(
        sweep_kernel,
        "sweep",
        [ids, cells, perfs, index, krylov, *fields, diag, inv],
        [
            (line(CHUNKS * MSG), "vmem"),
            (line(COLS * PLANE), "vmem"),
            (line(PLANE), "vmem"),
            (line(PLANE), "vmem"),
            (line(WELLS * 8), "vmem"),
        ],
        scratch=[(96, XS, LANES), (24, XS, LANES)]
        + [(8, XS, LANES)] * 3
        + [(24, XS, LANES)] * 2
        + [pltpu.SMEM((1, WELLS), jnp.int32), pltpu.SMEM((PERFS, WELLS), jnp.int32)]
        + [pltpu.SMEM((PERFS, WELLS), F32)],
        sems=17,
    )
    fixed, by_below, by_above = call(
        ahead_kernel,
        "ahead",
        [krylov, diag, inv, (base, "vmem"), (from_below, "vmem"), (from_above, "vmem")],
        [(line(12 * PLANE), "vmem"), (line(3 * PLANE), "vmem"), (line(3 * PLANE), "vmem")],
        scratch=[(96, XS, LANES), (24, XS, LANES), (72, XS, LANES)],
        sems=10,
    )
    message = lax.all_to_all(
        message.reshape(CHUNKS, MSG, LANES), "layer", split_axis=0, concat_axis=0, tiled=True
    )
    (reply,) = call(
        chain_kernel,
        "chain",
        [ids, cells, (rows(message), "vmem")],
        [(line(CHUNKS * MSG), "vmem")],
        scratch=[(LANES, 2 * LANES), pltpu.SMEM((1, WELLS), jnp.int32)],
        sems=1,
    )
    reply = lax.all_to_all(
        reply.reshape(CHUNKS, MSG, LANES), "layer", split_axis=0, concat_axis=0, tiled=True
    )
    precond, precond_out, x_a, x_b, layer_a, layer_b, outgoing, rates = call(
        precond_kernel,
        "precond",
        [
            ids, send_rows, (rows(reply), "vmem"), (fixed, "vmem"), (by_below, "vmem"),
            (by_above, "vmem"),
        ],
        [
            (line(12 * PLANE), "vmem"),
            (line(12 * PLANE), "hbm"),
            (line(96), "hbm"),
            (line(96), "hbm"),
            ((12, XS, LANES), "hbm"),
            ((12, XS, LANES), "hbm"),
            (line(TILES * 96), "hbm"),
            (line(8), "vmem"),
        ],
        scratch=[line(96), line(96), line(TILES * 96), pltpu.SMEM((SLOTS, TILES), jnp.int32)],
        sems=7,
    )
    across = lax.ppermute(precond_out, "ty", pairs(n_ty, False))
    x_a = lax.ppermute(x_a, "tx", pairs(n_tx, False))
    x_b = lax.ppermute(x_b, "tx", pairs(n_tx, True))
    layer_a = lax.ppermute(layer_a, "layer", pairs(n_layer, False))
    layer_b = lax.ppermute(layer_b, "layer", pairs(n_layer, True))
    arrived = lax.all_to_all(
        outgoing.reshape(TILES, 96, LANES), ("tx", "ty"), split_axis=0, concat_axis=0, tiled=True
    )
    devices = n_layer * n_tx * n_ty
    partial, edges, targets = call(
        stencil_kernel,
        "stencil",
        [
            ids, cells, recv_rows, counts, (precond, "vmem"), (across, "hbm"), (rows(layer_a), "hbm"),
            (rows(layer_b), "hbm"), (rows(block_diag), "hbm"), (rows(face_coef), "hbm"),
            (rates, "vmem"), (well_weights, "vmem"),
        ],
        [(line(12 * PLANE), "vmem"), (line(16), "vmem"), (line(PLANE), "vmem")],
        scratch=[line(12 * PLANE), line(12 * XS), line(12 * XS), line(9 * PLANE), line(6 * PLANE)]
        + [pltpu.SMEM((1, WELLS), jnp.int32), pltpu.SMEM((SLOTS, TILES), jnp.int32)]
        + [pltpu.SMEM((1, TILES), jnp.int32)],
        sems=8,
    )
    image, gram = call(
        finish_kernel,
        "finish",
        [
            ids, (partial, "vmem"), (x_a, "vmem"), (x_b, "vmem"), (arrived, "vmem"),
            (rows(fault_coef), "hbm"), (edges, "vmem"), (targets, "vmem"),
        ],
        [(line(12 * PLANE), "vmem"), (line(devices), "vmem")],
        scratch=[line(TILES * SLOTS)],
        alias={1: 0},
    )
    gathered = lax.all_to_all(gram, ALL, split_axis=0, concat_axis=0, tiled=True)
    entries = float(12 * PLANE * LANES // COLS * devices)

    def factor(*refs):
        factor_kernel(1.0 / entries, *refs)

    q, r_factor = call(
        factor,
        "factor",
        [(gathered, "vmem"), (image, "vmem")],
        [((12, PLANE, LANES), "hbm"), ((COLS, COLS), "hbm")],
        scratch=[(12, PLANE, LANES), (COLS, COLS)],
        sems=5,
    )
    return (q.reshape(krylov_block.shape), r_factor)


def solution(mesh):
    placed = (
        P(None, None, "layer", "tx", "ty"),
        P(None, "layer", "tx", "ty"),
        P("layer", "tx", "ty"),
        P("layer", "tx", "ty"),
        P("layer", "tx", "ty"),
        P(None, "layer", "tx", "ty"),
        P(None, "layer", "tx", "ty"),
        P(None, "layer", "tx", "ty"),
        P("layer", "tx", "ty", None, None),
        P("layer", "tx", "ty", None, None),
        P("layer", "tx", "ty", None),
        P("layer", "tx", "ty", None, None, None),
        P("tx", "ty", None),
        P("tx", "ty", None, None),
        P("tx", "ty", None, None),
    )
    return jax.shard_map(
        on_device,
        mesh=mesh,
        in_specs=placed,
        out_specs=(P(None, None, "layer", "tx", "ty"), P()),
        check_vma=False,
    )
```

time: 106 us -> 94.2 us (0.89)
  blocking collectives: 46 us -> 33.3 us
  starting transfers between devices: 15.1 us -> 18.7 us
  waiting for transfers between devices: 19.4 us -> 16.4 us
  local copies, waits for them, and re-layouts: 1.4 us -> 3.87 us
  Pallas kernels: 22.5 us -> 20.6 us
    ppermute x1, waiting for transfers between devices: 17.1 us -> 5.68 us  [on_device(): x_a = lax.ppermute(x_a, 'tx', pairs(n_tx, False))]
    all_to_all x1 -> x0, blocking collectives: 11.4 us -> none  [on_device(): lax.all_to_all(reply.reshape(CHUNKS, MSG, LANES), 'layer', split_axis=0,...]
    all_to_all x0 -> x1, waiting for transfers between devices: none -> 4.98 us  [on_device(): lax.all_to_all(reply.reshape(CHUNKS, MSG, LANES), 'layer', split_axis=0,...]
    all_to_all x0 -> x1, starting transfers between devices: none -> 3.53 us  [on_device(): lax.all_to_all(reply.reshape(CHUNKS, MSG, LANES), 'layer', split_axis=0,...]
    ppermute x1, waiting for transfers between devices: 0.01 us -> 3.36 us  [on_device(): layer_a = lax.ppermute(layer_a, 'layer', pairs(n_layer, False))]
    unnamed x20 -> x18, local copies, waits for them, and re-layouts: 1.4 us -> 3.87 us
    pallas_call x5 -> x7, Pallas kernels: 22.5 us -> 20.6 us  [call(): pl.pallas_call(kernel, name=name, out_shape=tuple((SPACES[where](dims, F3...]
  transfers between devices with their start and end apart: 6 -> 7, of which waited for: 2 -> 4; matrix products, arithmetic and copies ran while one was open for 0% -> 0% of each run, Pallas kernels for 0% -> 8%
where the time goes in v3:
time: 94.2 us; the launch traced here: 93.7 us
  blocking collectives  33.3 us (35%)
  Pallas kernels  20.6 us (22%)
  starting transfers between devices  18.7 us (20%)
  waiting for transfers between devices  16.4 us (17%)
  local copies, waits for them, and re-layouts  3.87 us (4%)
    pallas_call x7, Pallas kernels, call(): pl.pallas_call(kernel, name=name, out_shape=tuple((SPACES[where](dims, F3...  20.6 us
    all_to_all x1, blocking collectives, on_device(): lax.all_to_all(gram, ALL, split_axis=0, concat_axis=0, tiled=True)  18.8 us
    all_to_all x1, blocking collectives, on_device(): lax.all_to_all(message.reshape(CHUNKS, MSG, LANES), 'layer', split_axis=0...  14.6 us
    all_to_all x1, starting transfers between devices, on_device(): lax.all_to_all(outgoing.reshape(TILES, 96, LANES), ('tx', 'ty'), split_ax...  8.63 us
    ppermute x1, waiting for transfers between devices, on_device(): x_a = lax.ppermute(x_a, 'tx', pairs(n_tx, False))  5.68 us
    all_to_all x1, waiting for transfers between devices, on_device(): lax.all_to_all(reply.reshape(CHUNKS, MSG, LANES), 'layer', split_axis=0,...  4.98 us
    unnamed x18, local copies, waits for them, and re-layouts  3.87 us
    all_to_all x1, starting transfers between devices, on_device(): lax.all_to_all(reply.reshape(CHUNKS, MSG, LANES), 'layer', split_axis=0,...  3.53 us
  transfers between devices with their start and end apart: 7, of which 4 were waited for; matrix products, arithmetic and copies ran while one was open for 0% of the time, Pallas kernels for 8%

profile of v3, /device:TPU:1, one launch (start us, length us, event | category | flops | bytes accessed | tf_op | source)
XLA Modules:
  0.0 93.7 jit_solution(7208141508857210114)
XLA Ops:
  0.6 0.1 add_bitcast_fusion.ids
  0.7 4.2 %sweep.1 = (f32[384,128]{1,0:T(8,128)S(1)}, f32[1024,128]{1,0:T(8,128)S(1)}, f32[256,128]{1,0:T(8,128)S(1)}, f32[256,128]{1,0:T(8,128)S(1)}, f32[128,128]{1,0:T(8,128)S(1)}) custom-call(s32[1,3]{1,0:T(1,128)S(1)} %add_bitcast_fusion.ids, s32[1,16]{1,0:T(1,128)} %bitcast.56, s32[8,16]{1,0:T(8,128)} %bitcast.61, f32[8,16]{1,0:T(8,128)} %bitcast.62, ...), custom_call_target="tpu_custom_call" | custom-call | flops 1000000 | bytes 4719692 | tf_op jit(solution)/shard_map/sweep/pallas_call | solution.py:478
  4.9 14.6 %all_to_all.26 = f32[16,24,128]{2,1,0:T(8,128)S(1)} all-to-all(f32[16,24,128]{2,1,0:T(8,128)S(1)} %bitcast.41), channel_id=1, replica_groups=mesh['layer'=16,'tx'=8,'ty'=2] {'layer'}, dimensions={0} | all-to-all | bytes 393216 | tf_op jit(solution)/shard_map/all_to_all | solution.py:564
  19.5 2.2 %chain.1 = f32[384,128]{1,0:T(8,128)} custom-call(s32[1,3]{1,0:T(1,128)S(1)} %add_bitcast_fusion.ids, s32[1,16]{1,0:T(1,128)} %bitcast.57, f32[384,128]{1,0:T(8,128)S(1)} %bitcast.39), custom_call_target="tpu_custom_call" | custom-call | flops 1000000 | bytes 196684 | tf_op jit(solution)/shard_map/chain/pallas_call | solution.py:478
  21.7 3.5 %all-to-all-start.1 = ((f32[16,24,128]{2,1,0:T(8,128)}), f32[16,24,128]{2,1,0:T(8,128)S(1)}, u32[]{:S(2)}, u32[]{:S(2)}) async-start(f32[16,24,128]{2,1,0:T(8,128)} %bitcast.20), calls=%async_computation.1 | async-start | bytes 393216 | tf_op jit(solution)/shard_map/all_to_all | solution.py:575
  25.3 2.2 %ahead.1 = (f32[3072,128]{1,0:T(8,128)S(1)}, f32[768,128]{1,0:T(8,128)S(1)}, f32[768,128]{1,0:T(8,128)S(1)}) custom-call(f32[96,32,128]{2,1,0:T(8,128)} %bitcast.47, f32[72,32,128]{2,1,0:T(8,128)} %bitcast.44, f32[72,32,128]{2,1,0:T(8,128)} %bitcast.49, f32[1024,128]{1,0:T(8,128)S(1)} %get-tuple-element.26.base, ...), custom_call_target="tpu_custom_call" | custom-call | flops 1000000 | bytes 4718592 | tf_op jit(solution)/shard_map/ahead/pallas_call | solution.py:478
  27.5 5.0 %all-to-all-done.1 = f32[16,24,128]{2,1,0:T(8,128)S(1)} async-done(((f32[16,24,128]{2,1,0:T(8,128)}), f32[16,24,128]{2,1,0:T(8,128)S(1)}, u32[]{:S(2)}, u32[]{:S(2)}) %all-to-all-start.1) | async-done | bytes 196640 | tf_op jit(solution)/shard_map/all_to_all | solution.py:575
  32.4 3.0 %precond.1 = (f32[3072,128]{1,0:T(8,128)S(1)}, f32[3072,128]{1,0:T(8,128)}, f32[96,128]{1,0:T(8,128)}, f32[96,128]{1,0:T(8,128)}, f32[12,32,128]{2,1,0:T(8,128)}...) custom-call(s32[1,3]{1,0:T(1,128)S(1)} %add_bitcast_fusion.ids, s32[8,16]{1,0:T(8,128)} %bitcast.59, ...), custom_call_target="tpu_custom_call" | custom-call | flops 1000000 | bytes 2556428 | tf_op jit(solution)/shard_map/precond/pallas_call | solution.py:478
  35.5 0.0 copy-start
  35.5 1.2 %copy-done = f32[3072,128]{1,0:T(8,128)} copy-done((f32[3072,128]{1,0:T(8,128)}, f32[3072,128]{1,0:T(8,128)S(1)}, u32[]{:S(2)}) %copy-start) | copy-done | bytes 1572888
  36.6 0.0 copy-start.6
  36.6 0.0 copy-start.5
  36.6 0.0 copy-start.8
  36.6 0.0 copy-start.7
  36.6 3.3 %collective-permute-start = (f32[3072,128]{1,0:T(8,128)}, f32[3072,128]{1,0:T(8,128)S(1)}, u32[]{:S(2)}, u32[]{:S(2)}) collective-permute-start(f32[3072,128]{1,0:T(8,128)} %get-tuple-element.33), channel_id=1, source_target_pairs={{0,1},{1,0},{2,3},{3,2},{4,5},{5,4},{6,7},{7,6},{8,9},{9,8},{10,11... | collective-permute-start | bytes 4718600 | tf_op jit(solution)/shard_map/ppermute | solution.py:598
  40.0 8.6 %all-to-all-start.2 = ((f32[16,96,128]{2,1,0:T(8,128)}), f32[16,96,128]{2,1,0:T(8,128)S(1)}, u32[]{:S(2)}, u32[]{:S(2)}) async-start(f32[16,96,128]{2,1,0:T(8,128)} %bitcast.51), calls=%async_computation.2 | async-start | bytes 1572864 | tf_op jit(solution)/shard_map/all_to_all | solution.py:603
  48.6 0.0 copy-done.6
  48.6 0.4 collective-permute-start.1
  49.0 0.0 copy-done.5
  49.0 0.7 collective-permute-start.2
  49.7 0.0 copy-done.8
  49.7 1.4 %collective-permute-start.3 = (f32[96,128]{1,0:T(8,128)S(1)}, f32[96,128]{1,0:T(8,128)S(1)}, u32[]{:S(2)}, u32[]{:S(2)}) collective-permute-start(f32[96,128]{1,0:T(8,128)S(1)} %copy-done.8), channel_id=1, source_target_pairs={{0,2},{2,0},{4,6},{6,4},{8,10},{10,8},{12,14},{14,12},{1,3},{3,1},... | collective-permute-start | bytes 147464 | tf_op jit(solution)/shard_map/ppermute | solution.py:599
  51.2 0.0 copy-done.7
  51.2 0.7 collective-permute-start.4
  51.8 3.4 %collective-permute-done.1 = f32[12,32,128]{2,1,0:T(8,128)S(1)} collective-permute-done((f32[12,32,128]{2,1,0:T(8,128)S(1)}, f32[12,32,128]{2,1,0:T(8,128)S(1)}, u32[]{:S(2)}, u32[]{:S(2)}) %collective-permute-start.1) | collective-permute-done | bytes 196640 | tf_op jit(solution)/shard_map/ppermute | solution.py:601
  55.2 0.0 copy-start.3
  55.2 0.0 collective-permute-done.2
  55.2 0.0 copy-start.4
  55.2 0.0 collective-permute-done.across_h
  55.2 0.0 copy-start.2
  55.2 1.2 %copy-done.2 = f32[3072,128]{1,0:T(8,128)} copy-done((f32[3072,128]{1,0:T(8,128)}, f32[3072,128]{1,0:T(8,128)S(1)}, u32[]{:S(2)}) %copy-start.2) | copy-done | bytes 1572888
  56.4 0.0 copy-done.3
  56.4 0.1 copy-done.4
  56.5 0.0 copy-start.1
  56.5 1.4 %copy-done.1 = f32[3072,128]{1,0:T(8,128)S(1)} copy-done((f32[3072,128]{1,0:T(8,128)S(1)}, f32[3072,128]{1,0:T(8,128)}, u32[]{:S(2)}) %copy-start.1) | copy-done | bytes 1572888
  57.9 5.3 %stencil.1 = (f32[3072,128]{1,0:T(8,128)S(1)}, f32[16,128]{1,0:T(8,128)S(1)}, f32[256,128]{1,0:T(8,128)S(1)}) custom-call(s32[1,3]{1,0:T(1,128)S(1)} %add_bitcast_fusion.ids, s32[1,16]{1,0:T(1,128)} %bitcast.58, s32[8,16]{1,0:T(8,128)} %bitcast.60, s32[1,16]{1,0:T(1,128)} %bitcast.63, f32[3072,128]{1,0:T(8,128)S(1)} %copy-done.1, f32[3072,128]{1,0:T(8,128)} %copy-done.2, ...), custom_call_target="tpu_custom_call" | custom-call | flops 1000000 | bytes 5575308 | tf_op jit(solution)/shard_map/stencil/pallas_call | solution.py:478
  63.2 5.7 %collective-permute-done.3.x_a = f32[96,128]{1,0:T(8,128)S(1)} collective-permute-done((f32[96,128]{1,0:T(8,128)S(1)}, f32[96,128]{1,0:T(8,128)S(1)}, u32[]{:S(2)}, u32[]{:S(2)}) %collective-permute-start.3) | collective-permute-done | bytes 49184 | tf_op jit(solution)/shard_map/ppermute | solution.py:599
  68.9 0.0 collective-permute-done.4.x_b
  68.9 2.4 %all-to-all-done.2.arrived = f32[16,96,128]{2,1,0:T(8,128)S(1)} async-done(((f32[16,96,128]{2,1,0:T(8,128)}), f32[16,96,128]{2,1,0:T(8,128)S(1)}, u32[]{:S(2)}, u32[]{:S(2)}) %all-to-all-start.2) | async-done | bytes 786464 | tf_op jit(solution)/shard_map/all_to_all | solution.py:603
  71.3 2.2 %finish.1 = (f32[3072,128]{1,0:T(8,128)S(1)}, f32[256,128]{1,0:T(8,128)S(1)}) custom-call(s32[1,3]{1,0:T(1,128)S(1)} %add_bitcast_fusion.ids, f32[3072,128]{1,0:T(8,128)S(1)} %get-tuple-element.38._, f32[96,128]{1,0:T(8,128)S(1)} %collective-permute-done.3.x_a, f32[96,128]{1,0:T(8,128)S(1)} %collective-permute-done.4.x_b, ...), custom_call_target="tpu_custom_call", output_to_operand_aliasing={{0}: (1, {})} | custom-call | flops 1000000 | bytes 2662412 | tf_op jit(solution)/shard_map/finish/pallas_call | solution.py:478
  73.5 18.8 %all_to_all.27 = f32[256,1,128]{2,1,0:T(1,128)S(1)} all-to-all(f32[256,1,128]{2,1,0:T(1,128)S(1)} %bitcast.42), channel_id=1, replica_groups=mesh['layer'=16,'tx'=8,'ty'=2] {'layer','tx','ty'}, dimensions={0} | all-to-all | bytes 262144 | tf_op jit(solution)/shard_map/all_to_all | solution.py:632
  92.2 1.4 %factor.1 = (f32[12,256,128]{2,1,0:T(8,128)}, f32[4,4]{1,0:T(4,128)}) custom-call(f32[256,128]{1,0:T(8,128)S(1)} %bitcast.40, f32[3072,128]{1,0:T(8,128)S(1)} %get-tuple-element.45.refs_1_), custom_call_target="tpu_custom_call" | custom-call | flops 1000000 | bytes 1703936 | tf_op jit(solution)/shard_map/factor/pallas_call | solution.py:478
Async XLA Ops:
  21.7 10.7 %all-to-all-start.1 = ((f32[16,24,128]{2,1,0:T(8,128)}), f32[16,24,128]{2,1,0:T(8,128)S(1)}, u32[]{:S(2)}, u32[]{:S(2)}) async-start(f32[16,24,128]{2,1,0:T(8,128)} %bitcast.20), calls=%async_computation.1 | async-start | bytes 393216 | tf_op jit(solution)/shard_map/all_to_all | solution.py:575
  35.5 1.2 %copy-start = (f32[3072,128]{1,0:T(8,128)}, f32[3072,128]{1,0:T(8,128)S(1)}, u32[]{:S(2)}) copy-start(f32[3072,128]{1,0:T(8,128)S(1)} %get-tuple-element.32.precond) | copy-start | bytes 4718596
  36.6 12.0 %copy-start.6 = (f32[12,32,128]{2,1,0:T(8,128)S(1)}, f32[12,32,128]{2,1,0:T(8,128)}, u32[]{:S(2)}) copy-start(f32[12,32,128]{2,1,0:T(8,128)} %get-tuple-element.34) | copy-start | bytes 589828
  36.6 12.4 %copy-start.5 = (f32[12,32,128]{2,1,0:T(8,128)S(1)}, f32[12,32,128]{2,1,0:T(8,128)}, u32[]{:S(2)}) copy-start(f32[12,32,128]{2,1,0:T(8,128)} %get-tuple-element.35) | copy-start | bytes 589828
  36.6 13.1 %copy-start.8 = (f32[96,128]{1,0:T(8,128)S(1)}, f32[96,128]{1,0:T(8,128)}, u32[]{:S(2)}) copy-start(f32[96,128]{1,0:T(8,128)} %get-tuple-element.39) | copy-start | bytes 147460
  36.6 14.5 %copy-start.7 = (f32[96,128]{1,0:T(8,128)S(1)}, f32[96,128]{1,0:T(8,128)}, u32[]{:S(2)}) copy-start(f32[96,128]{1,0:T(8,128)} %get-tuple-element.40) | copy-start | bytes 147460
  36.6 18.5 %collective-permute-start = (f32[3072,128]{1,0:T(8,128)}, f32[3072,128]{1,0:T(8,128)S(1)}, u32[]{:S(2)}, u32[]{:S(2)}) collective-permute-start(f32[3072,128]{1,0:T(8,128)} %get-tuple-element.33), channel_id=1, source_target_pairs={{0,1},{1,0},{2,3},{3,2},{4,5},{5,4},{6,7},{7,6},{8,9},{9,8},{10,11... | collective-permute-start | bytes 4718600 | tf_op jit(solution)/shard_map/ppermute | solution.py:598
  40.0 31.3 %all-to-all-start.2 = ((f32[16,96,128]{2,1,0:T(8,128)}), f32[16,96,128]{2,1,0:T(8,128)S(1)}, u32[]{:S(2)}, u32[]{:S(2)}) async-start(f32[16,96,128]{2,1,0:T(8,128)} %bitcast.51), calls=%async_computation.2 | async-start | bytes 1572864 | tf_op jit(solution)/shard_map/all_to_all | solution.py:603
  48.6 6.6 %collective-permute-start.1 = (f32[12,32,128]{2,1,0:T(8,128)S(1)}, f32[12,32,128]{2,1,0:T(8,128)S(1)}, u32[]{:S(2)}, u32[]{:S(2)}) collective-permute-start(f32[12,32,128]{2,1,0:T(8,128)S(1)} %copy-done.6), channel_id=1, source_target_pairs={{0,16},{16,0},{32,48},{48,32},{64,80},{80,64},{96,112},{112,96},{1... | collective-permute-start | bytes 589832 | tf_op jit(solution)/shard_map/ppermute | solution.py:601
  49.0 6.2 %collective-permute-start.2 = (f32[12,32,128]{2,1,0:T(8,128)S(1)}, f32[12,32,128]{2,1,0:T(8,128)S(1)}, u32[]{:S(2)}, u32[]{:S(2)}) collective-permute-start(f32[12,32,128]{2,1,0:T(8,128)S(1)} %copy-done.5), channel_id=1, source_target_pairs={{16,32},{32,16},{48,64},{64,48},{80,96},{96,80},{112,128},{128,112... | collective-permute-start | bytes 589832 | tf_op jit(solution)/shard_map/ppermute | solution.py:602
  49.7 19.2 %collective-permute-start.3 = (f32[96,128]{1,0:T(8,128)S(1)}, f32[96,128]{1,0:T(8,128)S(1)}, u32[]{:S(2)}, u32[]{:S(2)}) collective-permute-start(f32[96,128]{1,0:T(8,128)S(1)} %copy-done.8), channel_id=1, source_target_pairs={{0,2},{2,0},{4,6},{6,4},{8,10},{10,8},{12,14},{14,12},{1,3},{3,1},... | collective-permute-start | bytes 147464 | tf_op jit(solution)/shard_map/ppermute | solution.py:599
  51.2 17.8 %collective-permute-start.4 = (f32[96,128]{1,0:T(8,128)S(1)}, f32[96,128]{1,0:T(8,128)S(1)}, u32[]{:S(2)}, u32[]{:S(2)}) collective-permute-start(f32[96,128]{1,0:T(8,128)S(1)} %copy-done.7), channel_id=1, source_target_pairs={{2,4},{4,2},{6,8},{8,6},{10,12},{12,10},{3,5},{5,3},{7,9},{9,7},{1... | collective-permute-start | bytes 147464 | tf_op jit(solution)/shard_map/ppermute | solution.py:600
  55.2 1.2 %copy-start.3 = (f32[12,32,128]{2,1,0:T(8,128)}, f32[12,32,128]{2,1,0:T(8,128)S(1)}, u32[]{:S(2)}) copy-start(f32[12,32,128]{2,1,0:T(8,128)S(1)} %collective-permute-done.1) | copy-start | bytes 589828
  55.2 1.3 %copy-start.4 = (f32[12,32,128]{2,1,0:T(8,128)}, f32[12,32,128]{2,1,0:T(8,128)S(1)}, u32[]{:S(2)}) copy-start(f32[12,32,128]{2,1,0:T(8,128)S(1)} %collective-permute-done.2) | copy-start | bytes 589828
  55.2 1.2 %copy-start.2 = (f32[3072,128]{1,0:T(8,128)}, f32[3072,128]{1,0:T(8,128)S(1)}, u32[]{:S(2)}) copy-start(f32[3072,128]{1,0:T(8,128)S(1)} %collective-permute-done.across_h) | copy-start | bytes 4718596
  56.5 1.4 %copy-start.1 = (f32[3072,128]{1,0:T(8,128)S(1)}, f32[3072,128]{1,0:T(8,128)}, u32[]{:S(2)}) copy-start(f32[3072,128]{1,0:T(8,128)} %copy-done) | copy-start | bytes 4718596

commit v4 on v3

--- a/solution.py
+++ b/solution.py
@@ -53,14 +53,13 @@
 
 def sweep_kernel(
     ids, cells_h, perfs_h, index_h, krylov_h, weights_h, pivots_h, lower_h, upper_h, diag_h, inv_h,
-    message, base, from_below, from_above, well_weights,
-    krylov, weights, pivots, lower, upper, diag, inv, cells, perfs, index, sems,
+    message, base, from_below, from_above, strengths, owners,
+    drawn, krylov, weights, pivots, lower, upper, diag, inv, cells, perfs, index, sems,
 ):
     pieces = [(krylov_h, krylov), (weights_h, weights), (pivots_h, pivots), (lower_h, lower)]
-    pieces += [(upper_h, upper)]
-    late = [(inv_h.at[pl.ds(0, 24)], inv)]
-    late += [(diag_h.at[pl.ds(24 * c, 8)], diag.at[pl.ds(8 * c, 8)]) for c in range(3)]
-    late += [(cells_h, cells), (perfs_h, perfs), (index_h, index)]
+    pieces += [(upper_h, upper), (inv_h.at[pl.ds(0, 24)], inv)]
+    pieces += [(diag_h.at[pl.ds(24 * c, 8)], diag.at[pl.ds(8 * c, 8)]) for c in range(3)]
+    late = [(cells_h, cells), (perfs_h, perfs), (index_h, index)]
     ready = fetch(halves(pieces) + late, sems)
     for block in range(BLOCKS):
         half = block // 2 * len(pieces)
@@ -93,43 +92,52 @@
             high = ratio if first else ratio * high
             from_below[at, :] = low
             from_above[at, :] = high
+            inverse = [inv[c * 8 + k, xs, :] for c in range(COMPS)]
+            share = 1.0 - (
+                inverse[0] * diag[k, xs, :]
+                + inverse[1] * diag[8 + k, xs, :]
+                + inverse[2] * diag[16 + k, xs, :]
+            )
+            drawn[rows_at(4, k, block), :] = share * low
+            drawn[rows_at(5, k, block), :] = share * high
             for s in range(COLS):
                 down[s] = levels[s][k] if first else levels[s][k] + ratio * down[s]
                 base[rows_at(s, k, block), :] = down[s]
+                value = inverse[0] * krylov[s * 24 + k, xs, :]
+                value += inverse[1] * krylov[s * 24 + 8 + k, xs, :]
+                value += inverse[2] * krylov[s * 24 + 16 + k, xs, :]
+                drawn[rows_at(s, k, block), :] = value + share * down[s]
         for s in range(COLS):
             message[chunk_rows(8 + 2 * s, block), :] = down[s]
         message[chunk_rows(18, block), :] = high
         message[chunk_rows(20, block), :] = low
     ready()
-
-    def near(ref, plane, x):
-        return ref.reshape(-1, LANES)[pl.ds(plane * PLANE + x, 8, stride=XS), :]
-
     sub, lane = iota((8, LANES), 0), iota((8, LANES), 1)
-    first_layer = ids[0, 0] * LAYERS
-    total = jnp.zeros((8, LANES), F32)
+    layer = perfs[...] - ids[0, 0] * LAYERS
+    strength = jnp.zeros((8, LANES), F32)
+    for k in range(LAYERS):
+        here = jnp.sum(jnp.where(layer == k, index[...], 0.0), axis=0, keepdims=True)
+        here = jnp.concatenate([here, jnp.zeros((1, LANES - WELLS), F32)], axis=1)
+        strength = jnp.where(sub == k, here, strength)
+    strengths[...] = strength
+    totals = [jnp.zeros((8, LANES), F32) for _ in range(6)]
+    owner = jnp.zeros((8, LANES), jnp.int32)
     for w in range(WELLS):
         cell = cells[0, w]
         x, y = lax.shift_right_logical(cell, 7), cell & 127
-        strength = jnp.zeros((8, LANES), F32)
-        for p in range(PERFS):
-            strength += jnp.where(sub == perfs[p, w] - first_layer, index[p, w], 0.0)
-        well_weights[pl.ds(w * 8, 8), :] = strength
-        picked = jnp.where(lane == y, strength, 0.0)
-        column = [near(inv, c, x) for c in range(COMPS)]
-        part = column[0] * near(diag, 0, x) + column[1] * near(diag, 1, x)
-        part = picked * (1.0 - (part + column[2] * near(diag, 2, x)))
-        values = []
-        for s in range(COLS):
-            value = column[0] * near(krylov, s * 3, x) + column[1] * near(krylov, s * 3 + 1, x)
-            value += column[2] * near(krylov, s * 3 + 2, x)
-            values.append(picked * value + part * base[pl.ds(s * PLANE + x, 8, stride=XS), :])
-        values.append(part * from_below[pl.ds(x, 8, stride=XS), :])
-        values.append(part * from_above[pl.ds(x, 8, stride=XS), :])
+        owner = jnp.where((lane & 15) == w, cell, owner)
+        picked = pltpu.roll(jnp.where(lane == w, strength, 0.0), (y + LANES - w) & 127, 1)
+        back = (w + LANES - y) & 127
         for q in range(6):
-            total += pltpu.roll(values[q], (q * WELLS + w + LANES - y) & 127, 1)
-    row = jnp.sum(total, axis=0, keepdims=True)
-    message[pl.ds(22, CHUNKS, stride=MSG), :] = jnp.broadcast_to(row, (CHUNKS, LANES))
+            value = drawn[pl.ds(q * PLANE + x, 8, stride=XS), :] * picked
+            totals[q] += pltpu.roll(value, back, 1)
+    owners[...] = owner - ids[0, 0] * LANES
+    total = totals[0]
+    for q in range(1, 6):
+        total += pltpu.roll(totals[q], q * WELLS, 1)
+    row = jnp.broadcast_to(jnp.sum(total, axis=0, keepdims=True), (CHUNKS, LANES))
+    kept = (iota((CHUNKS, LANES), 0) == 0) | (iota((CHUNKS, LANES), 1) >= COLS * WELLS)
+    message[pl.ds(22, CHUNKS, stride=MSG), :] = jnp.where(kept, row, 0.0)
     message[pl.ds(23, CHUNKS, stride=MSG), :] = jnp.zeros((CHUNKS, LANES), F32)
 
 
@@ -138,8 +146,7 @@
     return high, (matrix - high.astype(F32)).astype(jnp.bfloat16)
 
 
-def chain_kernel(ids, cells_h, message, reply, states, cells, sems):
-    ready = fetch([(cells_h, cells)], sems)
+def chain_kernel(owners, message, reply, states):
     sub, lane = iota((8, LANES), 0), iota((8, LANES), 1)
 
     def spread(rows, first):
@@ -167,15 +174,11 @@
                 + spread(tails[l], 4) * entering[l]
                 + spread(tails[l], 2) * state
             )
-    ready()
-    me = ids[0, 0]
     wide = (2 * LANES, 2 * LANES)
-    col = iota((1, 2 * LANES), 1)
-    owner = jnp.zeros((1, 2 * LANES), jnp.int32)
-    for w in range(WELLS):
-        owner = jnp.where((col & 15) == w, cells[0, w], owner)
+    owner = owners[0:1, :]
+    owner = jnp.concatenate([owner, owner], axis=1)
     line, column = iota(wide, 0), iota(wide, 1)
-    place = (lax.shift_right_logical(column, 7) * 16 + me) * LANES + (line & 127)
+    place = lax.shift_right_logical(column, 7) * (16 * LANES) + (line & 127)
     group = lax.shift_right_logical(column & 127, 4) - 4
     chosen = jnp.where(
         (jnp.broadcast_to(owner, wide) == place) & (group == lax.shift_right_logical(line, 7)),
@@ -193,7 +196,7 @@
         here = found[l * 8 : l * 8 + 8, :]
         total += row * jnp.where(odd, here[:, LANES:], here[:, :LANES])
     rates = pltpu.roll(total, 64, 1) + pltpu.roll(total, 48, 1)
-    fixed = jnp.broadcast_to(jnp.where(me == 0, fixed, 0.0), (8, LANES))
+    fixed = jnp.broadcast_to(fixed, (8, LANES))
     for s in range(COLS):
         mine = fixed if s == 0 else pltpu.roll(fixed, LANES - 16 * s, 1)
         rates += jnp.where(sub == 2 * s, mine, 0.0)
@@ -203,12 +206,13 @@
 
 
 def ahead_kernel(
-    krylov_h, diag_h, inv_h, base, from_below, from_above,
-    fixed, by_below, by_above, krylov, diag, inv, sems,
+    krylov_h, diag_h, inv_h, send_rows_h, base, from_below, from_above,
+    fixed_h, by_below_h, by_above_h, fixed_rows, by_below_rows, by_above_rows, columns,
+    fixed, by_below, by_above, krylov, diag, inv, send_rows, sems,
 ):
     pieces = [(krylov_h, krylov), (inv_h, inv)]
     pieces += [(diag_h.at[pl.ds(24 * c, 8)], diag.at[pl.ds(8 * c, 8)]) for c in range(3)]
-    ready = fetch(halves(pieces), sems)
+    ready = fetch(halves(pieces) + [(send_rows_h, send_rows)], sems)
     for block in range(BLOCKS):
         ready((block // 2 + 1) * len(pieces))
         xs = pl.ds(block * 8, 8)
@@ -232,73 +236,136 @@
                     fixed[rows_at(s * 3 + c, k, block), :] = (
                         row[0] * value[0] + row[1] * value[1] + row[2] * value[2]
                     ) + share[c] * pressure
+    ready()
+    sent = fetch(
+        [(fixed, fixed_h), (by_below, by_below_h), (by_above, by_above_h)], sems.at[pl.ds(11, 3)]
+    )
+    col = iota((8, LANES), 1) & 31
+    sub = iota((8, LANES), 0)
+    for u in range(TILES):
+        wanted = jnp.zeros((8, LANES), jnp.int32)
+        for j in range(SLOTS):
+            row = send_rows[j, u]
+            wanted = jnp.where(sub == j, row & 31, wanted)
+            fixed_rows[pl.ds(u * 96 + j, 8, stride=8), :] = fixed[pl.ds(row, 8, stride=PLANE), :]
+            fixed_rows[pl.ds(u * 96 + 64 + j, 4, stride=8), :] = fixed[
+                pl.ds(row + 8 * PLANE, 4, stride=PLANE), :
+            ]
+            at = pl.ds(u * 24 + j, 3, stride=8)
+            by_below_rows[at, :] = by_below[pl.ds(row, 3, stride=PLANE), :]
+            by_above_rows[at, :] = by_above[pl.ds(row, 3, stride=PLANE), :]
+        columns[pl.ds(u * 8, 8), :] = jnp.where(col == wanted, 1.0, 0.0)
+    sent()
+
+
+def outgoing_kernel(reply, fixed_rows, by_below_rows, by_above_rows, columns, outgoing_h, outgoing, sems):
+    planes = []
+    for q in range(2 * COLS):
+        planes.append(
+            jnp.concatenate([reply[chunk_rows(2 * q, block), :] for block in range(BLOCKS)], axis=0)
+        )
+    states = jnp.concatenate(planes, axis=1)
+    high = states.astype(jnp.bfloat16)
+    rest = states - high.astype(F32)
+    middle = rest.astype(jnp.bfloat16)
+    low = (rest - middle.astype(F32)).astype(jnp.bfloat16)
+    chosen = columns[:, 0:96].astype(jnp.bfloat16)
+    stacked = jnp.concatenate([high, middle, low], axis=0)
+    found = jnp.dot(chosen, stacked, preferred_element_type=F32)
+    sent = []
+    for u in range(TILES):
+        here = found[u * 8 : u * 8 + 8, :]
+        for c in range(COMPS):
+            at = pl.ds(u * 24 + c * 8, 8)
+            below, above = by_below_rows[at, :], by_above_rows[at, :]
+            for s in range(COLS):
+                at = pl.ds(u * 96 + (s * 3 + c) * 8, 8)
+                outgoing[at, :] = (
+                    fixed_rows[at, :]
+                    + below * here[:, s * LANES : (s + 1) * LANES]
+                    + above * here[:, (COLS + s) * LANES : (COLS + s + 1) * LANES]
+                )
+        if u % 8 == 7:
+            at = pl.ds((u - 7) * 96, 8 * 96)
+            copy = (outgoing.at[at], outgoing_h.at[at])
+            sent.append(fetch([copy], sems.at[pl.ds(u // 8, 1)]))
+    for wait in sent:
+        wait()
 
 
 def precond_kernel(
-    ids, send_rows_h, reply, fixed, by_below, by_above,
-    precond, precond_h, x_a_h, x_b_h, layer_a_h, layer_b_h, outgoing_h, rates,
-    x_a, x_b, outgoing, send_rows, sems,
+    ids, reply, fixed_h, by_below_h, by_above_h,
+    precond_h, x_a_h, x_b_h, layer_a_h, layer_b_h, across_h, rates,
+    precond, x_a, x_b, across, fixed, by_below, by_above, sems,
 ):
-    listed = fetch([(send_rows_h, send_rows)], sems.at[pl.ds(6, 1)])
-    for block in range(BLOCKS):
-        below = [reply[chunk_rows(2 * s, block), :] for s in range(COLS)]
-        above = [reply[chunk_rows(8 + 2 * s, block), :] for s in range(COLS)]
-        for k in range(LAYERS):
-            for c in range(COMPS):
-                at = rows_at(c, k, block)
-                low, high = by_below[at, :], by_above[at, :]
-                for s in range(COLS):
+    ready = fetch(
+        [(by_below_h, by_below), (by_above_h, by_above)]
+        + [
+            (fixed_h.at[pl.ds(s * 3 * PLANE, 3 * PLANE)], fixed.at[pl.ds(s * 3 * PLANE, 3 * PLANE)])
+            for s in range(COLS)
+        ],
+        sems,
+    )
+    total = reply[pl.ds(16, 8), :]
+    for j in range(1, CHUNKS):
+        total += reply[pl.ds(j * MSG + 16, 8), :]
+    rates[...] = total
+    for s in range(COLS):
+        ready(3 + s)
+        for block in range(BLOCKS):
+            below = reply[chunk_rows(2 * s, block), :]
+            above = reply[chunk_rows(8 + 2 * s, block), :]
+            for k in range(LAYERS):
+                for c in range(COMPS):
+                    at = rows_at(c, k, block)
+                    low, high = by_below[at, :], by_above[at, :]
                     at = rows_at(s * 3 + c, k, block)
-                    precond[at, :] = fixed[at, :] + low * below[s] + high * above[s]
+                    precond[at, :] = fixed[at, :] + low * below + high * above
     layer_even = (ids[0, 0] & 1) == 0
     x_even = (ids[0, 1] & 1) == 0
     layer_first = pl.multiple_of(jnp.where(layer_even, (LAYERS - 1) * XS, 0), XS)
     layer_second = pl.multiple_of(jnp.where(layer_even, 0, (LAYERS - 1) * XS), XS)
     planes = precond.reshape(12, PLANE, LANES)
-    ready = fetch(
-        [
-            (precond, precond_h),
+    x_a[...] = precond[pl.ds(jnp.where(x_even, XS - 1, 0), 96, stride=XS), :]
+    x_b[...] = precond[pl.ds(jnp.where(x_even, 0, XS - 1), 96, stride=XS), :]
+    lane = iota((XS, LANES), 1)
+    side = jnp.where(ids[0, 2] == 0, LANES - 1, 0)
+    edge = jnp.zeros((XS, LANES), F32)
+    for plane in range(96):
+        value = pltpu.roll(precond[pl.ds(plane * XS, XS), :], (plane + LANES - side) & 127, 1)
+        edge = jnp.where(lane == plane, value, edge)
+    across[...] = edge
+    sent = fetch(
+        [
+            (across, across_h),
+            (x_a, x_a_h),
+            (x_b, x_b_h),
             (planes.at[:, pl.ds(layer_first, XS)], layer_a_h),
             (planes.at[:, pl.ds(layer_second, XS)], layer_b_h),
-        ],
-        sems,
-    )
-    x_a[...] = precond[pl.ds(jnp.where(x_even, XS - 1, 0), 96, stride=XS), :]
-    x_b[...] = precond[pl.ds(jnp.where(x_even, 0, XS - 1), 96, stride=XS), :]
-    listed()
-    for u in range(TILES):
-        for j in range(SLOTS):
-            row = send_rows[j, u]
-            outgoing[pl.ds(u * 96 + j, 8, stride=8), :] = precond[pl.ds(row, 8, stride=PLANE), :]
-            outgoing[pl.ds(u * 96 + 64 + j, 4, stride=8), :] = precond[
-                pl.ds(row + 8 * PLANE, 4, stride=PLANE), :
-            ]
-    sent = fetch(
-        [(outgoing, outgoing_h), (x_a, x_a_h), (x_b, x_b_h)], sems.at[pl.ds(3, 3)]
-    )
-    total = reply[pl.ds(16, 8), :]
-    for j in range(1, CHUNKS):
-        total += reply[pl.ds(j * MSG + 16, 8), :]
-    rates[...] = total
-    ready()
+            (precond, precond_h),
+        ],
+        sems.at[pl.ds(6, 6)],
+    )
     sent()
 
 
 def stencil_kernel(
-    ids, cells_h, recv_rows_h, counts_h, precond, across_h, layer_a_h, layer_b_h, diag_h, faces_h,
-    rates, well_weights, image, edges, targets,
-    across, layer_a, layer_b, diag, faces, cells, recv_rows, counts, sems,
+    ids, cells_h, recv_rows_h, counts_h, precond_h, across_h, layer_a_h, layer_b_h, diag_h, faces_h,
+    coef_h, rates, strengths, image, edges, targets, coef,
+    precond, across, layer_a, layer_b, diag, faces, cells, recv_rows, counts, sems,
 ):
     ready = fetch(
         [
-            (cells_h, cells), (recv_rows_h, recv_rows), (counts_h, counts), (across_h, across),
+            (cells_h, cells), (recv_rows_h, recv_rows), (counts_h, counts), (precond_h, precond), (across_h, across),
             (layer_a_h, layer_a), (layer_b_h, layer_b), (diag_h, diag), (faces_h, faces),
+            (coef_h, coef),
         ],
         sems,
     )
     sub, lane = iota((8, LANES), 0), iota((8, LANES), 1)
     layer_even = (ids[0, 0] & 1) == 0
     y_first = ids[0, 2] == 0
+    side = jnp.where(y_first, LANES - 1, 0)
     row_x = iota((XS, LANES), 0)
     lane_y = iota((XS, LANES), 1)
     ready()
@@ -327,11 +394,13 @@
                 out -= face[1] * jnp.where(k == LAYERS - 1, outer, inner)
                 out -= face[2] * jnp.where(row_x == 0, 0.0, pltpu.roll(here, 1, 0))
                 out -= face[3] * jnp.where(row_x == XS - 1, 0.0, pltpu.roll(here, XS - 1, 0))
-                other = across[at(plane), :]
+                other = pltpu.roll(across[...], (side + LANES - plane * LAYERS - k) & 127, 1)
                 edge_low = jnp.where(y_first, 0.0, other)
                 edge_high = jnp.where(y_first, other, 0.0)
-                out -= face[4] * pltpu.roll(jnp.where(lane_y == LANES - 1, edge_low, here), 1, 1)
-                out -= face[5] * pltpu.roll(jnp.where(lane_y == 0, edge_high, here), LANES - 1, 1)
+                out -= face[4] * jnp.where(lane_y == 0, edge_low, pltpu.roll(here, 1, 1))
+                out -= face[5] * jnp.where(
+                    lane_y == LANES - 1, edge_high, pltpu.roll(here, LANES - 1, 1)
+                )
                 image[at(plane), :] = out
         return _
 
@@ -350,14 +419,13 @@
     for w in range(WELLS):
         cell = cells[0, w]
         x, y = lax.shift_right_logical(cell, 7), cell & 127
-        strength = well_weights[pl.ds(w * 8, 8), :]
+        strength = jnp.broadcast_to(strengths[:, w : w + 1], (8, LANES))
         placed = pltpu.roll(jnp.where(lane == w, rate, 0.0), (y + LANES - w) & 127, 1)
         for s in range(COLS):
             image[pl.ds(s * 3 * PLANE + x, 8, stride=XS), :] += strength * placed[2 * s : 2 * s + 1, :]
 
 
-def finish_kernel(ids, _, x_a, x_b, arrived, coef_h, edges, targets, image, gram, coef, sems):
-    ready = fetch([(coef_h, coef)], sems)
+def finish_kernel(ids, _, x_a, x_b, arrived, coef, edges, targets, image, gram):
     x_even = (ids[0, 1] & 1) == 0
     for plane in range(12):
         side = pl.ds(plane * LAYERS, LAYERS)
@@ -366,7 +434,6 @@
         image[at, :] -= edges[pl.ds(0, 8), :] * jnp.where(x_even, second, first)
         at = pl.ds(plane * PLANE + XS - 1, 8, stride=XS)
         image[at, :] -= edges[pl.ds(8, 8), :] * jnp.where(x_even, first, second)
-    ready()
     chosen = targets[...].astype(jnp.bfloat16)
     chosen = jnp.concatenate([chosen, chosen], axis=1)
     weight = coef[...]
@@ -478,9 +545,9 @@
     return pl.pallas_call(
         kernel,
         name=name,
-        out_shape=tuple(SPACES[where](dims, F32) for dims, where in outs),
+        out_shape=tuple(SPACES[o[1]](o[0], o[2] if len(o) > 2 else F32) for o in outs),
         in_specs=[pl.BlockSpec(memory_space=SPACES[where]) for _, where in ins],
-        out_specs=tuple(pl.BlockSpec(memory_space=SPACES[where]) for _, where in outs),
+        out_specs=tuple(pl.BlockSpec(memory_space=SPACES[o[1]]) for o in outs),
         scratch_shapes=[pltpu.VMEM(d, F32) if isinstance(d, tuple) else d for d in scratch]
         + ([pltpu.SemaphoreType.DMA((sems,))] if sems else []),
         input_output_aliases=alias or {},
@@ -535,7 +602,7 @@
     def line(count):
         return (count, LANES)
 
-    message, base, from_below, from_above, well_weights = call(
+    message, base, from_below, from_above, strengths, owners = call(
         sweep_kernel,
         "sweep",
         [ids, cells, perfs, index, krylov, *fields, diag, inv],
@@ -544,22 +611,33 @@
             (line(COLS * PLANE), "vmem"),
             (line(PLANE), "vmem"),
             (line(PLANE), "vmem"),
-            (line(WELLS * 8), "vmem"),
-        ],
-        scratch=[(96, XS, LANES), (24, XS, LANES)]
+            (line(8), "vmem"),
+            (line(8), "vmem", jnp.int32),
+        ],
+        scratch=[line(6 * PLANE), (96, XS, LANES), (24, XS, LANES)]
         + [(8, XS, LANES)] * 3
         + [(24, XS, LANES)] * 2
-        + [pltpu.SMEM((1, WELLS), jnp.int32), pltpu.SMEM((PERFS, WELLS), jnp.int32)]
-        + [pltpu.SMEM((PERFS, WELLS), F32)],
-        sems=17,
-    )
-    fixed, by_below, by_above = call(
+        + [pltpu.SMEM((1, WELLS), jnp.int32), pltpu.VMEM((PERFS, WELLS), jnp.int32)]
+        + [(PERFS, WELLS)],
+        sems=21,
+    )
+    fixed, by_below, by_above, fixed_rows, by_below_rows, by_above_rows, columns = call(
         ahead_kernel,
         "ahead",
-        [krylov, diag, inv, (base, "vmem"), (from_below, "vmem"), (from_above, "vmem")],
-        [(line(12 * PLANE), "vmem"), (line(3 * PLANE), "vmem"), (line(3 * PLANE), "vmem")],
-        scratch=[(96, XS, LANES), (24, XS, LANES), (72, XS, LANES)],
-        sems=10,
+        [krylov, diag, inv, send_rows, (base, "vmem"), (from_below, "vmem"), (from_above, "vmem")],
+        [
+            (line(12 * PLANE), "hbm"),
+            (line(3 * PLANE), "hbm"),
+            (line(3 * PLANE), "hbm"),
+            (line(TILES * 96), "vmem"),
+            (line(TILES * 24), "vmem"),
+            (line(TILES * 24), "vmem"),
+            (line(TILES * SLOTS), "vmem"),
+        ],
+        scratch=[line(12 * PLANE), line(3 * PLANE), line(3 * PLANE)]
+        + [(96, XS, LANES), (24, XS, LANES), (72, XS, LANES)]
+        + [pltpu.SMEM((SLOTS, TILES), jnp.int32)],
+        sems=14,
     )
     message = lax.all_to_all(
         message.reshape(CHUNKS, MSG, LANES), "layer", split_axis=0, concat_axis=0, tiled=True
@@ -567,66 +645,80 @@
     (reply,) = call(
         chain_kernel,
         "chain",
-        [ids, cells, (rows(message), "vmem")],
+        [(owners, "vmem"), (rows(message), "vmem")],
         [(line(CHUNKS * MSG), "vmem")],
-        scratch=[(LANES, 2 * LANES), pltpu.SMEM((1, WELLS), jnp.int32)],
-        sems=1,
+        scratch=[(LANES, 2 * LANES)],
+        sems=0,
     )
     reply = lax.all_to_all(
         reply.reshape(CHUNKS, MSG, LANES), "layer", split_axis=0, concat_axis=0, tiled=True
     )
-    precond, precond_out, x_a, x_b, layer_a, layer_b, outgoing, rates = call(
+    reply = rows(reply)
+    (outgoing,) = call(
+        outgoing_kernel,
+        "outgoing",
+        [
+            (reply, "vmem"), (fixed_rows, "vmem"), (by_below_rows, "vmem"),
+            (by_above_rows, "vmem"), (columns, "vmem"),
+        ],
+        [(line(TILES * 96), "hbm")],
+        scratch=[line(TILES * 96)],
+        sems=2,
+    )
+    arrived = lax.all_to_all(
+        outgoing.reshape(TILES, 96, LANES), ("tx", "ty"), split_axis=0, concat_axis=0, tiled=True
+    )
+    precond, x_a, x_b, layer_a, layer_b, across, rates = call(
         precond_kernel,
         "precond",
-        [
-            ids, send_rows, (rows(reply), "vmem"), (fixed, "vmem"), (by_below, "vmem"),
-            (by_above, "vmem"),
-        ],
-        [
-            (line(12 * PLANE), "vmem"),
+        [ids, (reply, "vmem"), (fixed, "hbm"), (by_below, "hbm"), (by_above, "hbm")],
+        [
             (line(12 * PLANE), "hbm"),
             (line(96), "hbm"),
             (line(96), "hbm"),
             ((12, XS, LANES), "hbm"),
             ((12, XS, LANES), "hbm"),
-            (line(TILES * 96), "hbm"),
+            (line(XS), "hbm"),
             (line(8), "vmem"),
         ],
-        scratch=[line(96), line(96), line(TILES * 96), pltpu.SMEM((SLOTS, TILES), jnp.int32)],
-        sems=7,
-    )
-    across = lax.ppermute(precond_out, "ty", pairs(n_ty, False))
+        scratch=[line(12 * PLANE), line(96), line(96), line(XS)]
+        + [line(12 * PLANE), line(3 * PLANE), line(3 * PLANE)],
+        sems=12,
+    )
+    across = lax.ppermute(across, "ty", pairs(n_ty, False))
     x_a = lax.ppermute(x_a, "tx", pairs(n_tx, False))
     x_b = lax.ppermute(x_b, "tx", pairs(n_tx, True))
     layer_a = lax.ppermute(layer_a, "layer", pairs(n_layer, False))
     layer_b = lax.ppermute(layer_b, "layer", pairs(n_layer, True))
-    arrived = lax.all_to_all(
-        outgoing.reshape(TILES, 96, LANES), ("tx", "ty"), split_axis=0, concat_axis=0, tiled=True
-    )
     devices = n_layer * n_tx * n_ty
-    partial, edges, targets = call(
+    partial, edges, targets, coef = call(
         stencil_kernel,
         "stencil",
         [
-            ids, cells, recv_rows, counts, (precond, "vmem"), (across, "hbm"), (rows(layer_a), "hbm"),
+            ids, cells, recv_rows, counts, (precond, "hbm"), (across, "hbm"), (rows(layer_a), "hbm"),
             (rows(layer_b), "hbm"), (rows(block_diag), "hbm"), (rows(face_coef), "hbm"),
-            (rates, "vmem"), (well_weights, "vmem"),
-        ],
-        [(line(12 * PLANE), "vmem"), (line(16), "vmem"), (line(PLANE), "vmem")],
-        scratch=[line(12 * PLANE), line(12 * XS), line(12 * XS), line(9 * PLANE), line(6 * PLANE)]
+            (rows(fault_coef), "hbm"), (rates, "vmem"), (strengths, "vmem"),
+        ],
+        [
+            (line(12 * PLANE), "vmem"),
+            (line(16), "vmem"),
+            (line(PLANE), "vmem"),
+            (line(TILES * SLOTS), "vmem"),
+        ],
+        scratch=[line(12 * PLANE), line(XS), line(12 * XS), line(12 * XS), line(9 * PLANE), line(6 * PLANE)]
         + [pltpu.SMEM((1, WELLS), jnp.int32), pltpu.SMEM((SLOTS, TILES), jnp.int32)]
         + [pltpu.SMEM((1, TILES), jnp.int32)],
-        sems=8,
+        sems=10,
     )
     image, gram = call(
         finish_kernel,
         "finish",
         [
             ids, (partial, "vmem"), (x_a, "vmem"), (x_b, "vmem"), (arrived, "vmem"),
-            (rows(fault_coef), "hbm"), (edges, "vmem"), (targets, "vmem"),
+            (coef, "vmem"), (edges, "vmem"), (targets, "vmem"),
         ],
         [(line(12 * PLANE), "vmem"), (line(devices), "vmem")],
-        scratch=[line(TILES * SLOTS)],
+        sems=0,
         alias={1: 0},
     )
     gathered = lax.all_to_all(gram, ALL, split_axis=0, concat_axis=0, tiled=True)

time: 94.2 us -> 89.9 us (0.954)
  waiting for transfers between devices: 16.4 us -> 11.9 us
  local copies, waits for them, and re-layouts: 3.87 us -> 0.73 us
  blocking collectives: 33.3 us -> 35.4 us
    unnamed x18 -> x6, local copies, waits for them, and re-layouts: 3.87 us -> 0.73 us
    all_to_all x1, starting transfers between devices: 8.63 us -> 11.7 us  [on_device(): lax.all_to_all(outgoing.reshape(TILES, 96, LANES), ('tx', 'ty'), split_ax...]
    ppermute x1, starting transfers between devices: 3.34 us -> 1.01 us  [on_device(): across = lax.ppermute(across, 'ty', pairs(n_ty, False))]
    ppermute x1, waiting for transfers between devices: 5.68 us -> 3.35 us  [on_device(): x_a = lax.ppermute(x_a, 'tx', pairs(n_tx, False))]
    all_to_all x1, blocking collectives: 18.8 us -> 20.8 us  [on_device(): lax.all_to_all(gram, ALL, split_axis=0, concat_axis=0, tiled=True)]
    ppermute x1, waiting for transfers between devices: 3.36 us -> 1.52 us  [on_device(): layer_a = lax.ppermute(layer_a, 'layer', pairs(n_layer, False))]
    all_to_all x1, waiting for transfers between devices: 4.98 us -> 3.57 us  [on_device(): lax.all_to_all(reply.reshape(CHUNKS, MSG, LANES), 'layer', split_axis=0,...]
    ppermute x1, waiting for transfers between devices: 0.01 us -> 1.05 us  [on_device(): across = lax.ppermute(across, 'ty', pairs(n_ty, False))]
  transfers between devices with their start and end apart: 7 -> 7, of which waited for: 4 -> 5; matrix products, arithmetic and copies ran while one was open for 0% -> 0% of each run, Pallas kernels for 8% -> 15%
where the time goes in v4:
time: 89.9 us; the launch traced here: 89.5 us
  blocking collectives  35.4 us (39%)
  Pallas kernels  21.3 us (24%)
  starting transfers between devices  19.4 us (22%)
  waiting for transfers between devices  11.9 us (13%)
    pallas_call x8, Pallas kernels, call(): pl.pallas_call(kernel, name=name, out_shape=tuple((SPACES[o[1]](o[0], o[2...  21.3 us
    all_to_all x1, blocking collectives, on_device(): lax.all_to_all(gram, ALL, split_axis=0, concat_axis=0, tiled=True)  20.8 us
    all_to_all x1, blocking collectives, on_device(): lax.all_to_all(message.reshape(CHUNKS, MSG, LANES), 'layer', split_axis=0...  14.6 us
    all_to_all x1, starting transfers between devices, on_device(): lax.all_to_all(outgoing.reshape(TILES, 96, LANES), ('tx', 'ty'), split_ax...  11.7 us
    all_to_all x1, waiting for transfers between devices, on_device(): lax.all_to_all(reply.reshape(CHUNKS, MSG, LANES), 'layer', split_axis=0,...  3.57 us
    all_to_all x1, starting transfers between devices, on_device(): lax.all_to_all(reply.reshape(CHUNKS, MSG, LANES), 'layer', split_axis=0,...  3.52 us
    ppermute x1, waiting for transfers between devices, on_device(): x_a = lax.ppermute(x_a, 'tx', pairs(n_tx, False))  3.35 us
    all_to_all x1, waiting for transfers between devices, on_device(): lax.all_to_all(outgoing.reshape(TILES, 96, LANES), ('tx', 'ty'), split_ax...  2.36 us
  transfers between devices with their start and end apart: 7, of which 5 were waited for; matrix products, arithmetic and copies ran while one was open for 0% of the time, Pallas kernels for 15%

profile of v4, /device:TPU:1, one launch (start us, length us, event | category | flops | bytes accessed | tf_op | source)
XLA Modules:
  0.0 89.5 jit_solution(17410190705628096916)
XLA Ops:
  0.6 0.1 add_bitcast_fusion.ids
  0.7 3.3 %sweep.1 = (f32[384,128]{1,0:T(8,128)S(1)}, f32[1024,128]{1,0:T(8,128)S(1)}, f32[256,128]{1,0:T(8,128)S(1)}, f32[256,128]{1,0:T(8,128)S(1)}, f32[8,128]{1,0:T(8,128)S(1)}, /*index=5*/s32[8,128]{1,0:T(8,128)S(1)}) custom-call(s32[1,3]{1,0:T(1,128)S(1)} %add_bitcast_fusion.ids, s32[1,16]{1,0:T(1,128)} %bitcast.61, s32[8,16]{1,0:T(8,128)} %bitcast.57, ...), custom_call_target="tpu_custom_call" | custom-call | flops 1000000 | bytes 4719692 | tf_op jit(solution)/shard_map/sweep/pallas_call | solution.py:545
  4.0 14.6 %all_to_all.26 = f32[16,24,128]{2,1,0:T(8,128)S(1)} all-to-all(f32[16,24,128]{2,1,0:T(8,128)S(1)} %bitcast.42), channel_id=1, replica_groups=mesh['layer'=16,'tx'=8,'ty'=2] {'layer'}, dimensions={0} | all-to-all | bytes 393216 | tf_op jit(solution)/shard_map/all_to_all | solution.py:642
  18.6 1.0 %chain.1 = f32[384,128]{1,0:T(8,128)} custom-call(s32[8,128]{1,0:T(8,128)S(1)} %get-tuple-element.30.owners, f32[384,128]{1,0:T(8,128)S(1)} %bitcast.40), custom_call_target="tpu_custom_call" | custom-call | flops 1000000 | bytes 200704 | tf_op jit(solution)/shard_map/chain/pallas_call | solution.py:545
  19.6 3.5 %all-to-all-start.1 = ((f32[16,24,128]{2,1,0:T(8,128)}), f32[16,24,128]{2,1,0:T(8,128)S(1)}, u32[]{:S(2)}, u32[]{:S(2)}) async-start(f32[16,24,128]{2,1,0:T(8,128)} %bitcast.18), calls=%async_computation.1 | async-start | bytes 393216 | tf_op jit(solution)/shard_map/all_to_all | solution.py:653
  23.1 3.6 %ahead.1 = (f32[3072,128]{1,0:T(8,128)}, f32[768,128]{1,0:T(8,128)}, f32[768,128]{1,0:T(8,128)}, f32[1536,128]{1,0:T(8,128)S(1)}, f32[384,128]{1,0:T(8,128)S(1)}...) custom-call(f32[96,32,128]{2,1,0:T(8,128)} %bitcast.48, f32[72,32,128]{2,1,0:T(8,128)} %bitcast.45, ...), custom_call_target="tpu_custom_call" | custom-call | flops 1000000 | bytes 4719104 | tf_op jit(solution)/shard_map/ahead/pallas_call | solution.py:545
  26.7 3.6 %all-to-all-done.1 = f32[16,24,128]{2,1,0:T(8,128)S(1)} async-done(((f32[16,24,128]{2,1,0:T(8,128)}), f32[16,24,128]{2,1,0:T(8,128)S(1)}, u32[]{:S(2)}, u32[]{:S(2)}) %all-to-all-start.1) | async-done | bytes 196640 | tf_op jit(solution)/shard_map/all_to_all | solution.py:653
  30.3 1.1 %outgoing.1 = f32[1536,128]{1,0:T(8,128)} custom-call(f32[384,128]{1,0:T(8,128)S(1)} %bitcast.38, f32[1536,128]{1,0:T(8,128)S(1)} %get-tuple-element.47.fixed_rows, f32[384,128]{1,0:T(8,128)S(1)} %get-tuple-element.48.by_below_rows, f32[384,128]{1,0:T(8,128)S(1)} %get-tuple-element.49.by_above_rows, f32[128,128]{1,0:T(8,128)S(1)} %get-tuple-element.50.columns), custom_call_target="tpu_custom_call" | custom-call | flops 1000000 | bytes 1441792 | tf_op jit(solution)/shard_map/outgoing/pallas_call | solution.py:545
  31.4 11.7 %all-to-all-start.2 = ((f32[16,96,128]{2,1,0:T(8,128)}), f32[16,96,128]{2,1,0:T(8,128)S(1)}, u32[]{:S(2)}, u32[]{:S(2)}) async-start(f32[16,96,128]{2,1,0:T(8,128)} %bitcast.51), calls=%async_computation.2 | async-start | bytes 1572864 | tf_op jit(solution)/shard_map/all_to_all | solution.py:668
  43.2 4.1 %precond.1 = (f32[3072,128]{1,0:T(8,128)}, f32[96,128]{1,0:T(8,128)}, f32[96,128]{1,0:T(8,128)}, f32[12,32,128]{2,1,0:T(8,128)}, f32[12,32,128]{2,1,0:T(8,128)},...) custom-call(s32[1,3]{1,0:T(1,128)S(1)} %add_bitcast_fusion.ids, f32[384,128]{1,0:T(8,128)S(1)} %bitcast.39, ...), custom_call_target="tpu_custom_call" | custom-call | flops 1000000 | bytes 2555916 | tf_op jit(solution)/shard_map/precond/pallas_call | solution.py:545
  47.3 0.4 collective-permute-start.1
  47.7 0.7 collective-permute-start.2
  48.4 1.5 %collective-permute-start.3 = (f32[96,128]{1,0:T(8,128)}, f32[96,128]{1,0:T(8,128)S(1)}, u32[]{:S(2)}, u32[]{:S(2)}) collective-permute-start(f32[96,128]{1,0:T(8,128)} %get-tuple-element.45), channel_id=1, source_target_pairs={{0,2},{2,0},{4,6},{6,4},{8,10},{10,8},{12,14},{14,12},{1,3},{3,1},... | collective-permute-start | bytes 147464 | tf_op jit(solution)/shard_map/ppermute | solution.py:689
  49.8 0.7 collective-permute-start.4
  50.5 1.0 %collective-permute-start = (f32[32,128]{1,0:T(8,128)}, f32[32,128]{1,0:T(8,128)S(1)}, u32[]{:S(2)}, u32[]{:S(2)}) collective-permute-start(f32[32,128]{1,0:T(8,128)} %get-tuple-element.39), channel_id=1, source_target_pairs={{0,1},{1,0},{2,3},{3,2},{4,5},{5,4},{6,7},{7,6},{8,9},{9,8},{10,11... | collective-permute-start | bytes 49160 | tf_op jit(solution)/shard_map/ppermute | solution.py:688
  51.5 1.0 %collective-permute-done.across_h = f32[32,128]{1,0:T(8,128)S(1)} collective-permute-done((f32[32,128]{1,0:T(8,128)}, f32[32,128]{1,0:T(8,128)S(1)}, u32[]{:S(2)}, u32[]{:S(2)}) %collective-permute-start) | collective-permute-done | bytes 16416 | tf_op jit(solution)/shard_map/ppermute | solution.py:688
  52.5 0.0 copy-start.2
  52.5 1.5 %collective-permute-done.1 = f32[12,32,128]{2,1,0:T(8,128)S(1)} collective-permute-done((f32[12,32,128]{2,1,0:T(8,128)}, f32[12,32,128]{2,1,0:T(8,128)S(1)}, u32[]{:S(2)}, u32[]{:S(2)}) %collective-permute-start.1) | collective-permute-done | bytes 196640 | tf_op jit(solution)/shard_map/ppermute | solution.py:691
  54.1 0.0 copy-start
  54.1 0.0 collective-permute-done.2
  54.1 0.0 copy-start.1
  54.1 0.0 copy-done.2
  54.1 0.7 copy-done
  54.7 0.1 copy-done.1
  54.8 5.3 %stencil.1 = (f32[3072,128]{1,0:T(8,128)S(1)}, f32[16,128]{1,0:T(8,128)S(1)}, f32[256,128]{1,0:T(8,128)S(1)}, f32[128,128]{1,0:T(8,128)S(1)}) custom-call(s32[1,3]{1,0:T(1,128)S(1)} %add_bitcast_fusion.ids, s32[1,16]{1,0:T(1,128)} %bitcast.62, s32[8,16]{1,0:T(8,128)} %bitcast.60, s32[1,16]{1,0:T(1,128)} %bitcast.63, ...), custom_call_target="tpu_custom_call" | custom-call | flops 1000000 | bytes 4022924 | tf_op jit(solution)/shard_map/stencil/pallas_call | solution.py:545
  60.1 3.4 %collective-permute-done.3.x_a = f32[96,128]{1,0:T(8,128)S(1)} collective-permute-done((f32[96,128]{1,0:T(8,128)}, f32[96,128]{1,0:T(8,128)S(1)}, u32[]{:S(2)}, u32[]{:S(2)}) %collective-permute-start.3) | collective-permute-done | bytes 49184 | tf_op jit(solution)/shard_map/ppermute | solution.py:689
  63.5 0.0 collective-permute-done.4.x_b
  63.5 2.4 %all-to-all-done.2.arrived = f32[16,96,128]{2,1,0:T(8,128)S(1)} async-done(((f32[16,96,128]{2,1,0:T(8,128)}), f32[16,96,128]{2,1,0:T(8,128)S(1)}, u32[]{:S(2)}, u32[]{:S(2)}) %all-to-all-start.2) | async-done | bytes 786464 | tf_op jit(solution)/shard_map/all_to_all | solution.py:668
  65.9 1.4 %finish.1 = (f32[3072,128]{1,0:T(8,128)S(1)}, f32[256,128]{1,0:T(8,128)S(1)}) custom-call(s32[1,3]{1,0:T(1,128)S(1)} %add_bitcast_fusion.ids, f32[3072,128]{1,0:T(8,128)S(1)} %get-tuple-element.44._, f32[96,128]{1,0:T(8,128)S(1)} %collective-permute-done.3.x_a, f32[96,128]{1,0:T(8,128)S(1)} %collective-permute-done.4.x_b, ...), custom_call_target="tpu_custom_call", output_to_operand_aliasing={{0}: (1, {})} | custom-call | flops 1000000 | bytes 2662412 | tf_op jit(solution)/shard_map/finish/pallas_call | solution.py:545
  67.3 20.8 %all_to_all.27 = f32[256,1,128]{2,1,0:T(1,128)S(1)} all-to-all(f32[256,1,128]{2,1,0:T(1,128)S(1)} %bitcast.43), channel_id=1, replica_groups=mesh['layer'=16,'tx'=8,'ty'=2] {'layer','tx','ty'}, dimensions={0} | all-to-all | bytes 262144 | tf_op jit(solution)/shard_map/all_to_all | solution.py:724
  88.0 1.4 %factor.1 = (f32[12,256,128]{2,1,0:T(8,128)}, f32[4,4]{1,0:T(4,128)}) custom-call(f32[256,128]{1,0:T(8,128)S(1)} %bitcast.41, f32[3072,128]{1,0:T(8,128)S(1)} %get-tuple-element.55.refs_1_), custom_call_target="tpu_custom_call" | custom-call | flops 1000000 | bytes 1703936 | tf_op jit(solution)/shard_map/factor/pallas_call | solution.py:545
Async XLA Ops:
  19.6 10.7 %all-to-all-start.1 = ((f32[16,24,128]{2,1,0:T(8,128)}), f32[16,24,128]{2,1,0:T(8,128)S(1)}, u32[]{:S(2)}, u32[]{:S(2)}) async-start(f32[16,24,128]{2,1,0:T(8,128)} %bitcast.18), calls=%async_computation.1 | async-start | bytes 393216 | tf_op jit(solution)/shard_map/all_to_all | solution.py:653
  31.4 34.4 %all-to-all-start.2 = ((f32[16,96,128]{2,1,0:T(8,128)}), f32[16,96,128]{2,1,0:T(8,128)S(1)}, u32[]{:S(2)}, u32[]{:S(2)}) async-start(f32[16,96,128]{2,1,0:T(8,128)} %bitcast.51), calls=%async_computation.2 | async-start | bytes 1572864 | tf_op jit(solution)/shard_map/all_to_all | solution.py:668
  47.3 6.8 %collective-permute-start.1 = (f32[12,32,128]{2,1,0:T(8,128)}, f32[12,32,128]{2,1,0:T(8,128)S(1)}, u32[]{:S(2)}, u32[]{:S(2)}) collective-permute-start(f32[12,32,128]{2,1,0:T(8,128)} %get-tuple-element.40), channel_id=1, source_target_pairs={{0,16},{16,0},{32,48},{48,32},{64,80},{80,64},{96,112},{112,96},{1... | collective-permute-start | bytes 589832 | tf_op jit(solution)/shard_map/ppermute | solution.py:691
  47.7 6.4 %collective-permute-start.2 = (f32[12,32,128]{2,1,0:T(8,128)}, f32[12,32,128]{2,1,0:T(8,128)S(1)}, u32[]{:S(2)}, u32[]{:S(2)}) collective-permute-start(f32[12,32,128]{2,1,0:T(8,128)} %get-tuple-element.41), channel_id=1, source_target_pairs={{16,32},{32,16},{48,64},{64,48},{80,96},{96,80},{112,128},{128,112... | collective-permute-start | bytes 589832 | tf_op jit(solution)/shard_map/ppermute | solution.py:692
  48.4 15.1 %collective-permute-start.3 = (f32[96,128]{1,0:T(8,128)}, f32[96,128]{1,0:T(8,128)S(1)}, u32[]{:S(2)}, u32[]{:S(2)}) collective-permute-start(f32[96,128]{1,0:T(8,128)} %get-tuple-element.45), channel_id=1, source_target_pairs={{0,2},{2,0},{4,6},{6,4},{8,10},{10,8},{12,14},{14,12},{1,3},{3,1},... | collective-permute-start | bytes 147464 | tf_op jit(solution)/shard_map/ppermute | solution.py:689
  49.8 13.7 %collective-permute-start.4 = (f32[96,128]{1,0:T(8,128)}, f32[96,128]{1,0:T(8,128)S(1)}, u32[]{:S(2)}, u32[]{:S(2)}) collective-permute-start(f32[96,128]{1,0:T(8,128)} %get-tuple-element.46), channel_id=1, source_target_pairs={{2,4},{4,2},{6,8},{8,6},{10,12},{12,10},{3,5},{5,3},{7,9},{9,7},{1... | collective-permute-start | bytes 147464 | tf_op jit(solution)/shard_map/ppermute | solution.py:690
  50.5 2.1 %collective-permute-start = (f32[32,128]{1,0:T(8,128)}, f32[32,128]{1,0:T(8,128)S(1)}, u32[]{:S(2)}, u32[]{:S(2)}) collective-permute-start(f32[32,128]{1,0:T(8,128)} %get-tuple-element.39), channel_id=1, source_target_pairs={{0,1},{1,0},{2,3},{3,2},{4,5},{5,4},{6,7},{7,6},{8,9},{9,8},{10,11... | collective-permute-start | bytes 49160 | tf_op jit(solution)/shard_map/ppermute | solution.py:688
  52.5 1.5 %copy-start.2 = (f32[32,128]{1,0:T(8,128)}, f32[32,128]{1,0:T(8,128)S(1)}, u32[]{:S(2)}) copy-start(f32[32,128]{1,0:T(8,128)S(1)} %collective-permute-done.across_h) | copy-start | bytes 49156
  54.1 0.7 copy-start
  54.1 0.7 copy-start.1

commit v5 on v4

--- a/solution.py
+++ b/solution.py
@@ -310,6 +310,7 @@
     for j in range(1, CHUNKS):
         total += reply[pl.ds(j * MSG + 16, 8), :]
     rates[...] = total
+    written = []
     for s in range(COLS):
         ready(3 + s)
         for block in range(BLOCKS):
@@ -321,6 +322,9 @@
                     low, high = by_below[at, :], by_above[at, :]
                     at = rows_at(s * 3 + c, k, block)
                     precond[at, :] = fixed[at, :] + low * below + high * above
+        at = pl.ds(s * 3 * PLANE, 3 * PLANE)
+        copy = (precond.at[at], precond_h.at[at])
+        written.append(fetch([copy], sems.at[pl.ds(11 + s, 1)]))
     layer_even = (ids[0, 0] & 1) == 0
     x_even = (ids[0, 1] & 1) == 0
     layer_first = pl.multiple_of(jnp.where(layer_even, (LAYERS - 1) * XS, 0), XS)
@@ -342,11 +346,11 @@
             (x_b, x_b_h),
             (planes.at[:, pl.ds(layer_first, XS)], layer_a_h),
             (planes.at[:, pl.ds(layer_second, XS)], layer_b_h),
-            (precond, precond_h),
-        ],
-        sems.at[pl.ds(6, 6)],
-    )
-    sent()
+        ],
+        sems.at[pl.ds(6, 5)],
+    )
+    for wait in [sent] + written:
+        wait()
 
 
 def stencil_kernel(
@@ -368,6 +372,14 @@
     side = jnp.where(y_first, LANES - 1, 0)
     row_x = iota((XS, LANES), 0)
     lane_y = iota((XS, LANES), 1)
+    ready(3)
+    slot = iota((1, LANES), 1)
+    target = jnp.full((1, LANES), -1, jnp.int32)
+    for u in range(TILES):
+        for j in range(SLOTS):
+            row = jnp.where(j < counts[0, u], recv_rows[j, u], -1)
+            target = jnp.where(slot == u * SLOTS + j, row, target)
+    targets[...] = jnp.where(iota((PLANE, LANES), 0) == target, 1.0, 0.0)
     ready()
 
     def column(k, _):
@@ -405,13 +417,6 @@
         return _
 
     lax.fori_loop(0, LAYERS, column, 0)
-    slot = iota((1, LANES), 1)
-    target = jnp.full((1, LANES), -1, jnp.int32)
-    for u in range(TILES):
-        for j in range(SLOTS):
-            row = jnp.where(j < counts[0, u], recv_rows[j, u], -1)
-            target = jnp.where(slot == u * SLOTS + j, row, target)
-    targets[...] = jnp.where(iota((PLANE, LANES), 0) == target, 1.0, 0.0)
     edges[pl.ds(0, 8), :] = faces[pl.ds(2 * PLANE, 8, stride=XS), :]
     edges[pl.ds(8, 8), :] = faces[pl.ds(3 * PLANE + XS - 1, 8, stride=XS), :]
     rate = rates[...]
@@ -683,7 +688,7 @@
         ],
         scratch=[line(12 * PLANE), line(96), line(96), line(XS)]
         + [line(12 * PLANE), line(3 * PLANE), line(3 * PLANE)],
-        sems=12,
+        sems=15,
     )
     across = lax.ppermute(across, "ty", pairs(n_ty, False))
     x_a = lax.ppermute(x_a, "tx", pairs(n_tx, False))

time: 89.9 us -> 89.4 us (level)
  transfers between devices with their start and end apart: 7 -> 7, of which waited for: 5 -> 5; matrix products, arithmetic and copies ran while one was open for 0% -> 0% of each run, Pallas kernels for 15% -> 14%
where the time goes in v5:
time: 89.4 us; the launch traced here: 88.9 us
  blocking collectives  34.8 us (39%)
  Pallas kernels  20.8 us (23%)
  starting transfers between devices  19.4 us (22%)
  waiting for transfers between devices  12.4 us (14%)
    pallas_call x8, Pallas kernels, call(): pl.pallas_call(kernel, name=name, out_shape=tuple((SPACES[o[1]](o[0], o[2...  20.8 us
    all_to_all x1, blocking collectives, on_device(): lax.all_to_all(gram, ALL, split_axis=0, concat_axis=0, tiled=True)  20.2 us
    all_to_all x1, blocking collectives, on_device(): lax.all_to_all(message.reshape(CHUNKS, MSG, LANES), 'layer', split_axis=0...  14.6 us
    all_to_all x1, starting transfers between devices, on_device(): lax.all_to_all(outgoing.reshape(TILES, 96, LANES), ('tx', 'ty'), split_ax...  11.7 us
    ppermute x1, waiting for transfers between devices, on_device(): x_a = lax.ppermute(x_a, 'tx', pairs(n_tx, False))  3.88 us
    all_to_all x1, waiting for transfers between devices, on_device(): lax.all_to_all(reply.reshape(CHUNKS, MSG, LANES), 'layer', split_axis=0,...  3.57 us
    all_to_all x1, starting transfers between devices, on_device(): lax.all_to_all(reply.reshape(CHUNKS, MSG, LANES), 'layer', split_axis=0,...  3.52 us
    all_to_all x1, waiting for transfers between devices, on_device(): lax.all_to_all(outgoing.reshape(TILES, 96, LANES), ('tx', 'ty'), split_ax...  2.36 us
  transfers between devices with their start and end apart: 7, of which 5 were waited for; matrix products, arithmetic and copies ran while one was open for 0% of the time, Pallas kernels for 14%

profile of v5, /device:TPU:1, one launch (start us, length us, event | category | flops | bytes accessed | tf_op | source)
XLA Modules:
  0.0 88.9 jit_solution(638911488246891027)
XLA Ops:
  0.6 0.1 add_bitcast_fusion.ids
  0.7 3.3 %sweep.1 = (f32[384,128]{1,0:T(8,128)S(1)}, f32[1024,128]{1,0:T(8,128)S(1)}, f32[256,128]{1,0:T(8,128)S(1)}, f32[256,128]{1,0:T(8,128)S(1)}, f32[8,128]{1,0:T(8,128)S(1)}, /*index=5*/s32[8,128]{1,0:T(8,128)S(1)}) custom-call(s32[1,3]{1,0:T(1,128)S(1)} %add_bitcast_fusion.ids, s32[1,16]{1,0:T(1,128)} %bitcast.61, s32[8,16]{1,0:T(8,128)} %bitcast.57, ...), custom_call_target="tpu_custom_call" | custom-call | flops 1000000 | bytes 4719692 | tf_op jit(solution)/shard_map/sweep/pallas_call | solution.py:550
  4.0 14.6 %all_to_all.26 = f32[16,24,128]{2,1,0:T(8,128)S(1)} all-to-all(f32[16,24,128]{2,1,0:T(8,128)S(1)} %bitcast.42), channel_id=1, replica_groups=mesh['layer'=16,'tx'=8,'ty'=2] {'layer'}, dimensions={0} | all-to-all | bytes 393216 | tf_op jit(solution)/shard_map/all_to_all | solution.py:647
  18.6 1.0 %chain.1 = f32[384,128]{1,0:T(8,128)} custom-call(s32[8,128]{1,0:T(8,128)S(1)} %get-tuple-element.30.owners, f32[384,128]{1,0:T(8,128)S(1)} %bitcast.40), custom_call_target="tpu_custom_call" | custom-call | flops 1000000 | bytes 200704 | tf_op jit(solution)/shard_map/chain/pallas_call | solution.py:550
  19.6 3.5 %all-to-all-start.1 = ((f32[16,24,128]{2,1,0:T(8,128)}), f32[16,24,128]{2,1,0:T(8,128)S(1)}, u32[]{:S(2)}, u32[]{:S(2)}) async-start(f32[16,24,128]{2,1,0:T(8,128)} %bitcast.18), calls=%async_computation.1 | async-start | bytes 393216 | tf_op jit(solution)/shard_map/all_to_all | solution.py:658
  23.1 3.6 %ahead.1 = (f32[3072,128]{1,0:T(8,128)}, f32[768,128]{1,0:T(8,128)}, f32[768,128]{1,0:T(8,128)}, f32[1536,128]{1,0:T(8,128)S(1)}, f32[384,128]{1,0:T(8,128)S(1)}...) custom-call(f32[96,32,128]{2,1,0:T(8,128)} %bitcast.48, f32[72,32,128]{2,1,0:T(8,128)} %bitcast.45, ...), custom_call_target="tpu_custom_call" | custom-call | flops 1000000 | bytes 4719104 | tf_op jit(solution)/shard_map/ahead/pallas_call | solution.py:550
  26.7 3.6 %all-to-all-done.1 = f32[16,24,128]{2,1,0:T(8,128)S(1)} async-done(((f32[16,24,128]{2,1,0:T(8,128)}), f32[16,24,128]{2,1,0:T(8,128)S(1)}, u32[]{:S(2)}, u32[]{:S(2)}) %all-to-all-start.1) | async-done | bytes 196640 | tf_op jit(solution)/shard_map/all_to_all | solution.py:658
  30.3 1.1 %outgoing.1 = f32[1536,128]{1,0:T(8,128)} custom-call(f32[384,128]{1,0:T(8,128)S(1)} %bitcast.38, f32[1536,128]{1,0:T(8,128)S(1)} %get-tuple-element.47.fixed_rows, f32[384,128]{1,0:T(8,128)S(1)} %get-tuple-element.48.by_below_rows, f32[384,128]{1,0:T(8,128)S(1)} %get-tuple-element.49.by_above_rows, f32[128,128]{1,0:T(8,128)S(1)} %get-tuple-element.50.columns), custom_call_target="tpu_custom_call" | custom-call | flops 1000000 | bytes 1441792 | tf_op jit(solution)/shard_map/outgoing/pallas_call | solution.py:550
  31.4 11.7 %all-to-all-start.2 = ((f32[16,96,128]{2,1,0:T(8,128)}), f32[16,96,128]{2,1,0:T(8,128)S(1)}, u32[]{:S(2)}, u32[]{:S(2)}) async-start(f32[16,96,128]{2,1,0:T(8,128)} %bitcast.51), calls=%async_computation.2 | async-start | bytes 1572864 | tf_op jit(solution)/shard_map/all_to_all | solution.py:673
  43.2 3.6 %precond.1 = (f32[3072,128]{1,0:T(8,128)}, f32[96,128]{1,0:T(8,128)}, f32[96,128]{1,0:T(8,128)}, f32[12,32,128]{2,1,0:T(8,128)}, f32[12,32,128]{2,1,0:T(8,128)},...) custom-call(s32[1,3]{1,0:T(1,128)S(1)} %add_bitcast_fusion.ids, f32[384,128]{1,0:T(8,128)S(1)} %bitcast.39, ...), custom_call_target="tpu_custom_call" | custom-call | flops 1000000 | bytes 2555916 | tf_op jit(solution)/shard_map/precond/pallas_call | solution.py:550
  46.8 0.4 collective-permute-start.1
  47.2 0.7 collective-permute-start.2
  47.9 1.4 %collective-permute-start.3 = (f32[96,128]{1,0:T(8,128)}, f32[96,128]{1,0:T(8,128)S(1)}, u32[]{:S(2)}, u32[]{:S(2)}) collective-permute-start(f32[96,128]{1,0:T(8,128)} %get-tuple-element.45), channel_id=1, source_target_pairs={{0,2},{2,0},{4,6},{6,4},{8,10},{10,8},{12,14},{14,12},{1,3},{3,1},... | collective-permute-start | bytes 147464 | tf_op jit(solution)/shard_map/ppermute | solution.py:694
  49.3 0.7 collective-permute-start.4
  50.0 1.0 %collective-permute-start = (f32[32,128]{1,0:T(8,128)}, f32[32,128]{1,0:T(8,128)S(1)}, u32[]{:S(2)}, u32[]{:S(2)}) collective-permute-start(f32[32,128]{1,0:T(8,128)} %get-tuple-element.39), channel_id=1, source_target_pairs={{0,1},{1,0},{2,3},{3,2},{4,5},{5,4},{6,7},{7,6},{8,9},{9,8},{10,11... | collective-permute-start | bytes 49160 | tf_op jit(solution)/shard_map/ppermute | solution.py:693
  51.0 1.0 %collective-permute-done.across_h = f32[32,128]{1,0:T(8,128)S(1)} collective-permute-done((f32[32,128]{1,0:T(8,128)}, f32[32,128]{1,0:T(8,128)S(1)}, u32[]{:S(2)}, u32[]{:S(2)}) %collective-permute-start) | collective-permute-done | bytes 16416 | tf_op jit(solution)/shard_map/ppermute | solution.py:693
  52.1 0.0 copy-start.2
  52.1 1.5 %collective-permute-done.1 = f32[12,32,128]{2,1,0:T(8,128)S(1)} collective-permute-done((f32[12,32,128]{2,1,0:T(8,128)}, f32[12,32,128]{2,1,0:T(8,128)S(1)}, u32[]{:S(2)}, u32[]{:S(2)}) %collective-permute-start.1) | collective-permute-done | bytes 196640 | tf_op jit(solution)/shard_map/ppermute | solution.py:696
  53.6 0.0 copy-start
  53.6 0.0 collective-permute-done.2
  53.6 0.0 copy-start.1
  53.6 0.0 copy-done.2
  53.6 0.7 copy-done
  54.3 0.1 copy-done.1
  54.3 5.3 %stencil.1 = (f32[3072,128]{1,0:T(8,128)S(1)}, f32[16,128]{1,0:T(8,128)S(1)}, f32[256,128]{1,0:T(8,128)S(1)}, f32[128,128]{1,0:T(8,128)S(1)}) custom-call(s32[1,3]{1,0:T(1,128)S(1)} %add_bitcast_fusion.ids, s32[1,16]{1,0:T(1,128)} %bitcast.62, s32[8,16]{1,0:T(8,128)} %bitcast.60, s32[1,16]{1,0:T(1,128)} %bitcast.63, ...), custom_call_target="tpu_custom_call" | custom-call | flops 1000000 | bytes 4022924 | tf_op jit(solution)/shard_map/stencil/pallas_call | solution.py:550
  59.6 3.9 %collective-permute-done.3.x_a = f32[96,128]{1,0:T(8,128)S(1)} collective-permute-done((f32[96,128]{1,0:T(8,128)}, f32[96,128]{1,0:T(8,128)S(1)}, u32[]{:S(2)}, u32[]{:S(2)}) %collective-permute-start.3) | collective-permute-done | bytes 49184 | tf_op jit(solution)/shard_map/ppermute | solution.py:694
  63.5 0.0 collective-permute-done.4.x_b
  63.5 2.4 %all-to-all-done.2.arrived = f32[16,96,128]{2,1,0:T(8,128)S(1)} async-done(((f32[16,96,128]{2,1,0:T(8,128)}), f32[16,96,128]{2,1,0:T(8,128)S(1)}, u32[]{:S(2)}, u32[]{:S(2)}) %all-to-all-start.2) | async-done | bytes 786464 | tf_op jit(solution)/shard_map/all_to_all | solution.py:673
  65.9 1.4 %finish.1 = (f32[3072,128]{1,0:T(8,128)S(1)}, f32[256,128]{1,0:T(8,128)S(1)}) custom-call(s32[1,3]{1,0:T(1,128)S(1)} %add_bitcast_fusion.ids, f32[3072,128]{1,0:T(8,128)S(1)} %get-tuple-element.44._, f32[96,128]{1,0:T(8,128)S(1)} %collective-permute-done.3.x_a, f32[96,128]{1,0:T(8,128)S(1)} %collective-permute-done.4.x_b, ...), custom_call_target="tpu_custom_call", output_to_operand_aliasing={{0}: (1, {})} | custom-call | flops 1000000 | bytes 2662412 | tf_op jit(solution)/shard_map/finish/pallas_call | solution.py:550
  67.3 20.2 %all_to_all.27 = f32[256,1,128]{2,1,0:T(1,128)S(1)} all-to-all(f32[256,1,128]{2,1,0:T(1,128)S(1)} %bitcast.43), channel_id=1, replica_groups=mesh['layer'=16,'tx'=8,'ty'=2] {'layer','tx','ty'}, dimensions={0} | all-to-all | bytes 262144 | tf_op jit(solution)/shard_map/all_to_all | solution.py:729
  87.5 1.4 %factor.1 = (f32[12,256,128]{2,1,0:T(8,128)}, f32[4,4]{1,0:T(4,128)}) custom-call(f32[256,128]{1,0:T(8,128)S(1)} %bitcast.41, f32[3072,128]{1,0:T(8,128)S(1)} %get-tuple-element.55.refs_1_), custom_call_target="tpu_custom_call" | custom-call | flops 1000000 | bytes 1703936 | tf_op jit(solution)/shard_map/factor/pallas_call | solution.py:550
Async XLA Ops:
  19.6 10.7 %all-to-all-start.1 = ((f32[16,24,128]{2,1,0:T(8,128)}), f32[16,24,128]{2,1,0:T(8,128)S(1)}, u32[]{:S(2)}, u32[]{:S(2)}) async-start(f32[16,24,128]{2,1,0:T(8,128)} %bitcast.18), calls=%async_computation.1 | async-start | bytes 393216 | tf_op jit(solution)/shard_map/all_to_all | solution.py:658
  31.4 34.4 %all-to-all-start.2 = ((f32[16,96,128]{2,1,0:T(8,128)}), f32[16,96,128]{2,1,0:T(8,128)S(1)}, u32[]{:S(2)}, u32[]{:S(2)}) async-start(f32[16,96,128]{2,1,0:T(8,128)} %bitcast.51), calls=%async_computation.2 | async-start | bytes 1572864 | tf_op jit(solution)/shard_map/all_to_all | solution.py:673
  46.8 6.8 %collective-permute-start.1 = (f32[12,32,128]{2,1,0:T(8,128)}, f32[12,32,128]{2,1,0:T(8,128)S(1)}, u32[]{:S(2)}, u32[]{:S(2)}) collective-permute-start(f32[12,32,128]{2,1,0:T(8,128)} %get-tuple-element.40), channel_id=1, source_target_pairs={{0,16},{16,0},{32,48},{48,32},{64,80},{80,64},{96,112},{112,96},{1... | collective-permute-start | bytes 589832 | tf_op jit(solution)/shard_map/ppermute | solution.py:696
  47.2 6.4 %collective-permute-start.2 = (f32[12,32,128]{2,1,0:T(8,128)}, f32[12,32,128]{2,1,0:T(8,128)S(1)}, u32[]{:S(2)}, u32[]{:S(2)}) collective-permute-start(f32[12,32,128]{2,1,0:T(8,128)} %get-tuple-element.41), channel_id=1, source_target_pairs={{16,32},{32,16},{48,64},{64,48},{80,96},{96,80},{112,128},{128,112... | collective-permute-start | bytes 589832 | tf_op jit(solution)/shard_map/ppermute | solution.py:697
  47.9 15.6 %collective-permute-start.3 = (f32[96,128]{1,0:T(8,128)}, f32[96,128]{1,0:T(8,128)S(1)}, u32[]{:S(2)}, u32[]{:S(2)}) collective-permute-start(f32[96,128]{1,0:T(8,128)} %get-tuple-element.45), channel_id=1, source_target_pairs={{0,2},{2,0},{4,6},{6,4},{8,10},{10,8},{12,14},{14,12},{1,3},{3,1},... | collective-permute-start | bytes 147464 | tf_op jit(solution)/shard_map/ppermute | solution.py:694
  49.3 14.1 %collective-permute-start.4 = (f32[96,128]{1,0:T(8,128)}, f32[96,128]{1,0:T(8,128)S(1)}, u32[]{:S(2)}, u32[]{:S(2)}) collective-permute-start(f32[96,128]{1,0:T(8,128)} %get-tuple-element.46), channel_id=1, source_target_pairs={{2,4},{4,2},{6,8},{8,6},{10,12},{12,10},{3,5},{5,3},{7,9},{9,7},{1... | collective-permute-start | bytes 147464 | tf_op jit(solution)/shard_map/ppermute | solution.py:695
  50.0 2.1 %collective-permute-start = (f32[32,128]{1,0:T(8,128)}, f32[32,128]{1,0:T(8,128)S(1)}, u32[]{:S(2)}, u32[]{:S(2)}) collective-permute-start(f32[32,128]{1,0:T(8,128)} %get-tuple-element.39), channel_id=1, source_target_pairs={{0,1},{1,0},{2,3},{3,2},{4,5},{5,4},{6,7},{7,6},{8,9},{9,8},{10,11... | collective-permute-start | bytes 49160 | tf_op jit(solution)/shard_map/ppermute | solution.py:693
  52.1 1.5 %copy-start.2 = (f32[32,128]{1,0:T(8,128)}, f32[32,128]{1,0:T(8,128)S(1)}, u32[]{:S(2)}) copy-start(f32[32,128]{1,0:T(8,128)S(1)} %collective-permute-done.across_h) | copy-start | bytes 49156
  53.6 0.7 copy-start
  53.6 0.7 copy-start.1
